TPU v7x, 256 devices: a whole 4x4x8 slice. The times are simulated.
256 devices in a mesh: slab: 8 (over y, core), angle: 32 (over z, x).
Axes of the slice: x: 4, y: 4, z: 8, core: 2. Of those that a mesh axis runs over, the one named last changes fastest.
Arguments:
- volume: float32 [8192, 128], P(('slab', 'angle')), may hold values from -6 to 6
- measured: float32 [2048, 128], P('angle'), may hold values from 30 to 1000
- footprint: bfloat16 [49152, 128, 128], P(('slab', 'angle')), may hold values from 0.0099487305 to 1
- block_voxel: int32 [49152], P(('slab', 'angle')), may hold values from 0 to 1023, as said below
- block_tile: int32 [49152], P(('slab', 'angle')), may hold values from 0 to 63
- block_rows: int32 [49152], P(('slab', 'angle')), may hold values from 0 to 128, as said below
Outputs:
- new_volume: float32 [8192, 128], P(('slab', 'angle'))
- weighted_residual: float32 [2048, 128], P('angle')
Inputs may be any that keep to these rules, and one draw needn't show every extreme that they name: `block_rows`: 0 marks an empty slot; the live slots of each device come first, each device has at least 48 live slots, some device has all 192 live, and every device has a live slot covering all 128 rows. On each device the slots form aligned groups of 12 in a row whose voxel blocks all lie in one share block_voxel // 32, different groups of a device in different shares; so at most 12 slots of a device name one share, and in each slab one share is named by 12 slots of every device.
All inputs are finite; a program needn't handle non-finite values.
Results may differ from a plain program's by a relative error of at most 0.00042.
Values may be sent and summed in bfloat16 or wider, within the bound.
No kernel may reach another device: no remote copies, remote signals or barrier semaphores. Data moves between devices by JAX's collectives and lax.ppermute only.
A program may use at most 64 MiB of HBM per device.

v0:
```python
import jax
import jax.numpy as jnp
from jax import lax
from jax.sharding import PartitionSpec as P


def residual_of(summed, measured_part):
    return (measured_part - summed[:, 0]) / jnp.maximum(summed[:, 1], 1.0)


def on_device(volume, measured, footprint, block_voxel, block_tile, block_rows):
    width = volume.shape[1]
    kept_blocks = volume.shape[0]
    tile_count = measured.shape[0]
    angle_count = lax.axis_size("angle")
    slab_blocks = kept_blocks * angle_count
    row_live = jnp.arange(width, dtype=jnp.int32)[None, :] < block_rows[:, None]
    coarse = volume.astype(jnp.bfloat16)
    slab_values = lax.all_gather(coarse, "angle", axis=0, tiled=True)
    picked = slab_values[block_voxel]
    stacked = jnp.stack([picked, jnp.ones_like(picked)], 1)
    forward = jnp.einsum("bpv,bkv->bkp", footprint, stacked, preferred_element_type=jnp.float32)
    forward = forward * row_live[:, None, :].astype(jnp.float32)
    tile_onehot = (block_tile[:, None] == jnp.arange(tile_count, dtype=jnp.int32)[None, :]).astype(
        jnp.float32
    )
    partial_sums = jnp.einsum("bt,bkp->tkp", tile_onehot, forward, precision=lax.Precision.HIGHEST)
    summed = lax.psum(partial_sums, "slab")
    weighted = residual_of(summed, measured)
    live_bf = row_live.astype(jnp.bfloat16)
    coarse_res = weighted.astype(jnp.bfloat16)
    res_rows = coarse_res[block_tile] * live_bf
    back_in = jnp.stack([res_rows, live_bf], 1)
    backward = jnp.einsum("bpv,bkp->bkv", footprint, back_in, preferred_element_type=jnp.float32)
    per_block = jnp.zeros((slab_blocks, 2, width), jnp.float32).at[block_voxel].add(backward)
    owned = lax.psum_scatter(per_block, "angle", scatter_dimension=0, tiled=True)
    correction = owned[:, 0] / jnp.maximum(owned[:, 1], 1.0)
    return (volume + correction, weighted)


def solution(mesh):
    in_specs = (
        P(("slab", "angle"), None),
        P("angle", None),
        P(("slab", "angle"), None, None),
        P(("slab", "angle")),
        P(("slab", "angle")),
        P(("slab", "angle")),
    )
    out_specs = (P(("slab", "angle"), None), P("angle", None))
    return jax.shard_map(
        on_device, mesh=mesh, in_specs=in_specs, out_specs=out_specs, check_vma=False
    )
```

profile of v0, /device:TPU:32, one launch (start us, length us, event | category | flops | bytes accessed | tf_op | source)
XLA Modules:
  0.0 302.5 jit_solution(17212364756897373537)
XLA Ops:
  7.2 0.0 copy-start.3
  7.2 0.0 copy-start.4
  7.2 0.0 copy-start.2
  7.2 0.0 all-reduce.5.cloned.1.call-start
  7.2 0.7 compare_select_fusion.2
  7.9 0.7 convert_element_type.25
  8.7 51.3 %all_gather.3 = bf16[1024,128]{1,0:T(8,128)(2,1)S(1)} all-gather(bf16[32,128]{1,0:T(8,128)(2,1)S(1)} %convert_element_type.25), channel_id=1, replica_groups=mesh['slab'=8,'angle'=32] {'angle'}, dimensions={0}, use_global_device_ids=true | all-gather | bytes 270336 | tf_op jit(solution)/shard_map/all_gather | solution.py:19
  60.0 0.8 gather_fusion
  60.7 0.1 copy.11
  60.8 0.8 fusion.7
  61.6 6.1 %convolution_multiply_fusion = f32[192,2,128]{2,1,0:T(2,128)S(1)} fusion(bf16[192,128,128]{2,1,0:T(8,128)(2,1)} %param.8, f32[192,128]{1,0:T(8,128)S(1)} %fusion.7, bf16[192,1,128]{2,1,0:T(2,128)(2,1)S(1)} %copy.11), kind=kOutput, calls=%fused_computation.3 | convolution fusion | flops 12632064 | bytes 6635520 | tf_op jit(solution)/shard_map/bpv,bkv->bkp/dot_general | solution.py:22
  67.7 0.0 copy-done.4
  67.7 0.9 fusion
  68.6 0.0 all-reduce.5.cloned.1.call-update
  68.6 0.0 all-reduce.7.cloned.1.call-start
  68.7 0.0 copy-done.3
  68.7 0.3 compare_convert_fusion
  69.0 62.0 %all-reduce.5.cloned.1.call-done = f32[64,2,128]{2,0,1:T(8,128)} async-done(((f32[64,2,128]{2,0,1:T(8,128)}), f32[64,2,128]{2,0,1:T(8,128)}) %all-reduce.5.cloned.1.call-update) | async-done | bytes 65552 | tf_op jit(solution)/shard_map/psum | solution.py:28
  131.0 0.0 copy-done.2
  131.0 1.4 fusion.17
  132.4 0.8 gather_fusion.1
  133.2 0.3 compare_select_fusion
  133.4 4.5 %fusion.2 = f32[192,2,128]{2,1,0:T(2,128)S(1)} fusion(bf16[192,128,128]{2,1,0:T(8,128)(2,1)} %param.8, bf16[192,1,128]{2,1,0:T(2,128)(2,1)S(1)} %compare_convert_fusion, bf16[192,1,128]{2,1,0:T(2,128)(2,1)S(1)} %compare_select_fusion), kind=kOutput, calls=%fused_computation.8 | convolution fusion | flops 12779520 | bytes 6586368 | tf_op jit(solution)/shard_map/bpv,bkp->bkv/dot_general | solution.py:34
  138.0 0.3 broadcast_in_dim.6
  138.2 7.2 %scatter_fusion = f32[1024,2,128]{2,1,0:T(2,128)S(1)} fusion(f32[1024,2,128]{2,1,0:T(2,128)S(1)} %broadcast_in_dim.6, s32[192]{0:T(256)S(1)} %compare_select_fusion.2, f32[192,2,128]{2,1,0:T(2,128)S(1)} %fusion.2), kind=kCustom, calls=%fused_computation.2 | custom fusion | flops 49152 | bytes 590592 | tf_op jit(solution)/shard_map/scatter-add | solution.py:35
  145.4 1.0 copy-done
  146.4 0.0 all-reduce.7.cloned.1.call-update
  146.5 0.6 dynamic-slice
  147.7 146.4 %all-reduce.7.cloned.1.call-done = f32[1024,2,128]{2,1,0:T(2,128)} async-done(((f32[1024,2,128]{2,1,0:T(2,128)}), f32[1024,2,128]{2,1,0:T(2,128)}) %all-reduce.7.cloned.1.call-update) | async-done | bytes 1048592
  294.2 0.9 fusion.14
  295.0 0.0 copy-done.1
  295.0 0.6 add.24
  (7 shorter events, 0.0 us)
Async XLA Ops:
  7.2 61.5 %copy-start.3 = (s32[192]{0:T(256)S(1)}, s32[192]{0:T(256)}, u32[]{:S(2)}) copy-start(s32[192]{0:T(256)} %param.11) | copy-start | bytes 2308
  7.2 60.5 %copy-start.4 = (s32[192]{0:T(256)S(1)}, s32[192]{0:T(256)}, u32[]{:S(2)}) copy-start(s32[192]{0:T(256)} %param.10) | copy-start | bytes 2308
  7.2 123.8 %copy-start.2 = (f32[64,128]{1,0:T(8,128)S(1)}, f32[64,128]{1,0:T(8,128)}, u32[]{:S(2)}) copy-start(f32[64,128]{1,0:T(8,128)} %param.7) | copy-start | bytes 98308
  7.2 123.8 %all-reduce.5.cloned.1.call-start = ((), (), s32[]{:S(2)}) async-start(), calls=%async_computation | async-start | bytes 131072 | tf_op jit(solution)/shard_map/psum | solution.py:28
  67.7 78.8 %copy-start.5 = (u32[256]{0:T(256)S(1)}, u32[256]{0:T(256)}, u32[]{:S(2)}) copy-start(u32[256]{0:T(256)} %constant.24) | copy-start | bytes 3076
  67.7 227.3 %copy-start.1 = (f32[32,128]{1,0:T(8,128)S(1)}, f32[32,128]{1,0:T(8,128)}, u32[]{:S(2)}) copy-start(f32[32,128]{1,0:T(8,128)} %param.6) | copy-start | bytes 49156
  68.6 225.6 %all-reduce.7.cloned.1.call-start = ((), (), s32[]{:S(2)}) async-start(), calls=%async_computation.1 | async-start | bytes 2097152
  145.4 1.0 copy-start
Sparse Core Ops, SparseCore 0:
  68.7 62.1 all-reduce.4
  146.6 147.5 all-reduce.6
where the time goes:
time: 304 us; the launch traced here: 302 us
  waiting for transfers between devices  208 us (68%)
  blocking collectives  51.3 us (17%)
  between operations  14.8 us (5%)
  other arithmetic  12.8 us (4%)
  matrix products  11.5 us (4%)
  local copies, waits for them, and re-layouts  3.54 us (1%)
    unnamed x3, waiting for transfers between devices  146 us
    psum x1, waiting for transfers between devices, on_device(): summed = lax.psum(partial_sums, 'slab')  62 us
    all_gather x1, blocking collectives, on_device(): slab_values = lax.all_gather(coarse, 'angle', axis=0, tiled=True)  51.3 us
    scatter-add x1, other arithmetic, on_device(): jnp.zeros((slab_blocks, 2, width), jnp.float32).at[block_voxel]  7.17 us
    dot_general x1, matrix products, on_device(): jnp.einsum('bpv,bkv->bkp', footprint, stacked, preferred_element_type=jnp...  6.11 us
  transfers between devices with their start and end apart: 2, of which 2 were waited for; matrix products, arithmetic and copies ran while one was open for 0% of the time, Pallas kernels for 0%

commit v1 on v0

v1 whole, which is shorter than its diff:
```python
import jax
import jax.numpy as jnp
from jax import lax
from jax.experimental import pallas as pl
from jax.experimental.pallas import tpu as pltpu
from jax.sharding import PartitionSpec as P

BLK = 128
NB = 192
CAP = 12
GROUP = 16
F32 = jnp.float32
BF16 = jnp.bfloat16
VMEM = pl.BlockSpec(memory_space=pltpu.VMEM)
SMEM = pl.BlockSpec(memory_space=pltpu.SMEM)
PARAMS = pltpu.CompilerParams(vmem_limit_bytes=40 * 1024 * 1024)


def dot(a, b, contract=((1,), (0,))):
    return lax.dot_general(a, b, (contract, ((), ())), preferred_element_type=F32)


def split3(x):
    hi = x.astype(BF16)
    rest = x - hi.astype(F32)
    mid = rest.astype(BF16)
    lo = (rest - mid.astype(F32)).astype(BF16)
    return jnp.concatenate([hi, mid, lo], axis=1)


def exact_dot(onehot, x):
    n = x.shape[1]
    y = dot(onehot, split3(x))
    return y[:, :n] + (y[:, n : 2 * n] + y[:, 2 * n :])


def forward_kernel(slab_ref, voxel_hot_ref, tile_hot_t_ref, live_ref, foot_ref, part_ref, slots):
    values = slab_ref[:, 0:32, :].reshape(1024, BLK)
    picked = dot(voxel_hot_ref[...], values).astype(BF16)
    slots[:, 0:BLK] = picked.astype(F32)
    row = lax.broadcasted_iota(jnp.int32, (GROUP, BLK), 0)
    ones = jnp.ones((GROUP, BLK), BF16)

    @pl.loop(0, NB // GROUP)
    def _(g):
        at = pl.ds(pl.multiple_of(g * GROUP, GROUP), GROUP)
        lhs = jnp.concatenate([slots[at, 0:BLK].astype(BF16), ones], axis=0)
        proj = jnp.zeros((GROUP, BLK), F32)
        rsum = jnp.zeros((GROUP, BLK), F32)
        for i in range(GROUP):
            out = dot(lhs, foot_ref[g * GROUP + i], ((1,), (1,)))
            proj = jnp.where(row == i, out[:GROUP], proj)
            rsum = jnp.where(row == i, out[GROUP:], rsum)
        live = live_ref[at, :].astype(F32)
        slots[at, 0:BLK] = proj * live
        slots[at, BLK:] = rsum * live

    part_ref[...] = exact_dot(tile_hot_t_ref[...], slots[...])


def backward_kernel(share_ref, parts_ref, measured_ref, tile_hot_ref, live_ref, foot_ref, weighted_ref, send_ref, rows, backs):
    total = jnp.sum(parts_ref[...], axis=0)
    weighted = (measured_ref[...] - total[:, :BLK]) / jnp.maximum(total[:, BLK:], 1.0)
    weighted_ref[...] = weighted
    rows[...] = dot(tile_hot_ref[...], weighted.astype(BF16))
    row = lax.broadcasted_iota(jnp.int32, (GROUP, BLK), 0)

    @pl.loop(0, NB // GROUP)
    def _(g):
        at = pl.ds(pl.multiple_of(g * GROUP, GROUP), GROUP)
        live = live_ref[at, :].astype(F32)
        res = rows[at, :] * live
        diag = jnp.concatenate(
            [
                jnp.concatenate([jnp.where(row == i, res, 0.0), jnp.where(row == i, live, 0.0)], axis=0)
                for i in range(GROUP)
            ],
            axis=1,
        ).astype(BF16)
        foot = foot_ref[pl.ds(g * GROUP, GROUP)].reshape(GROUP * BLK, BLK)
        out = dot(diag, foot)
        backs[0, at, :] = out[:GROUP]
        backs[1, at, :] = out[GROUP:]

    send_ref[...] = jnp.zeros_like(send_ref)
    for j in range(NB // CAP):
        share = share_ref[j]
        send_ref[share, 0:CAP, :] = backs[0, CAP * j : CAP * (j + 1), :]
        send_ref[share, CAP : 2 * CAP, :] = backs[1, CAP * j : CAP * (j + 1), :]


def update_kernel(recv_ref, hot_ref, volume_ref, out_ref):
    received = recv_ref[...].reshape(32 * 2 * CAP, BLK)
    summed = exact_dot(hot_ref[...], received)
    out_ref[...] = volume_ref[...] + summed[:32] / jnp.maximum(summed[32:], 1.0)


def on_device(volume, measured, footprint, block_voxel, block_tile, block_rows):
    iota = lambda n: jnp.arange(n, dtype=jnp.int32)
    groups = NB // CAP
    share = block_voxel.reshape(groups, CAP)[:, 0] // 32
    within = block_voxel.reshape(groups, CAP) % 32

    coarse = volume.astype(BF16)
    named = (share[None, :] == iota(32)[:, None]).astype(F32)
    places = jnp.sum(named[:, :, None] * within.astype(F32)[None], axis=1)
    places = jnp.pad(places, ((0, 0), (0, BLK - CAP))).astype(BF16)
    send = jnp.concatenate([jnp.broadcast_to(coarse, (32, 32, BLK)), places[:, None, :]], axis=1)
    slab_values = lax.all_to_all(send, "angle", 0, 0)

    voxel_hot = (block_voxel[:, None] == iota(1024)[None, :]).astype(BF16)
    tile_hot = (block_tile[:, None] == iota(64)[None, :]).astype(BF16)
    tile_hot_t = (block_tile[None, :] == iota(64)[:, None]).astype(BF16)
    live = (iota(BLK)[None, :] < block_rows[:, None]).astype(BF16)

    part = pl.pallas_call(
        forward_kernel,
        out_shape=jax.ShapeDtypeStruct((64, 2 * BLK), F32),
        in_specs=[VMEM] * 5,
        out_specs=VMEM,
        scratch_shapes=[pltpu.VMEM((NB, 2 * BLK), F32)],
        compiler_params=PARAMS,
        name="forward",
    )(slab_values, voxel_hot, tile_hot_t, live, footprint)

    part = part + lax.ppermute(part, "slab", [(i, i ^ 1) for i in range(8)])
    same_core = [[2 * y + c for y in range(4)] for c in range(2)]
    parts = lax.all_to_all(jnp.broadcast_to(part, (4, 64, 2 * BLK)), "slab", 0, 0, axis_index_groups=same_core)

    weighted, send_back = pl.pallas_call(
        backward_kernel,
        out_shape=(
            jax.ShapeDtypeStruct((64, BLK), F32),
            jax.ShapeDtypeStruct((32, 2 * CAP, BLK), F32),
        ),
        in_specs=[SMEM] + [VMEM] * 5,
        out_specs=(VMEM, VMEM),
        scratch_shapes=[pltpu.VMEM((NB, BLK), F32), pltpu.VMEM((2, NB, BLK), F32)],
        compiler_params=PARAMS,
        name="backward",
    )(share, parts, measured, tile_hot, live, footprint)

    received = lax.all_to_all(send_back, "angle", 0, 0)

    place = slab_values[:, 32, :CAP].astype(jnp.int32)
    none = jnp.full_like(place, -1)
    hot_back = jnp.concatenate([place, none], axis=1).reshape(1, -1) == iota(32)[:, None]
    hot_cols = jnp.concatenate([none, place], axis=1).reshape(1, -1) == iota(32)[:, None]
    hot = jnp.concatenate([hot_back, hot_cols], axis=0).astype(BF16)
    new_volume = pl.pallas_call(
        update_kernel,
        out_shape=jax.ShapeDtypeStruct((32, BLK), F32),
        in_specs=[VMEM] * 3,
        out_specs=VMEM,
        compiler_params=PARAMS,
        name="update",
    )(received, hot, volume)
    return new_volume, weighted


def solution(mesh):
    in_specs = (
        P(("slab", "angle"), None),
        P("angle", None),
        P(("slab", "angle"), None, None),
        P(("slab", "angle")),
        P(("slab", "angle")),
        P(("slab", "angle")),
    )
    out_specs = (P(("slab", "angle"), None), P("angle", None))
    return jax.shard_map(
        on_device, mesh=mesh, in_specs=in_specs, out_specs=out_specs, check_vma=False
    )
```

time: 304 us -> 76.1 us (0.25)
  waiting for transfers between devices: 208 us -> 32.5 us
  blocking collectives: 51.3 us -> 0 us
  starting transfers between devices: 0.08 us -> 20.5 us
  between operations: 14.8 us -> 0.79 us
  matrix products: 11.5 us -> 0 us
  Pallas kernels: 0 us -> 9.93 us
  other arithmetic: 12.8 us -> 4.11 us
  local copies, waits for them, and re-layouts: 3.54 us -> 7.64 us
    unnamed x3 -> x0, waiting for transfers between devices: 146 us -> none
    psum x1 -> x0, waiting for transfers between devices: 62 us -> none  [on_device(): summed = lax.psum(partial_sums, 'slab')]
    all_gather x1 -> x0, blocking collectives: 51.3 us -> none  [on_device(): slab_values = lax.all_gather(coarse, 'angle', axis=0, tiled=True)]
    all_to_all x0 -> x3, waiting for transfers between devices: none -> 31.3 us  [the longest x1 13.3 us: on_device(): received = lax.all_to_all(send_back, 'angle', 0, 0)]
    all_to_all x0 -> x3, starting transfers between devices: none -> 20.4 us  [the longest x1 11.2 us: on_device(): slab_values = lax.all_to_all(send, 'angle', 0, 0)]
    dot_general x3 -> x0, matrix products: 11.5 us -> none  [the longest x1 6.11 us: on_device(): jnp.einsum('bpv,bkv->bkp', footprint, stacked, preferred_element_type=jnp...]
    pallas_call x0 -> x3, Pallas kernels: none -> 9.93 us  [the longest x1 5.12 us: on_device(): pl.pallas_call(forward_kernel, out_shape=jax.ShapeDtypeStruct((64, 2 * BL...]
    scatter-add x1 -> x0, other arithmetic: 7.17 us -> none  [on_device(): jnp.zeros((slab_blocks, 2, width), jnp.float32).at[block_voxel]]
  transfers between devices with their start and end apart: 2 -> 4, of which waited for: 2 -> 4; matrix products, arithmetic and copies ran while one was open for 0% -> 4% of each run, Pallas kernels for 0% -> 0%
where the time goes in v1:
time: 76.1 us; the launch traced here: 75.5 us
  waiting for transfers between devices  32.5 us (43%)
  starting transfers between devices  20.5 us (27%)
  Pallas kernels  9.93 us (13%)
  local copies, waits for them, and re-layouts  7.64 us (10%)
  other arithmetic  4.11 us (5%)
  between operations  0.79 us (1%)
    all_to_all x1, waiting for transfers between devices, on_device(): received = lax.all_to_all(send_back, 'angle', 0, 0)  13.3 us
    all_to_all x1, starting transfers between devices, on_device(): slab_values = lax.all_to_all(send, 'angle', 0, 0)  11.2 us
    all_to_all x1, waiting for transfers between devices, on_device(): slab_values = lax.all_to_all(send, 'angle', 0, 0)  11.1 us
    all_to_all x1, waiting for transfers between devices, on_device(): lax.all_to_all(jnp.broadcast_to(part, (4, 64, 2 * BLK)), 'slab', 0, 0, ax...  6.89 us
    unnamed x10, local copies, waits for them, and re-layouts  5.58 us
    pallas_call x1, Pallas kernels, on_device(): pl.pallas_call(forward_kernel, out_shape=jax.ShapeDtypeStruct((64, 2 * BL...  5.12 us
    all_to_all x1, starting transfers between devices, on_device(): received = lax.all_to_all(send_back, 'angle', 0, 0)  4.76 us
    all_to_all x1, starting transfers between devices, on_device(): lax.all_to_all(jnp.broadcast_to(part, (4, 64, 2 * BLK)), 'slab', 0, 0, ax...  4.47 us
  transfers between devices with their start and end apart: 4, of which 4 were waited for; matrix products, arithmetic and copies ran while one was open for 4% of the time, Pallas kernels for 0%

profile of v1, /device:TPU:32, one launch (start us, length us, event | category | flops | bytes accessed | tf_op | source)
XLA Modules:
  0.0 75.5 jit_solution(1714227325766121538)
XLA Ops:
  0.6 0.0 copy-start.4
  0.6 0.0 copy-start.3
  0.7 0.8 %reshape.88 = s32[16,12]{1,0:T(8,128)S(1)} reshape(s32[192]{0:T(256)} %param.9) | data formatting | bytes 1536 | tf_op jit(solution)/shard_map/reshape | solution.py:101
  1.4 0.1 slice_reduce_fusion
  1.6 0.1 fusion.6
  1.6 0.1 copy.11
  1.7 0.1 multiply_reduce_fusion
  1.9 0.1 copy.13
  2.0 0.7 convert_element_type.41
  2.7 0.8 pad_maximum_fusion
  3.5 11.2 %all-to-all-start = ((bf16[32,33,128]{2,1,0:T(8,128)(2,1)}), bf16[32,33,128]{2,1,0:T(8,128)(2,1)S(1)}, u32[]{:S(2)}, u32[]{:S(2)}) async-start(bf16[32,33,128]{2,1,0:T(8,128)(2,1)} %pad_maximum_fusion), calls=%async_computation | async-start | bytes 655360 | tf_op jit(solution)/shard_map/all_to_all | solution.py:109
  14.7 0.7 fusion.3.tile_hot_t_ref
  15.4 0.8 %fusion.1.live_ref = bf16[192,128]{1,0:T(8,128)(2,1)S(1)} fusion(s32[192]{0:T(256)} %param.11), kind=kLoop, calls=%fused_computation.9 | loop fusion | flops 49152 | bytes 49920 | tf_op jit(solution)/shard_map/convert_element_type | solution.py:114
  16.1 0.8 %fusion.voxel_hot_ref = bf16[192,1024]{1,0:T(8,128)(2,1)S(1)} fusion(s32[192]{0:T(256)} %param.9), kind=kLoop, calls=%fused_computation.1 | loop fusion | flops 393216 | bytes 393984 | tf_op jit(solution)/shard_map/convert_element_type | solution.py:111
  17.0 11.1 %all-to-all-done.slab_ref = bf16[32,33,128]{2,1,0:T(8,128)(2,1)S(1)} async-done(((bf16[32,33,128]{2,1,0:T(8,128)(2,1)}), bf16[32,33,128]{2,1,0:T(8,128)(2,1)S(1)}, u32[]{:S(2)}, u32[]{:S(2)}) %all-to-all-start) | async-done | bytes 270368 | tf_op jit(solution)/shard_map/all_to_all | solution.py:109
  28.1 2.8 %copy-done = bf16[192,128,128]{2,1,0:T(8,128)(2,1)S(1)} copy-done((bf16[192,128,128]{2,1,0:T(8,128)(2,1)S(1)}, bf16[192,128,128]{2,1,0:T(8,128)(2,1)}, u32[]{:S(2)}) %copy-start) | copy-done | bytes 6291480
  30.9 5.1 %forward.1 = f32[64,256]{1,0:T(8,128)S(1)} custom-call(bf16[32,33,128]{2,1,0:T(8,128)(2,1)S(1)} %all-to-all-done.slab_ref, bf16[192,1024]{1,0:T(8,128)(2,1)S(1)} %fusion.voxel_hot_ref, bf16[64,192]{1,0:T(8,128)(2,1)S(1)} %fusion.3.tile_hot_t_ref, bf16[192,128]{1,0:T(8,128)(2,1)S(1)} %fusion.1.live_ref, bf16[192,128,128]{2,1,0:T(8,128)(2,1)S(1)} %copy-done), custom_call_target="tpu_custom_call" | custom-call | tf_op jit(solution)/shard_map/forward/pallas_call | solution.py:116
  36.0 0.1 collective-permute-start
  36.1 1.2 %collective-permute-done = f32[64,256]{1,0:T(8,128)S(1)} collective-permute-done((f32[64,256]{1,0:T(8,128)S(1)}, f32[64,256]{1,0:T(8,128)S(1)}, u32[]{:S(2)}, u32[]{:S(2)}) %collective-permute-start) | collective-permute-done | bytes 65568 | tf_op jit(solution)/shard_map/ppermute | solution.py:126
  37.4 0.7 broadcast_in_dim.8
  38.1 4.5 %all-to-all-start.1 = ((f32[4,64,256]{2,1,0:T(8,128)}), f32[4,64,256]{2,1,0:T(8,128)S(1)}, u32[]{:S(2)}, u32[]{:S(2)}) async-start(f32[4,64,256]{2,1,0:T(8,128)} %broadcast_in_dim.8), calls=%async_computation.1 | async-start | bytes 524288 | tf_op jit(solution)/shard_map/all_to_all | solution.py:128
  42.5 0.1 fusion.2.tile_hot_ref
  42.6 6.9 %all-to-all-done.1.parts_ref = f32[4,64,256]{2,1,0:T(8,128)S(1)} async-done(((f32[4,64,256]{2,1,0:T(8,128)}), f32[4,64,256]{2,1,0:T(8,128)S(1)}, u32[]{:S(2)}, u32[]{:S(2)}) %all-to-all-start.1) | async-done | bytes 262176 | tf_op jit(solution)/shard_map/all_to_all | solution.py:128
  49.5 2.8 %copy-done.1 = bf16[192,128,128]{2,1,0:T(8,128)(2,1)S(1)} copy-done((bf16[192,128,128]{2,1,0:T(8,128)(2,1)S(1)}, bf16[192,128,128]{2,1,0:T(8,128)(2,1)}, u32[]{:S(2)}) %copy-start.1) | copy-done | bytes 6291480
  52.3 4.0 %backward.1 = (f32[64,128]{1,0:T(8,128)}, f32[32,24,128]{2,1,0:T(8,128)}) custom-call(s32[16]{0:T(128)S(1)} %and_select_fusion.share_ref, f32[4,64,256]{2,1,0:T(8,128)S(1)} %all-to-all-done.1.parts_ref, f32[64,128]{1,0:T(8,128)S(1)} %copy-done.3, bf16[192,64]{1,0:T(8,128)(2,1)S(1)} %fusion.2.tile_hot_ref, bf16[192,128]{1,0:T(8,128)(2,1)S(1)} %fusion.1.live_ref, ...), custom_call_target="tpu_custom_call" | custom-call | tf_op jit(solution)/shard_map/backward/pallas_call | solution.py:130
  56.3 4.8 %all-to-all-start.2 = ((f32[32,24,128]{2,1,0:T(8,128)}), f32[32,24,128]{2,1,0:T(8,128)S(1)}, u32[]{:S(2)}, u32[]{:S(2)}) async-start(f32[32,24,128]{2,1,0:T(8,128)} %get-tuple-element.4), calls=%async_computation.2 | async-start | bytes 786432 | tf_op jit(solution)/shard_map/all_to_all | solution.py:143
  61.1 0.1 fusion.7
  61.2 0.1 eq.100
  61.2 0.1 eq.104
  61.4 13.3 %all-to-all-done.2.recv_ref = f32[32,24,128]{2,1,0:T(8,128)S(1)} async-done(((f32[32,24,128]{2,1,0:T(8,128)}), f32[32,24,128]{2,1,0:T(8,128)S(1)}, u32[]{:S(2)}, u32[]{:S(2)}) %all-to-all-start.2) | async-done | bytes 393248 | tf_op jit(solution)/shard_map/all_to_all | solution.py:143
  74.6 0.0 copy-done.2
  74.7 0.8 %update.1 = f32[32,128]{1,0:T(8,128)} custom-call(f32[32,24,128]{2,1,0:T(8,128)S(1)} %all-to-all-done.2.recv_ref, bf16[64,768]{1,0:T(8,128)(2,1)S(1)} %add_convert_fusion.hot_ref, f32[32,128]{1,0:T(8,128)S(1)} %copy-done.2), custom_call_target="tpu_custom_call" | custom-call | tf_op jit(solution)/shard_map/update/pallas_call | solution.py:150
  (13 shorter events, 0.1 us)
Async XLA Ops:
  0.6 41.9 %copy-start.4 = (s32[192]{0:T(256)S(1)}, s32[192]{0:T(256)}, u32[]{:S(2)}) copy-start(s32[192]{0:T(256)} %param.10) | copy-start | bytes 2308
  0.6 48.9 %copy-start.3 = (f32[64,128]{1,0:T(8,128)S(1)}, f32[64,128]{1,0:T(8,128)}, u32[]{:S(2)}) copy-start(f32[64,128]{1,0:T(8,128)} %measured_ref.1) | copy-start | bytes 98308
  3.5 24.6 %all-to-all-start = ((bf16[32,33,128]{2,1,0:T(8,128)(2,1)}), bf16[32,33,128]{2,1,0:T(8,128)(2,1)S(1)}, u32[]{:S(2)}, u32[]{:S(2)}) async-start(bf16[32,33,128]{2,1,0:T(8,128)(2,1)} %pad_maximum_fusion), calls=%async_computation | async-start | bytes 655360 | tf_op jit(solution)/shard_map/all_to_all | solution.py:109
  28.1 2.8 %copy-start = (bf16[192,128,128]{2,1,0:T(8,128)(2,1)S(1)}, bf16[192,128,128]{2,1,0:T(8,128)(2,1)}, u32[]{:S(2)}) copy-start(bf16[192,128,128]{2,1,0:T(8,128)(2,1)} %foot_ref.3) | copy-start | bytes 18874372
  30.9 43.8 %copy-start.2 = (f32[32,128]{1,0:T(8,128)S(1)}, f32[32,128]{1,0:T(8,128)}, u32[]{:S(2)}) copy-start(f32[32,128]{1,0:T(8,128)} %volume_ref.1) | copy-start | bytes 49156
  36.0 1.3 %collective-permute-start = (f32[64,256]{1,0:T(8,128)S(1)}, f32[64,256]{1,0:T(8,128)S(1)}, u32[]{:S(2)}, u32[]{:S(2)}) collective-permute-start(f32[64,256]{1,0:T(8,128)S(1)} %forward.1), channel_id=1, source_target_pairs={{0,32},{32,0},{64,96},{96,64},{128,160},{160,128},{192,224},{224,1... | collective-permute-start | bytes 196616 | tf_op jit(solution)/shard_map/ppermute | solution.py:126
  38.1 11.5 %all-to-all-start.1 = ((f32[4,64,256]{2,1,0:T(8,128)}), f32[4,64,256]{2,1,0:T(8,128)S(1)}, u32[]{:S(2)}, u32[]{:S(2)}) async-start(f32[4,64,256]{2,1,0:T(8,128)} %broadcast_in_dim.8), calls=%async_computation.1 | async-start | bytes 524288 | tf_op jit(solution)/shard_map/all_to_all | solution.py:128
  49.5 2.8 %copy-start.1 = (bf16[192,128,128]{2,1,0:T(8,128)(2,1)S(1)}, bf16[192,128,128]{2,1,0:T(8,128)(2,1)}, u32[]{:S(2)}) copy-start(bf16[192,128,128]{2,1,0:T(8,128)(2,1)} %foot_ref.3) | copy-start | bytes 18874372
  56.3 18.4 %all-to-all-start.2 = ((f32[32,24,128]{2,1,0:T(8,128)}), f32[32,24,128]{2,1,0:T(8,128)S(1)}, u32[]{:S(2)}, u32[]{:S(2)}) async-start(f32[32,24,128]{2,1,0:T(8,128)} %get-tuple-element.4), calls=%async_computation.2 | async-start | bytes 786432 | tf_op jit(solution)/shard_map/all_to_all | solution.py:143

commit v2 on v0

v2 whole, which is shorter than its diff:
```python
import jax
import jax.numpy as jnp
from jax import lax
from jax.experimental import pallas as pl
from jax.experimental.pallas import tpu as pltpu
from jax.sharding import PartitionSpec as P

BLK = 128
NB = 192
CAP = 12
SHARES = 32
HALF = NB // 2
F32 = jnp.float32
BF16 = jnp.bfloat16
VMEM = pl.BlockSpec(memory_space=pltpu.VMEM)
SMEM = pl.BlockSpec(memory_space=pltpu.SMEM)
HBM = pl.BlockSpec(memory_space=pltpu.HBM)
PARAMS = pltpu.CompilerParams(vmem_limit_bytes=40 * 1024 * 1024)
ROWS = ((1,), (0,))
LANES = ((1,), (1,))
SUBLANES = ((0,), (0,))


def dot(a, b, contract=ROWS):
    return lax.dot_general(a, b, (contract, ((), ())), preferred_element_type=F32)


def iota(shape, dim):
    return lax.broadcasted_iota(jnp.int32, shape, dim)


def exact_dot(onehot, x, contract=ROWS):
    hi = x.astype(BF16)
    rest = x - hi.astype(F32)
    mid = rest.astype(BF16)
    lo = (rest - mid.astype(F32)).astype(BF16)
    return dot(onehot, hi, contract) + (dot(onehot, mid, contract) + dot(onehot, lo, contract))


def offer_kernel(voxel_any, volume_any, foot_any, send_ref, voxel_ref, volume_ref, sems):
    copies = [
        pltpu.make_async_copy(volume_any, volume_ref, sems.at[0]),
        pltpu.make_async_copy(voxel_any, voxel_ref, sems.at[1]),
    ]
    for copy in copies:
        copy.start()
    copies[0].wait()
    coarse = volume_ref[...].astype(BF16)
    for d in range(SHARES):
        send_ref[d, 0:32, :] = coarse
        send_ref[d, 32:40, :] = jnp.zeros((8, BLK), BF16)
    copies[1].wait()
    spot = iota((8, BLK), 0) * BLK + iota((8, BLK), 1) - 2 * CAP * lax.axis_index("angle")
    for j in range(NB // CAP):
        places = jnp.zeros((8, BLK), jnp.int32)
        for i in range(CAP):
            place = (voxel_ref[CAP * j + i] & 31) + 1
            places = jnp.where(spot == i, place, places)
            places = jnp.where(spot == CAP + i, place + 32, places)
        send_ref[voxel_ref[CAP * j] >> 5, 32:40, :] = places.astype(F32).astype(BF16)


def forward_kernel(slab_ref, voxel_ref, tile_ref, rows_ref, foot_ref, part_ref, places_ref):
    places_ref[...] = jnp.sum(slab_ref[:, 32:40, :].astype(F32), axis=0)
    voxel = voxel_ref[...].reshape(1, NB)
    tile = tile_ref[...].reshape(1, NB)
    rows = rows_ref[...].reshape(1, NB)
    voxel_hot = jnp.where(iota((1024, NB), 0) == voxel, 1.0, 0.0).astype(BF16)
    picked = dot(slab_ref[:, 0:32, :].reshape(1024, BLK), voxel_hot, SUBLANES)
    lane = iota((1, BLK), 1)
    even = lane % 2 == 0
    one = jnp.ones((BLK, BLK), F32)
    ones = jnp.concatenate([jnp.where(even, one, 0.0), jnp.where(even, 0.0, one)], axis=0)
    sums = []
    for h in range(2):
        mine = jnp.concatenate([picked[:, HALF * h : HALF * (h + 1)], jnp.zeros((BLK, 32), F32)], axis=1)
        cols = jnp.concatenate([jnp.where(even, mine, 0.0), jnp.where(even, 0.0, mine)], axis=0)
        cols = jnp.concatenate([cols, ones], axis=1).astype(BF16)
        total = jnp.zeros((BLK, 2 * BLK), F32)
        for q in range(HALF // 2):
            k = HALF * h + 2 * q
            pair = jnp.concatenate([foot_ref[k], foot_ref[k + 1]], axis=1)
            both = iota((1, 2 * BLK), 1) % BLK // 2 == q
            total = jnp.where(both, dot(pair, cols), total)
        sums.append(total)
    live = iota((BLK, NB), 0) < rows
    tile_hot = jnp.where(iota((64, NB), 0) == tile, 1.0, 0.0).astype(BF16)
    for n in range(2):
        both = jnp.concatenate([s[:, BLK * n : BLK * n + HALF] for s in sums], axis=1)
        part_ref[:, BLK * n : BLK * (n + 1)] = exact_dot(tile_hot, jnp.where(live, both, 0.0), LANES)


def spread_kernel(mine_ref, other_ref, out_ref):
    both = mine_ref[...] + other_ref[...]
    for y in range(4):
        out_ref[y] = both


def backward_kernel(voxel_ref, parts_ref, measured_ref, tile_ref, rows_ref, foot_ref, weighted_ref, send_ref):
    total = (parts_ref[0] + parts_ref[1]) + (parts_ref[2] + parts_ref[3])
    weighted = (measured_ref[...] - total[:, :BLK]) / jnp.maximum(total[:, BLK:], 1.0)
    weighted_ref[...] = weighted
    tile = tile_ref[...].reshape(1, NB)
    rows = rows_ref[...].reshape(1, NB)
    tile_hot = jnp.where(iota((64, NB), 0) == tile, 1.0, 0.0).astype(BF16)
    live = jnp.where(iota((BLK, NB), 0) < rows, 1.0, 0.0).T
    res = dot(tile_hot, weighted.astype(BF16), SUBLANES) * live
    send_ref[...] = jnp.zeros_like(send_ref)
    row = iota((2 * CAP, BLK), 0) % CAP
    for j in range(NB // CAP):
        at = slice(CAP * j, CAP * (j + 1))
        both = jnp.concatenate([res[at], live[at]], axis=0)
        diag = jnp.concatenate([jnp.where(row == i, both, 0.0) for i in range(CAP)], axis=1).astype(BF16)
        foot = foot_ref[at].reshape(CAP * BLK, BLK)
        send_ref[voxel_ref[CAP * j] >> 5] = dot(diag, foot)


def update_kernel(recv_ref, places_ref, volume_ref, out_ref):
    wanted = (iota((2 * 32, BLK), 0) + 1).astype(F32)
    hot = jnp.concatenate(
        [jnp.where(places_ref[m : m + 1, :] == wanted, 1.0, 0.0) for m in range(SHARES * 2 * CAP // BLK)], axis=1
    ).astype(BF16)
    summed = exact_dot(hot, recv_ref[...].reshape(SHARES * 2 * CAP, BLK))
    out_ref[...] = volume_ref[...] + summed[:32] / jnp.maximum(summed[32:], 1.0)


def call(kernel, name, out, specs, *args):
    out = [jax.ShapeDtypeStruct(*o) for o in out]
    return pl.pallas_call(
        kernel, out_shape=out, in_specs=specs, out_specs=[VMEM] * len(out), compiler_params=PARAMS, name=name
    )(*args)


def on_device(volume, measured, footprint, block_voxel, block_tile, block_rows):
    (offer,) = pl.pallas_call(
        offer_kernel,
        out_shape=[jax.ShapeDtypeStruct((SHARES, 40, BLK), BF16)],
        in_specs=[HBM] * 3,
        out_specs=[VMEM],
        scratch_shapes=[pltpu.SMEM((NB,), jnp.int32), pltpu.VMEM((32, BLK), F32), pltpu.SemaphoreType.DMA((2,))],
        compiler_params=PARAMS,
        name="offer",
    )(*(pltpu.with_memory_space_constraint(x, pltpu.HBM) for x in (block_voxel, volume, footprint)))
    slab_values = lax.all_to_all(offer, "angle", 0, 0)

    part, places = call(
        forward_kernel,
        "forward",
        [((64, 2 * BLK), F32), ((8, BLK), F32)],
        [VMEM] * 5,
        slab_values, block_voxel, block_tile, block_rows, footprint,
    )
    other = lax.ppermute(part, "slab", [(i, i ^ 1) for i in range(8)])
    (spread,) = call(spread_kernel, "spread", [((4, 64, 2 * BLK), F32)], [VMEM] * 2, part, other)
    same_core = [[2 * y + c for y in range(4)] for c in range(2)]
    parts = lax.all_to_all(spread, "slab", 0, 0, axis_index_groups=same_core)

    weighted, send_back = call(
        backward_kernel,
        "backward",
        [((64, BLK), F32), ((SHARES, 2 * CAP, BLK), F32)],
        [SMEM] + [VMEM] * 5,
        block_voxel, parts, measured, block_tile, block_rows, footprint,
    )
    received = lax.all_to_all(send_back, "angle", 0, 0)
    (new_volume,) = call(update_kernel, "update", [((32, BLK), F32)], [VMEM] * 3, received, places, volume)
    return new_volume, weighted


def solution(mesh):
    in_specs = (
        P(("slab", "angle"), None),
        P("angle", None),
        P(("slab", "angle"), None, None),
        P(("slab", "angle")),
        P(("slab", "angle")),
        P(("slab", "angle")),
    )
    out_specs = (P(("slab", "angle"), None), P("angle", None))
    return jax.shard_map(
        on_device, mesh=mesh, in_specs=in_specs, out_specs=out_specs, check_vma=False
    )
```

time: 304 us -> 62.7 us (0.21)
  waiting for transfers between devices: 208 us -> 1.24 us
  between operations: 14.8 us -> 0.72 us
  other arithmetic: 12.8 us -> 0 us
  matrix products: 11.5 us -> 0 us
  Pallas kernels: 0 us -> 6.52 us
  local copies, waits for them, and re-layouts: 3.54 us -> 0.03 us
    unnamed x3 -> x0, waiting for transfers between devices: 146 us -> none
    psum x1 -> x0, waiting for transfers between devices: 62 us -> none  [on_device(): summed = lax.psum(partial_sums, 'slab')]
    all_to_all x0 -> x3, blocking collectives: none -> 53.9 us  [the longest x1 24.5 us: on_device(): slab_values = lax.all_to_all(offer, 'angle', 0, 0)]
    all_gather x1 -> x0, blocking collectives: 51.3 us -> none  [on_device(): slab_values = lax.all_gather(coarse, 'angle', axis=0, tiled=True)]
    dot_general x3 -> x0, matrix products: 11.5 us -> none  [the longest x1 6.11 us: on_device(): jnp.einsum('bpv,bkv->bkp', footprint, stacked, preferred_element_type=jnp...]
    scatter-add x1 -> x0, other arithmetic: 7.17 us -> none  [on_device(): jnp.zeros((slab_blocks, 2, width), jnp.float32).at[block_voxel]]
    pallas_call x0 -> x5, Pallas kernels: none -> 6.52 us  [the longest x4 5.37 us: call(): pl.pallas_call(kernel, out_shape=out, in_specs=specs, out_specs=[VMEM] *...]
    convert_element_type x4 -> x0, other arithmetic: 3.16 us -> none  [the longest x1 1.4 us: on_device(): coarse_res = weighted.astype(jnp.bfloat16)]
  transfers between devices with their start and end apart: 2 -> 1, of which waited for: 2 -> 1; matrix products, arithmetic and copies ran while one was open for 0% -> 0% of each run, Pallas kernels for 0% -> 0%
where the time goes in v2:
time: 62.7 us; the launch traced here: 62.5 us
  blocking collectives  53.9 us (86%)
  Pallas kernels  6.52 us (10%)
  waiting for transfers between devices  1.24 us (2%)
  between operations  0.72 us (1%)
    all_to_all x1, blocking collectives, on_device(): slab_values = lax.all_to_all(offer, 'angle', 0, 0)  24.5 us
    all_to_all x1, blocking collectives, on_device(): received = lax.all_to_all(send_back, 'angle', 0, 0)  18.1 us
    all_to_all x1, blocking collectives, on_device(): parts = lax.all_to_all(spread, 'slab', 0, 0, axis_index_groups=same_core)  11.3 us
    pallas_call x4, Pallas kernels, call(): pl.pallas_call(kernel, out_shape=out, in_specs=specs, out_specs=[VMEM] *...  5.37 us
  transfers between devices with their start and end apart: 1, of which 1 were waited for; matrix products, arithmetic and copies ran while one was open for 0% of the time, Pallas kernels for 0%

profile of v2, /device:TPU:32, one launch (start us, length us, event | category | flops | bytes accessed | tf_op | source)
XLA Modules:
  0.0 62.5 jit_solution(5420560854189690358)
XLA Ops:
  0.6 0.0 copy-start.3
  0.6 0.0 copy-start
  0.7 0.0 copy-start.5
  0.7 0.0 copy-start.4
  0.7 0.0 copy-start.2
  0.7 1.1 %offer.1 = bf16[32,40,128]{2,1,0:T(8,128)(2,1)S(1)} custom-call(s32[192]{0:T(256)} %voxel_ref.3, f32[32,128]{1,0:T(8,128)} %volume_ref.1, bf16[192,128,128]{2,1,0:T(8,128)(2,1)} %foot_ref.3), custom_call_target="tpu_custom_call" | custom-call | tf_op jit(solution)/shard_map/offer/pallas_call | solution.py:135
  1.8 24.5 %all_to_all.15.slab_ref = bf16[32,40,128]{2,1,0:T(8,128)(2,1)S(1)} all-to-all(bf16[32,40,128]{2,1,0:T(8,128)(2,1)S(1)} %offer.1), channel_id=1, replica_groups=mesh['slab'=8,'angle'=32] {'angle'}, dimensions={0} | all-to-all | bytes 655360 | tf_op jit(solution)/shard_map/all_to_all | solution.py:144
  26.4 0.0 copy-done.3
  26.4 0.0 copy-done
  26.4 0.0 copy-done.5
  26.4 0.0 copy-done.4
  26.4 0.0 copy-start.1
  26.4 2.6 %forward.1 = (f32[64,256]{1,0:T(8,128)S(1)}, f32[8,128]{1,0:T(8,128)S(1)}) custom-call(bf16[32,40,128]{2,1,0:T(8,128)(2,1)S(1)} %all_to_all.15.slab_ref, s32[192]{0:T(256)S(1)} %copy-done.3, s32[192]{0:T(256)S(1)} %copy-done.4, s32[192]{0:T(256)S(1)} %copy-done.5, bf16[192,128,128]{2,1,0:T(8,128)(2,1)S(1)} %copy-done), custom_call_target="tpu_custom_call" | custom-call | tf_op jit(solution)/shard_map/forward/pallas_call | solution.py:129
  29.0 0.1 collective-permute-start
  29.1 1.2 %collective-permute-done.other_ref = f32[64,256]{1,0:T(8,128)S(1)} collective-permute-done((f32[64,256]{1,0:T(8,128)S(1)}, f32[64,256]{1,0:T(8,128)S(1)}, u32[]{:S(2)}, u32[]{:S(2)}) %collective-permute-start) | collective-permute-done | bytes 65568 | tf_op jit(solution)/shard_map/ppermute | solution.py:153
  30.4 11.3 %all_to_all.16.parts_ref = f32[4,64,256]{2,1,0:T(8,128)S(1)} all-to-all(f32[4,64,256]{2,1,0:T(8,128)S(1)} %spread.1), channel_id=1, replica_groups={{0,64,128,192},{32,96,160,224},{1,65,129,193},{33,97,161,225},{2,66,130..., dimensions={0} | all-to-all | bytes 524288 | tf_op jit(solution)/shard_map/all_to_all | solution.py:156
  41.7 0.0 copy-done.2
  41.7 1.8 %backward.1 = (f32[64,128]{1,0:T(8,128)}, f32[32,24,128]{2,1,0:T(8,128)S(1)}) custom-call(s32[192]{0:T(256)S(1)} %copy-done.3, f32[4,64,256]{2,1,0:T(8,128)S(1)} %all_to_all.16.parts_ref, f32[64,128]{1,0:T(8,128)S(1)} %copy-done.2, s32[192]{0:T(256)S(1)} %copy-done.4, s32[192]{0:T(256)S(1)} %copy-done.5, bf16[192,128,128]{2,1,0:T(8,128)(2,1)S(1)} %copy-done), custom_call_target="tpu_custom_call" | custom-call | tf_op jit(solution)/shard_map/backward/pallas_call | solution.py:129
  43.5 18.1 %all_to_all.17.recv_ref = f32[32,24,128]{2,1,0:T(8,128)S(1)} all-to-all(f32[32,24,128]{2,1,0:T(8,128)S(1)} %get-tuple-element.7), channel_id=1, replica_groups=mesh['slab'=8,'angle'=32] {'angle'}, dimensions={0} | all-to-all | bytes 786432 | tf_op jit(solution)/shard_map/all_to_all | solution.py:165
  61.7 0.0 copy-done.1
  61.7 0.9 %update.1 = f32[32,128]{1,0:T(8,128)} custom-call(f32[32,24,128]{2,1,0:T(8,128)S(1)} %all_to_all.17.recv_ref, f32[8,128]{1,0:T(8,128)S(1)} %get-tuple-element.8.places_ref, f32[32,128]{1,0:T(8,128)S(1)} %copy-done.1), custom_call_target="tpu_custom_call" | custom-call | tf_op jit(solution)/shard_map/update/pallas_call | solution.py:129
  (1 shorter events, 0.0 us)
Async XLA Ops:
  0.6 25.8 %copy-start.3 = (s32[192]{0:T(256)S(1)}, s32[192]{0:T(256)}, u32[]{:S(2)}) copy-start(s32[192]{0:T(256)} %voxel_ref.3) | copy-start | bytes 2308
  0.6 25.7 %copy-start = (bf16[192,128,128]{2,1,0:T(8,128)(2,1)S(1)}, bf16[192,128,128]{2,1,0:T(8,128)(2,1)}, u32[]{:S(2)}) copy-start(bf16[192,128,128]{2,1,0:T(8,128)(2,1)} %foot_ref.3) | copy-start | bytes 18874372
  0.7 25.7 %copy-start.5 = (s32[192]{0:T(256)S(1)}, s32[192]{0:T(256)}, u32[]{:S(2)}) copy-start(s32[192]{0:T(256)} %rows_ref.3) | copy-start | bytes 2308
  0.7 25.7 %copy-start.4 = (s32[192]{0:T(256)S(1)}, s32[192]{0:T(256)}, u32[]{:S(2)}) copy-start(s32[192]{0:T(256)} %tile_ref.3) | copy-start | bytes 2308
  0.7 41.0 %copy-start.2 = (f32[64,128]{1,0:T(8,128)S(1)}, f32[64,128]{1,0:T(8,128)}, u32[]{:S(2)}) copy-start(f32[64,128]{1,0:T(8,128)} %measured_ref.1) | copy-start | bytes 98308
  26.4 35.3 %copy-start.1 = (f32[32,128]{1,0:T(8,128)S(1)}, f32[32,128]{1,0:T(8,128)}, u32[]{:S(2)}) copy-start(f32[32,128]{1,0:T(8,128)} %volume_ref.1) | copy-start | bytes 49156
  29.0 1.3 %collective-permute-start = (f32[64,256]{1,0:T(8,128)S(1)}, f32[64,256]{1,0:T(8,128)S(1)}, u32[]{:S(2)}, u32[]{:S(2)}) collective-permute-start(f32[64,256]{1,0:T(8,128)S(1)} %get-tuple-element.6.mine_ref), channel_id=1, source_target_pairs={{0,32},{32,0},{64,96},{96,64},{128,160},{160,128},{192,224},{224,1... | collective-permute-start | bytes 196616 | tf_op jit(solution)/shard_map/ppermute | solution.py:153

commit v3 on v2

v3 whole, which is shorter than its diff:
```python
import jax
import jax.numpy as jnp
from jax import lax
from jax.experimental import pallas as pl
from jax.experimental.pallas import tpu as pltpu
from jax.sharding import PartitionSpec as P

BLK = 128
NB = 192
CAP = 12
SHARES = 32
HALF = NB // 2
F32 = jnp.float32
BF16 = jnp.bfloat16
VMEM = pl.BlockSpec(memory_space=pltpu.VMEM)
SMEM = pl.BlockSpec(memory_space=pltpu.SMEM)
HBM = pl.BlockSpec(memory_space=pltpu.HBM)
PARAMS = pltpu.CompilerParams(vmem_limit_bytes=40 * 1024 * 1024)
ROWS = ((1,), (0,))
LANES = ((1,), (1,))
SUBLANES = ((0,), (0,))


def dot(a, b, contract=ROWS):
    return lax.dot_general(a, b, (contract, ((), ())), preferred_element_type=F32)


def iota(shape, dim):
    return lax.broadcasted_iota(jnp.int32, shape, dim)


def exact_dot(onehot, x, contract=ROWS):
    hi = x.astype(BF16)
    rest = x - hi.astype(F32)
    mid = rest.astype(BF16)
    lo = (rest - mid.astype(F32)).astype(BF16)
    return dot(onehot, hi, contract) + (dot(onehot, mid, contract) + dot(onehot, lo, contract))


def hot_columns(ref, n):
    return jnp.where(iota((n, NB), 0) == ref[...].reshape(1, NB), 1.0, 0.0).astype(BF16)


def live_rows(rows_ref):
    return jnp.where(iota((BLK, NB), 0) < rows_ref[...].reshape(1, NB), 1.0, 0.0).T


def offer_kernel(voxel_any, volume_any, foot_any, send_ref, voxel_ref, volume_ref, sems):
    copies = [
        pltpu.make_async_copy(volume_any, volume_ref, sems.at[0]),
        pltpu.make_async_copy(voxel_any, voxel_ref, sems.at[1]),
    ]
    for copy in copies:
        copy.start()
    copies[0].wait()
    coarse = volume_ref[...].astype(BF16)
    for d in range(SHARES):
        send_ref[d, 0:32, :] = coarse
        send_ref[d, 32:40, :] = jnp.zeros((8, BLK), BF16)
    copies[1].wait()
    spot = iota((8, BLK), 0) * BLK + iota((8, BLK), 1) - 2 * CAP * lax.axis_index("angle")
    for j in range(NB // CAP):
        places = jnp.zeros((8, BLK), jnp.int32)
        for i in range(CAP):
            places = jnp.where(spot == i, (voxel_ref[CAP * j + i] & 31) + 1, places)
        send_ref[voxel_ref[CAP * j] >> 5, 32:40, :] = places.astype(F32).astype(BF16)


def forward_kernel(slab_ref, voxel_ref, tile_ref, rows_ref, foot_ref, part_ref, places_ref):
    picked = dot(slab_ref[:, 0:32, :].reshape(1024, BLK), hot_columns(voxel_ref, 1024), SUBLANES)
    even = iota((1, BLK), 1) % 2 == 0
    one = jnp.ones((BLK, BLK), F32)
    ones = jnp.concatenate([jnp.where(even, one, 0.0), jnp.where(even, 0.0, one)], axis=0)
    sums = []
    for h in range(2):
        mine = jnp.concatenate([picked[:, HALF * h : HALF * (h + 1)], jnp.zeros((BLK, BLK - HALF), F32)], axis=1)
        cols = jnp.concatenate([jnp.where(even, mine, 0.0), jnp.where(even, 0.0, mine)], axis=0)
        cols = jnp.concatenate([cols, ones], axis=1).astype(BF16)
        total = jnp.zeros((BLK, 2 * BLK), F32)
        for q in range(HALF // 2):
            k = HALF * h + 2 * q
            pair = jnp.concatenate([foot_ref[k], foot_ref[k + 1]], axis=1)
            both = iota((1, 2 * BLK), 1) % BLK // 2 == q
            total = jnp.where(both, dot(pair, cols), total)
        sums.append(total)
    live = iota((BLK, NB), 0) < rows_ref[...].reshape(1, NB)
    tile_hot = hot_columns(tile_ref, 64)
    for n in range(2):
        both = jnp.concatenate([x[:, BLK * n : BLK * n + HALF] for x in sums], axis=1)
        part_ref[:, BLK * n : BLK * (n + 1)] = exact_dot(tile_hot, jnp.where(live, both, 0.0), LANES)
    back = jnp.sum(slab_ref[:, 32:40, :].astype(F32), axis=0)
    later = jnp.concatenate([back[:, BLK - CAP :], back[:, : BLK - CAP]], axis=1)
    above = jnp.concatenate([later[7:8], later[:7]], axis=0)
    later = jnp.where(iota((8, BLK), 1) < CAP, above, later)
    places_ref[...] = back + jnp.where(later > 0.0, later + 32.0, 0.0)


def backward_kernel(voxel_ref, mine_ref, across_ref, left_ref, right_ref, measured_ref, tile_ref, rows_ref, foot_ref, weighted_ref, send_ref):
    total = (mine_ref[...] + across_ref[...]) + (left_ref[...] + right_ref[...])
    weighted = (measured_ref[...] - total[:, :BLK]) / jnp.maximum(total[:, BLK:], 1.0)
    weighted_ref[...] = weighted
    live = live_rows(rows_ref)
    residual = dot(hot_columns(tile_ref, 64), weighted.astype(BF16), SUBLANES) * live
    send_ref[...] = jnp.zeros_like(send_ref)
    row = iota((2 * CAP, BLK), 0) % CAP
    for j in range(NB // CAP):
        at = slice(CAP * j, CAP * (j + 1))
        both = jnp.concatenate([residual[at], live[at]], axis=0)
        diag = jnp.concatenate([jnp.where(row == i, both, 0.0) for i in range(CAP)], axis=1).astype(BF16)
        send_ref[voxel_ref[CAP * j] >> 5] = dot(diag, foot_ref[at].reshape(CAP * BLK, BLK))


def update_kernel(recv_ref, places_ref, volume_ref, weighted_ref, out_ref, weighted_out_ref):
    weighted_out_ref[...] = weighted_ref[...]
    wanted = (iota((2 * 32, BLK), 0) + 1).astype(F32)
    hot = jnp.concatenate(
        [jnp.where(places_ref[m : m + 1, :] == wanted, 1.0, 0.0) for m in range(SHARES * 2 * CAP // BLK)], axis=1
    ).astype(BF16)
    summed = exact_dot(hot, recv_ref[...].reshape(SHARES * 2 * CAP, BLK))
    out_ref[...] = volume_ref[...] + summed[:32] / jnp.maximum(summed[32:], 1.0)


def call(kernel, name, out, specs, *args, scratch=()):
    out = [jax.ShapeDtypeStruct(*o) for o in out]
    return pl.pallas_call(
        kernel,
        out_shape=out,
        in_specs=specs,
        out_specs=[VMEM] * len(out),
        scratch_shapes=scratch,
        compiler_params=PARAMS,
        name=name,
    )(*args)


def on_device(volume, measured, footprint, block_voxel, block_tile, block_rows):
    (offer,) = call(
        offer_kernel,
        "offer",
        [((SHARES, 40, BLK), BF16)],
        [HBM] * 3,
        *(pltpu.with_memory_space_constraint(x, pltpu.HBM) for x in (block_voxel, volume, footprint)),
        scratch=[pltpu.SMEM((NB,), jnp.int32), pltpu.VMEM((32, BLK), F32), pltpu.SemaphoreType.DMA((2,))],
    )
    slab_values = lax.all_to_all(offer, "angle", 0, 0)
    part, places = call(
        forward_kernel,
        "forward",
        [((64, 2 * BLK), F32), ((8, BLK), F32)],
        [VMEM] * 5,
        slab_values, block_voxel, block_tile, block_rows, footprint,
    )
    part = part + lax.ppermute(part, "slab", [(i, i ^ 1) for i in range(8)])
    across, left, right = (
        lax.ppermute(part, "slab", [(i, (i + 2 * k) % 8) for i in range(8)]) for k in (2, 1, 3)
    )

    weighted, send_back = call(
        backward_kernel,
        "backward",
        [((64, BLK), F32), ((SHARES, 2 * CAP, BLK), F32)],
        [SMEM] + [VMEM] * 8,
        block_voxel, part, across, left, right, measured, block_tile, block_rows, footprint,
    )
    received = lax.all_to_all(send_back, "angle", 0, 0)
    return call(
        update_kernel,
        "update",
        [((32, BLK), F32), ((64, BLK), F32)],
        [VMEM] * 4,
        received, places, volume, weighted,
    )


def solution(mesh):
    in_specs = (
        P(("slab", "angle"), None),
        P("angle", None),
        P(("slab", "angle"), None, None),
        P(("slab", "angle")),
        P(("slab", "angle")),
        P(("slab", "angle")),
    )
    out_specs = (P(("slab", "angle"), None), P("angle", None))
    return jax.shard_map(
        on_device, mesh=mesh, in_specs=in_specs, out_specs=out_specs, check_vma=False
    )
```

time: 62.7 us -> 60.9 us (0.971)
  blocking collectives: 53.9 us -> 42.8 us
  starting transfers between devices: 0.09 us -> 5.4 us
  waiting for transfers between devices: 1.24 us -> 5.53 us
    all_to_all x1 -> x0, blocking collectives: 11.3 us -> none  [on_device(): parts = lax.all_to_all(spread, 'slab', 0, 0, axis_index_groups=same_core)]
    ppermute x1 -> x4, starting transfers between devices: 0.09 us -> 5.4 us  [the longest x3 5.3 us: on_device(): lax.ppermute(part, 'slab', [(i, (i + 2 * k) % 8) for i in range(8)])]
    ppermute x1 -> x4, waiting for transfers between devices: 1.24 us -> 5.53 us  [the longest x3 4.29 us: on_device(): lax.ppermute(part, 'slab', [(i, (i + 2 * k) % 8) for i in range(8)])]
    pallas_call x1 -> x0, Pallas kernels: 1.15 us -> none  [on_device(): pl.pallas_call(offer_kernel, out_shape=[jax.ShapeDtypeStruct((SHARES, 40,...]
    pallas_call x4, Pallas kernels: 5.37 us -> 6.29 us  [call(): pl.pallas_call(kernel, out_shape=out, in_specs=specs, out_specs=[VMEM] *...]
  transfers between devices with their start and end apart: 1 -> 4, of which waited for: 1 -> 2; matrix products, arithmetic and copies ran while one was open for 0% -> 0% of each run, Pallas kernels for 0% -> 0%
where the time goes in v3:
time: 60.9 us; the launch traced here: 60.8 us
  blocking collectives  42.8 us (70%)
  Pallas kernels  6.29 us (10%)
  waiting for transfers between devices  5.53 us (9%)
  starting transfers between devices  5.4 us (9%)
  between operations  0.73 us (1%)
    all_to_all x1, blocking collectives, on_device(): slab_values = lax.all_to_all(offer, 'angle', 0, 0)  24.5 us
    all_to_all x1, blocking collectives, on_device(): received = lax.all_to_all(send_back, 'angle', 0, 0)  18.3 us
    pallas_call x4, Pallas kernels, call(): pl.pallas_call(kernel, out_shape=out, in_specs=specs, out_specs=[VMEM] *...  6.29 us
    ppermute x3, starting transfers between devices, on_device(): lax.ppermute(part, 'slab', [(i, (i + 2 * k) % 8) for i in range(8)])  5.3 us
    ppermute x3, waiting for transfers between devices, on_device(): lax.ppermute(part, 'slab', [(i, (i + 2 * k) % 8) for i in range(8)])  4.29 us
    ppermute x1, waiting for transfers between devices, on_device(): part = part + lax.ppermute(part, 'slab', [(i, i ^ 1) for i in range(8)])  1.24 us
  transfers between devices with their start and end apart: 4, of which 2 were waited for; matrix products, arithmetic and copies ran while one was open for 0% of the time, Pallas kernels for 0%

profile of v3, /device:TPU:32, one launch (start us, length us, event | category | flops | bytes accessed | tf_op | source)
XLA Modules:
  0.0 60.8 jit_solution(5346272106041845529)
XLA Ops:
  0.6 0.0 copy-start.3
  0.6 0.0 copy-start
  0.7 0.0 copy-start.5
  0.7 0.0 copy-start.4
  0.7 0.0 copy-start.2
  0.7 1.1 %offer.1 = bf16[32,40,128]{2,1,0:T(8,128)(2,1)S(1)} custom-call(s32[192]{0:T(256)} %voxel_ref.3, f32[32,128]{1,0:T(8,128)} %volume_ref.1, bf16[192,128,128]{2,1,0:T(8,128)(2,1)} %foot_ref.3), custom_call_target="tpu_custom_call" | custom-call | tf_op jit(solution)/shard_map/offer/pallas_call | solution.py:125
  1.8 24.5 %all_to_all.10.slab_ref = bf16[32,40,128]{2,1,0:T(8,128)(2,1)S(1)} all-to-all(bf16[32,40,128]{2,1,0:T(8,128)(2,1)S(1)} %offer.1), channel_id=1, replica_groups=mesh['slab'=8,'angle'=32] {'angle'}, dimensions={0} | all-to-all | bytes 655360 | tf_op jit(solution)/shard_map/all_to_all | solution.py:145
  26.3 0.0 copy-done.3
  26.3 0.0 copy-done
  26.3 0.0 copy-done.5
  26.3 0.0 copy-done.4
  26.3 0.0 copy-start.1
  26.4 2.6 %forward.1 = (f32[64,256]{1,0:T(8,128)S(1)}, f32[8,128]{1,0:T(8,128)S(1)}) custom-call(bf16[32,40,128]{2,1,0:T(8,128)(2,1)S(1)} %all_to_all.10.slab_ref, s32[192]{0:T(256)S(1)} %copy-done.3, s32[192]{0:T(256)S(1)} %copy-done.4, s32[192]{0:T(256)S(1)} %copy-done.5, bf16[192,128,128]{2,1,0:T(8,128)(2,1)S(1)} %copy-done), custom_call_target="tpu_custom_call" | custom-call | tf_op jit(solution)/shard_map/forward/pallas_call | solution.py:125
  29.0 0.1 collective-permute-start
  29.1 1.2 %collective-permute-done = f32[64,256]{1,0:T(8,128)S(1)} collective-permute-done((f32[64,256]{1,0:T(8,128)S(1)}, f32[64,256]{1,0:T(8,128)S(1)}, u32[]{:S(2)}, u32[]{:S(2)}) %collective-permute-start) | collective-permute-done | bytes 65568 | tf_op jit(solution)/shard_map/ppermute | solution.py:153
  30.3 3.1 %collective-permute-start.3 = (f32[64,256]{1,0:T(8,128)S(1)}, f32[64,256]{1,0:T(8,128)S(1)}, u32[]{:S(2)}, u32[]{:S(2)}) collective-permute-start(f32[64,256]{1,0:T(8,128)S(1)} %add.3.mine_ref), channel_id=1, source_target_pairs={{0,192},{32,224},{64,0},{96,32},{128,64},{160,96},{192,128},{224,1... | collective-permute-start | bytes 196616 | tf_op jit(solution)/shard_map/ppermute | solution.py:155
  33.4 0.0 collective-permute-start.2
  33.4 2.2 %collective-permute-start.1 = (f32[64,256]{1,0:T(8,128)S(1)}, f32[64,256]{1,0:T(8,128)S(1)}, u32[]{:S(2)}, u32[]{:S(2)}) collective-permute-start(f32[64,256]{1,0:T(8,128)S(1)} %add.3.mine_ref), channel_id=1, source_target_pairs={{0,128},{32,160},{64,192},{96,224},{128,0},{160,32},{192,64},{224,... | collective-permute-start | bytes 196616 | tf_op jit(solution)/shard_map/ppermute | solution.py:155
  35.6 0.0 collective-permute-done.3.right_ref
  35.7 4.3 %collective-permute-done.2.left_ref = f32[64,256]{1,0:T(8,128)S(1)} collective-permute-done((f32[64,256]{1,0:T(8,128)S(1)}, f32[64,256]{1,0:T(8,128)S(1)}, u32[]{:S(2)}, u32[]{:S(2)}) %collective-permute-start.2) | collective-permute-done | bytes 65568 | tf_op jit(solution)/shard_map/ppermute | solution.py:155
  39.9 0.0 collective-permute-done.1.across_ref
  39.9 0.0 copy-done.2
  39.9 1.7 %backward.1 = (f32[64,128]{1,0:T(8,128)S(1)}, f32[32,24,128]{2,1,0:T(8,128)S(1)}) custom-call(s32[192]{0:T(256)S(1)} %copy-done.3, f32[64,256]{1,0:T(8,128)S(1)} %add.3.mine_ref, f32[64,256]{1,0:T(8,128)S(1)} %collective-permute-done.1.across_ref, f32[64,256]{1,0:T(8,128)S(1)} %collective-permute-done.2.left_ref, ...), custom_call_target="tpu_custom_call" | custom-call | tf_op jit(solution)/shard_map/backward/pallas_call | solution.py:125
  41.6 18.3 %all_to_all.11.recv_ref = f32[32,24,128]{2,1,0:T(8,128)S(1)} all-to-all(f32[32,24,128]{2,1,0:T(8,128)S(1)} %get-tuple-element.7), channel_id=1, replica_groups=mesh['slab'=8,'angle'=32] {'angle'}, dimensions={0} | all-to-all | bytes 786432 | tf_op jit(solution)/shard_map/all_to_all | solution.py:165
  59.9 0.0 copy-done.1
  59.9 0.9 %update.1 = (f32[32,128]{1,0:T(8,128)}, f32[64,128]{1,0:T(8,128)}) custom-call(f32[32,24,128]{2,1,0:T(8,128)S(1)} %all_to_all.11.recv_ref, f32[8,128]{1,0:T(8,128)S(1)} %get-tuple-element.8.places_ref, f32[32,128]{1,0:T(8,128)S(1)} %copy-done.1, f32[64,128]{1,0:T(8,128)S(1)} %get-tuple-element.9.weighted_ref), custom_call_target="tpu_custom_call" | custom-call | tf_op jit(solution)/shard_map/update/pallas_call | solution.py:125
  (1 shorter events, 0.0 us)
Async XLA Ops:
  0.6 25.7 %copy-start.3 = (s32[192]{0:T(256)S(1)}, s32[192]{0:T(256)}, u32[]{:S(2)}) copy-start(s32[192]{0:T(256)} %voxel_ref.3) | copy-start | bytes 2308
  0.6 25.7 %copy-start = (bf16[192,128,128]{2,1,0:T(8,128)(2,1)S(1)}, bf16[192,128,128]{2,1,0:T(8,128)(2,1)}, u32[]{:S(2)}) copy-start(bf16[192,128,128]{2,1,0:T(8,128)(2,1)} %foot_ref.3) | copy-start | bytes 18874372
  0.7 25.7 %copy-start.5 = (s32[192]{0:T(256)S(1)}, s32[192]{0:T(256)}, u32[]{:S(2)}) copy-start(s32[192]{0:T(256)} %rows_ref.3) | copy-start | bytes 2308
  0.7 25.7 %copy-start.4 = (s32[192]{0:T(256)S(1)}, s32[192]{0:T(256)}, u32[]{:S(2)}) copy-start(s32[192]{0:T(256)} %tile_ref.3) | copy-start | bytes 2308
  0.7 39.3 %copy-start.2 = (f32[64,128]{1,0:T(8,128)S(1)}, f32[64,128]{1,0:T(8,128)}, u32[]{:S(2)}) copy-start(f32[64,128]{1,0:T(8,128)} %measured_ref.1) | copy-start | bytes 98308
  26.3 33.5 %copy-start.1 = (f32[32,128]{1,0:T(8,128)S(1)}, f32[32,128]{1,0:T(8,128)}, u32[]{:S(2)}) copy-start(f32[32,128]{1,0:T(8,128)} %volume_ref.1) | copy-start | bytes 49156
  29.0 1.3 %collective-permute-start = (f32[64,256]{1,0:T(8,128)S(1)}, f32[64,256]{1,0:T(8,128)S(1)}, u32[]{:S(2)}, u32[]{:S(2)}) collective-permute-start(f32[64,256]{1,0:T(8,128)S(1)} %get-tuple-element.6), channel_id=1, source_target_pairs={{0,32},{32,0},{64,96},{96,64},{128,160},{160,128},{192,224},{224,1... | collective-permute-start | bytes 196616 | tf_op jit(solution)/shard_map/ppermute | solution.py:153
  30.3 5.3 %collective-permute-start.3 = (f32[64,256]{1,0:T(8,128)S(1)}, f32[64,256]{1,0:T(8,128)S(1)}, u32[]{:S(2)}, u32[]{:S(2)}) collective-permute-start(f32[64,256]{1,0:T(8,128)S(1)} %add.3.mine_ref), channel_id=1, source_target_pairs={{0,192},{32,224},{64,0},{96,32},{128,64},{160,96},{192,128},{224,1... | collective-permute-start | bytes 196616 | tf_op jit(solution)/shard_map/ppermute | solution.py:155
  33.4 6.5 %collective-permute-start.2 = (f32[64,256]{1,0:T(8,128)S(1)}, f32[64,256]{1,0:T(8,128)S(1)}, u32[]{:S(2)}, u32[]{:S(2)}) collective-permute-start(f32[64,256]{1,0:T(8,128)S(1)} %add.3.mine_ref), channel_id=1, source_target_pairs={{0,64},{32,96},{64,128},{96,160},{128,192},{160,224},{192,0},{224,... | collective-permute-start | bytes 196616 | tf_op jit(solution)/shard_map/ppermute | solution.py:155
  33.4 6.5 %collective-permute-start.1 = (f32[64,256]{1,0:T(8,128)S(1)}, f32[64,256]{1,0:T(8,128)S(1)}, u32[]{:S(2)}, u32[]{:S(2)}) collective-permute-start(f32[64,256]{1,0:T(8,128)S(1)} %add.3.mine_ref), channel_id=1, source_target_pairs={{0,128},{32,160},{64,192},{96,224},{128,0},{160,32},{192,64},{224,... | collective-permute-start | bytes 196616 | tf_op jit(solution)/shard_map/ppermute | solution.py:155

commit v4 on v3

--- a/solution.py
+++ b/solution.py
@@ -9,7 +9,7 @@
 NB = 192
 CAP = 12
 SHARES = 32
-HALF = NB // 2
+SET = 64
 F32 = jnp.float32
 BF16 = jnp.bfloat16
 VMEM = pl.BlockSpec(memory_space=pltpu.VMEM)
@@ -45,6 +45,10 @@
     return jnp.where(iota((BLK, NB), 0) < rows_ref[...].reshape(1, NB), 1.0, 0.0).T
 
 
+def twice(x):
+    return jnp.concatenate([x[:, g : g + SET] for g in range(0, NB, SET) for _ in range(2)], axis=1)
+
+
 def offer_kernel(voxel_any, volume_any, foot_any, send_ref, voxel_ref, volume_ref, sems):
     copies = [
         pltpu.make_async_copy(volume_any, volume_ref, sems.at[0]),
@@ -69,25 +73,20 @@
 def forward_kernel(slab_ref, voxel_ref, tile_ref, rows_ref, foot_ref, part_ref, places_ref):
     picked = dot(slab_ref[:, 0:32, :].reshape(1024, BLK), hot_columns(voxel_ref, 1024), SUBLANES)
     even = iota((1, BLK), 1) % 2 == 0
-    one = jnp.ones((BLK, BLK), F32)
-    ones = jnp.concatenate([jnp.where(even, one, 0.0), jnp.where(even, 0.0, one)], axis=0)
     sums = []
-    for h in range(2):
-        mine = jnp.concatenate([picked[:, HALF * h : HALF * (h + 1)], jnp.zeros((BLK, BLK - HALF), F32)], axis=1)
-        cols = jnp.concatenate([jnp.where(even, mine, 0.0), jnp.where(even, 0.0, mine)], axis=0)
-        cols = jnp.concatenate([cols, ones], axis=1).astype(BF16)
-        total = jnp.zeros((BLK, 2 * BLK), F32)
-        for q in range(HALF // 2):
-            k = HALF * h + 2 * q
-            pair = jnp.concatenate([foot_ref[k], foot_ref[k + 1]], axis=1)
-            both = iota((1, 2 * BLK), 1) % BLK // 2 == q
-            total = jnp.where(both, dot(pair, cols), total)
+    for g in range(0, NB, SET):
+        mine = jnp.concatenate([picked[:, g : g + SET], jnp.ones((BLK, SET), F32)], axis=1)
+        cols = jnp.concatenate([jnp.where(even, mine, 0.0), jnp.where(even, 0.0, mine)], axis=0).astype(BF16)
+        total = jnp.zeros((BLK, BLK), F32)
+        for q in range(SET // 2):
+            pair = jnp.concatenate([foot_ref[g + 2 * q], foot_ref[g + 2 * q + 1]], axis=1)
+            total = jnp.where(iota((1, BLK), 1) % SET // 2 == q, dot(pair, cols), total)
         sums.append(total)
-    live = iota((BLK, NB), 0) < rows_ref[...].reshape(1, NB)
-    tile_hot = hot_columns(tile_ref, 64)
-    for n in range(2):
-        both = jnp.concatenate([x[:, BLK * n : BLK * n + HALF] for x in sums], axis=1)
-        part_ref[:, BLK * n : BLK * (n + 1)] = exact_dot(tile_hot, jnp.where(live, both, 0.0), LANES)
+    live = iota((BLK, 2 * NB), 0) < twice(rows_ref[...].reshape(1, NB))
+    tile = twice(tile_ref[...].reshape(1, NB))
+    wanted = tile + jnp.where(iota((1, 2 * NB), 1) % BLK < SET, 0, 64)
+    tile_hot = jnp.where(iota((BLK, 2 * NB), 0) == wanted, 1.0, 0.0).astype(BF16)
+    part_ref[...] = exact_dot(tile_hot, jnp.where(live, jnp.concatenate(sums, axis=1), 0.0), LANES)
     back = jnp.sum(slab_ref[:, 32:40, :].astype(F32), axis=0)
     later = jnp.concatenate([back[:, BLK - CAP :], back[:, : BLK - CAP]], axis=1)
     above = jnp.concatenate([later[7:8], later[:7]], axis=0)
@@ -97,7 +96,7 @@
 
 def backward_kernel(voxel_ref, mine_ref, across_ref, left_ref, right_ref, measured_ref, tile_ref, rows_ref, foot_ref, weighted_ref, send_ref):
     total = (mine_ref[...] + across_ref[...]) + (left_ref[...] + right_ref[...])
-    weighted = (measured_ref[...] - total[:, :BLK]) / jnp.maximum(total[:, BLK:], 1.0)
+    weighted = (measured_ref[...] - total[:64]) / jnp.maximum(total[64:], 1.0)
     weighted_ref[...] = weighted
     live = live_rows(rows_ref)
     residual = dot(hot_columns(tile_ref, 64), weighted.astype(BF16), SUBLANES) * live
@@ -146,7 +145,7 @@
     part, places = call(
         forward_kernel,
         "forward",
-        [((64, 2 * BLK), F32), ((8, BLK), F32)],
+        [((2 * 64, BLK), F32), ((8, BLK), F32)],
         [VMEM] * 5,
         slab_values, block_voxel, block_tile, block_rows, footprint,
     )

time: 60.9 us -> 60.7 us (level)
  no operation moved by 1% of the time
where the time goes in v4:
time: 60.7 us; the launch traced here: 60.5 us
  blocking collectives  42.8 us (71%)
  Pallas kernels  6.04 us (10%)
  waiting for transfers between devices  5.53 us (9%)
  starting transfers between devices  5.39 us (9%)
  between operations  0.73 us (1%)
    all_to_all x1, blocking collectives, on_device(): slab_values = lax.all_to_all(offer, 'angle', 0, 0)  24.5 us
    all_to_all x1, blocking collectives, on_device(): received = lax.all_to_all(send_back, 'angle', 0, 0)  18.3 us
    pallas_call x4, Pallas kernels, call(): pl.pallas_call(kernel, out_shape=out, in_specs=specs, out_specs=[VMEM] *...  6.04 us
    ppermute x3, starting transfers between devices, on_device(): lax.ppermute(part, 'slab', [(i, (i + 2 * k) % 8) for i in range(8)])  5.29 us
    ppermute x3, waiting for transfers between devices, on_device(): lax.ppermute(part, 'slab', [(i, (i + 2 * k) % 8) for i in range(8)])  4.29 us
    ppermute x1, waiting for transfers between devices, on_device(): part = part + lax.ppermute(part, 'slab', [(i, i ^ 1) for i in range(8)])  1.24 us
  transfers between devices with their start and end apart: 4, of which 2 were waited for; matrix products, arithmetic and copies ran while one was open for 0% of the time, Pallas kernels for 0%

profile of v4, /device:TPU:32, one launch (start us, length us, event | category | flops | bytes accessed | tf_op | source)
XLA Modules:
  0.0 60.5 jit_solution(6680301678315961921)
XLA Ops:
  0.6 0.0 copy-start.3
  0.6 0.0 copy-start
  0.7 0.0 copy-start.5
  0.7 0.0 copy-start.4
  0.7 0.0 copy-start.2
  0.7 1.1 %offer.1 = bf16[32,40,128]{2,1,0:T(8,128)(2,1)S(1)} custom-call(s32[192]{0:T(256)} %voxel_ref.3, f32[32,128]{1,0:T(8,128)} %volume_ref.1, bf16[192,128,128]{2,1,0:T(8,128)(2,1)} %foot_ref.3), custom_call_target="tpu_custom_call" | custom-call | tf_op jit(solution)/shard_map/offer/pallas_call | solution.py:124
  1.8 24.5 %all_to_all.10.slab_ref = bf16[32,40,128]{2,1,0:T(8,128)(2,1)S(1)} all-to-all(bf16[32,40,128]{2,1,0:T(8,128)(2,1)S(1)} %offer.1), channel_id=1, replica_groups=mesh['slab'=8,'angle'=32] {'angle'}, dimensions={0} | all-to-all | bytes 655360 | tf_op jit(solution)/shard_map/all_to_all | solution.py:144
  26.3 0.0 copy-done.3
  26.3 0.0 copy-done
  26.3 0.0 copy-done.5
  26.3 0.0 copy-done.4
  26.3 0.0 copy-start.1
  26.4 2.4 %forward.1 = (f32[128,128]{1,0:T(8,128)S(1)}, f32[8,128]{1,0:T(8,128)S(1)}) custom-call(bf16[32,40,128]{2,1,0:T(8,128)(2,1)S(1)} %all_to_all.10.slab_ref, s32[192]{0:T(256)S(1)} %copy-done.3, s32[192]{0:T(256)S(1)} %copy-done.4, s32[192]{0:T(256)S(1)} %copy-done.5, bf16[192,128,128]{2,1,0:T(8,128)(2,1)S(1)} %copy-done), custom_call_target="tpu_custom_call" | custom-call | tf_op jit(solution)/shard_map/forward/pallas_call | solution.py:124
  28.7 0.1 collective-permute-start
  28.8 1.2 %collective-permute-done = f32[128,128]{1,0:T(8,128)S(1)} collective-permute-done((f32[128,128]{1,0:T(8,128)S(1)}, f32[128,128]{1,0:T(8,128)S(1)}, u32[]{:S(2)}, u32[]{:S(2)}) %collective-permute-start) | collective-permute-done | bytes 65568 | tf_op jit(solution)/shard_map/ppermute | solution.py:152
  30.1 3.1 %collective-permute-start.3 = (f32[128,128]{1,0:T(8,128)S(1)}, f32[128,128]{1,0:T(8,128)S(1)}, u32[]{:S(2)}, u32[]{:S(2)}) collective-permute-start(f32[128,128]{1,0:T(8,128)S(1)} %add.3.mine_ref), channel_id=1, source_target_pairs={{0,192},{32,224},{64,0},{96,32},{128,64},{160,96},{192,128},{224,1... | collective-permute-start | bytes 196616 | tf_op jit(solution)/shard_map/ppermute | solution.py:154
  33.2 0.0 collective-permute-start.2
  33.2 2.2 %collective-permute-start.1 = (f32[128,128]{1,0:T(8,128)S(1)}, f32[128,128]{1,0:T(8,128)S(1)}, u32[]{:S(2)}, u32[]{:S(2)}) collective-permute-start(f32[128,128]{1,0:T(8,128)S(1)} %add.3.mine_ref), channel_id=1, source_target_pairs={{0,128},{32,160},{64,192},{96,224},{128,0},{160,32},{192,64},{224,... | collective-permute-start | bytes 196616 | tf_op jit(solution)/shard_map/ppermute | solution.py:154
  35.4 0.0 collective-permute-done.3.right_ref
  35.4 4.3 %collective-permute-done.2.left_ref = f32[128,128]{1,0:T(8,128)S(1)} collective-permute-done((f32[128,128]{1,0:T(8,128)S(1)}, f32[128,128]{1,0:T(8,128)S(1)}, u32[]{:S(2)}, u32[]{:S(2)}) %collective-permute-start.2) | collective-permute-done | bytes 65568 | tf_op jit(solution)/shard_map/ppermute | solution.py:154
  39.7 0.0 collective-permute-done.1.across_ref
  39.7 0.0 copy-done.2
  39.7 1.7 %backward.1 = (f32[64,128]{1,0:T(8,128)S(1)}, f32[32,24,128]{2,1,0:T(8,128)S(1)}) custom-call(s32[192]{0:T(256)S(1)} %copy-done.3, f32[128,128]{1,0:T(8,128)S(1)} %add.3.mine_ref, f32[128,128]{1,0:T(8,128)S(1)} %collective-permute-done.1.across_ref, f32[128,128]{1,0:T(8,128)S(1)} %collective-permute-done.2.left_ref, ...), custom_call_target="tpu_custom_call" | custom-call | tf_op jit(solution)/shard_map/backward/pallas_call | solution.py:124
  41.4 18.3 %all_to_all.11.recv_ref = f32[32,24,128]{2,1,0:T(8,128)S(1)} all-to-all(f32[32,24,128]{2,1,0:T(8,128)S(1)} %get-tuple-element.7), channel_id=1, replica_groups=mesh['slab'=8,'angle'=32] {'angle'}, dimensions={0} | all-to-all | bytes 786432 | tf_op jit(solution)/shard_map/all_to_all | solution.py:164
  59.7 0.0 copy-done.1
  59.7 0.9 %update.1 = (f32[32,128]{1,0:T(8,128)}, f32[64,128]{1,0:T(8,128)}) custom-call(f32[32,24,128]{2,1,0:T(8,128)S(1)} %all_to_all.11.recv_ref, f32[8,128]{1,0:T(8,128)S(1)} %get-tuple-element.8.places_ref, f32[32,128]{1,0:T(8,128)S(1)} %copy-done.1, f32[64,128]{1,0:T(8,128)S(1)} %get-tuple-element.9.weighted_ref), custom_call_target="tpu_custom_call" | custom-call | tf_op jit(solution)/shard_map/update/pallas_call | solution.py:124
  (1 shorter events, 0.0 us)
Async XLA Ops:
  0.6 25.7 %copy-start.3 = (s32[192]{0:T(256)S(1)}, s32[192]{0:T(256)}, u32[]{:S(2)}) copy-start(s32[192]{0:T(256)} %voxel_ref.3) | copy-start | bytes 2308
  0.6 25.7 %copy-start = (bf16[192,128,128]{2,1,0:T(8,128)(2,1)S(1)}, bf16[192,128,128]{2,1,0:T(8,128)(2,1)}, u32[]{:S(2)}) copy-start(bf16[192,128,128]{2,1,0:T(8,128)(2,1)} %foot_ref.3) | copy-start | bytes 18874372
  0.7 25.7 %copy-start.5 = (s32[192]{0:T(256)S(1)}, s32[192]{0:T(256)}, u32[]{:S(2)}) copy-start(s32[192]{0:T(256)} %rows_ref.3) | copy-start | bytes 2308
  0.7 25.7 %copy-start.4 = (s32[192]{0:T(256)S(1)}, s32[192]{0:T(256)}, u32[]{:S(2)}) copy-start(s32[192]{0:T(256)} %tile_ref.3) | copy-start | bytes 2308
  0.7 39.0 %copy-start.2 = (f32[64,128]{1,0:T(8,128)S(1)}, f32[64,128]{1,0:T(8,128)}, u32[]{:S(2)}) copy-start(f32[64,128]{1,0:T(8,128)} %measured_ref.1) | copy-start | bytes 98308
  26.3 33.3 %copy-start.1 = (f32[32,128]{1,0:T(8,128)S(1)}, f32[32,128]{1,0:T(8,128)}, u32[]{:S(2)}) copy-start(f32[32,128]{1,0:T(8,128)} %volume_ref.1) | copy-start | bytes 49156
  28.7 1.3 %collective-permute-start = (f32[128,128]{1,0:T(8,128)S(1)}, f32[128,128]{1,0:T(8,128)S(1)}, u32[]{:S(2)}, u32[]{:S(2)}) collective-permute-start(f32[128,128]{1,0:T(8,128)S(1)} %get-tuple-element.6), channel_id=1, source_target_pairs={{0,32},{32,0},{64,96},{96,64},{128,160},{160,128},{192,224},{224,1... | collective-permute-start | bytes 196616 | tf_op jit(solution)/shard_map/ppermute | solution.py:152
  30.1 5.3 %collective-permute-start.3 = (f32[128,128]{1,0:T(8,128)S(1)}, f32[128,128]{1,0:T(8,128)S(1)}, u32[]{:S(2)}, u32[]{:S(2)}) collective-permute-start(f32[128,128]{1,0:T(8,128)S(1)} %add.3.mine_ref), channel_id=1, source_target_pairs={{0,192},{32,224},{64,0},{96,32},{128,64},{160,96},{192,128},{224,1... | collective-permute-start | bytes 196616 | tf_op jit(solution)/shard_map/ppermute | solution.py:154
  33.2 6.5 %collective-permute-start.2 = (f32[128,128]{1,0:T(8,128)S(1)}, f32[128,128]{1,0:T(8,128)S(1)}, u32[]{:S(2)}, u32[]{:S(2)}) collective-permute-start(f32[128,128]{1,0:T(8,128)S(1)} %add.3.mine_ref), channel_id=1, source_target_pairs={{0,64},{32,96},{64,128},{96,160},{128,192},{160,224},{192,0},{224,... | collective-permute-start | bytes 196616 | tf_op jit(solution)/shard_map/ppermute | solution.py:154
  33.2 6.5 %collective-permute-start.1 = (f32[128,128]{1,0:T(8,128)S(1)}, f32[128,128]{1,0:T(8,128)S(1)}, u32[]{:S(2)}, u32[]{:S(2)}) collective-permute-start(f32[128,128]{1,0:T(8,128)S(1)} %add.3.mine_ref), channel_id=1, source_target_pairs={{0,128},{32,160},{64,192},{96,224},{128,0},{160,32},{192,64},{224,... | collective-permute-start | bytes 196616 | tf_op jit(solution)/shard_map/ppermute | solution.py:154

commit v5 on v4

v5 whole, which is shorter than its diff:
```python
import jax
import jax.numpy as jnp
from jax import lax
from jax.experimental import pallas as pl
from jax.experimental.pallas import tpu as pltpu
from jax.sharding import PartitionSpec as P

BLK = 128
NB = 192
CAP = 12
SHARES = 32
SET = 64
LINES = 2 * CAP
F32 = jnp.float32
BF16 = jnp.bfloat16
VMEM = pl.BlockSpec(memory_space=pltpu.VMEM)
SMEM = pl.BlockSpec(memory_space=pltpu.SMEM)
HBM = pl.BlockSpec(memory_space=pltpu.HBM)
PARAMS = pltpu.CompilerParams(vmem_limit_bytes=40 * 1024 * 1024)
ROWS = ((1,), (0,))
LANES = ((1,), (1,))
SUBLANES = ((0,), (0,))


def dot(a, b, contract=ROWS):
    return lax.dot_general(a, b, (contract, ((), ())), preferred_element_type=F32)


def iota(shape, dim):
    return lax.broadcasted_iota(jnp.int32, shape, dim)


def exact_dot(onehot, x, contract=ROWS):
    hi = x.astype(BF16)
    rest = x - hi.astype(F32)
    mid = rest.astype(BF16)
    lo = (rest - mid.astype(F32)).astype(BF16)
    return dot(onehot, hi, contract) + (dot(onehot, mid, contract) + dot(onehot, lo, contract))


def per_slot(vectors, matrices, group=16):
    row = iota((group, BLK), 0)
    out = []
    for g in range(0, NB, group):
        mine = vectors[g : g + group]
        diag = jnp.concatenate([jnp.where(row == i, mine, 0.0) for i in range(group)], axis=1).astype(BF16)
        out.append(dot(diag, matrices[g : g + group].reshape(group * BLK, BLK)))
    return jnp.concatenate(out, axis=0)


def hot_columns(ref, n):
    return jnp.where(iota((n, NB), 0) == ref[...].reshape(1, NB), 1.0, 0.0).astype(BF16)


def twice(x):
    return jnp.concatenate([x[:, g : g + SET] for g in range(0, NB, SET) for _ in range(2)], axis=1)


def power(k):
    return lax.shift_left(jnp.ones_like(k), k).astype(F32)


def quantize(x, place):
    largest = jnp.max(jnp.abs(x), axis=1, keepdims=True)
    k = jnp.clip(jnp.floor(jnp.log2(jnp.maximum(largest, 2.0**-20))).astype(jnp.int32) + 15, 1, 31)
    q = jnp.clip(jnp.round(x * (power(31 - k) * 0.25)), -32767.0, 32767.0)
    return q.astype(jnp.int32), 128 * (k - 1) + place + 1


def offer_kernel(volume_any, foot_any, send_ref, volume_ref, sem):
    copy = pltpu.make_async_copy(volume_any, volume_ref, sem)
    copy.start()
    copy.wait()
    send_ref[...] = jnp.broadcast_to(volume_ref[...].astype(BF16), (SHARES, 32, BLK))


def forward_kernel(slab_ref, voxel_ref, tile_ref, rows_ref, foot_ref, part_ref):
    picked = dot(slab_ref[...].reshape(1024, BLK), hot_columns(voxel_ref, 1024), SUBLANES)
    even = iota((1, BLK), 1) % 2 == 0
    sums = []
    for g in range(0, NB, SET):
        mine = jnp.concatenate([picked[:, g : g + SET], jnp.ones((BLK, SET), F32)], axis=1)
        cols = jnp.concatenate([jnp.where(even, mine, 0.0), jnp.where(even, 0.0, mine)], axis=0).astype(BF16)
        total = jnp.zeros((BLK, BLK), F32)
        for q in range(SET // 2):
            pair = jnp.concatenate([foot_ref[g + 2 * q], foot_ref[g + 2 * q + 1]], axis=1)
            total = jnp.where(iota((1, BLK), 1) % SET // 2 == q, dot(pair, cols), total)
        sums.append(total)
    live = iota((BLK, 2 * NB), 0) < twice(rows_ref[...].reshape(1, NB))
    tile = twice(tile_ref[...].reshape(1, NB))
    wanted = tile + jnp.where(iota((1, 2 * NB), 1) % BLK < SET, 0, 64)
    tile_hot = jnp.where(iota((BLK, 2 * NB), 0) == wanted, 1.0, 0.0).astype(BF16)
    part_ref[...] = exact_dot(tile_hot, jnp.where(live, jnp.concatenate(sums, axis=1), 0.0), LANES)


def columns_kernel(voxel_ref, rows_ref, foot_ref, live_ref, place_ref, sums_ref, codes_ref):
    live = jnp.where(iota((BLK, NB), 0) < rows_ref[...].reshape(1, NB), 1.0, 0.0).T
    live_ref[...] = live
    place = (jnp.broadcast_to(voxel_ref[...].reshape(1, NB), (BLK, NB)) & 31).astype(F32).T.astype(jnp.int32)
    place_ref[...] = place
    sums_ref[...], codes_ref[...] = quantize(per_slot(live, foot_ref), place + 32)


def backward_kernel(voxel_ref, mine_ref, across_ref, left_ref, right_ref, measured_ref, tile_ref, live_ref, place_ref, sums_ref, codes_ref, foot_ref, weighted_ref, send_ref):
    total = (mine_ref[...] + across_ref[...]) + (left_ref[...] + right_ref[...])
    weighted = (measured_ref[...] - total[:64]) / jnp.maximum(total[64:], 1.0)
    weighted_ref[...] = weighted
    residual = dot(hot_columns(tile_ref, 64), weighted.astype(BF16), SUBLANES) * live_ref[...]
    backs, codes = quantize(per_slot(residual, foot_ref), place_ref[...])
    send_ref[...] = jnp.zeros_like(send_ref)
    first = LINES * lax.axis_index("angle")
    line = iota((LINES, BLK), 0)
    mine = iota((LINES, BLK), 1) == (first + line) & (BLK - 1)
    spot = iota((8, BLK), 0) * BLK + iota((8, BLK), 1) - first
    spot = (spot >= 0) & (spot < LINES)
    for j in range(NB // CAP):
        at = slice(CAP * j, CAP * (j + 1))
        code = jnp.concatenate([codes[at], codes_ref[at]], axis=0)
        code = jnp.sum(jnp.where(mine, code, 0), axis=0, keepdims=True)
        code = jnp.where(spot, jnp.broadcast_to(code, (8, BLK)), 0)
        send_ref[voxel_ref[CAP * j] >> 5] = jnp.concatenate([backs[at], sums_ref[at], code], axis=0).astype(jnp.int16)


def update_kernel(recv_ref, volume_ref, weighted_ref, out_ref, weighted_out_ref):
    weighted_out_ref[...] = weighted_ref[...]
    codes = jnp.sum(recv_ref[:, LINES:, :].astype(jnp.int32), axis=0)
    scale = power(lax.shift_right_logical(codes, 7)) * 2.0**-28
    place = (codes & 127) - 1
    wanted = iota((2 * 32, BLK), 0)
    hot = jnp.concatenate(
        [
            jnp.where(place[m : m + 1, :] == wanted, jnp.broadcast_to(scale[m : m + 1, :], wanted.shape), 0.0)
            for m in range(SHARES * LINES // BLK)
        ],
        axis=1,
    ).astype(BF16)
    values = recv_ref[:, :LINES, :].astype(F32).reshape(SHARES * LINES, BLK)
    high = jnp.floor(values * (1.0 / 256.0)) * 256.0
    summed = dot(hot, high.astype(BF16)) + dot(hot, (values - high).astype(BF16))
    out_ref[...] = volume_ref[...] + summed[:32] / jnp.maximum(summed[32:], 1.0)


def call(kernel, name, out, specs, *args, scratch=()):
    out = [jax.ShapeDtypeStruct(*o) for o in out]
    return pl.pallas_call(
        kernel,
        out_shape=out,
        in_specs=specs,
        out_specs=[VMEM] * len(out),
        scratch_shapes=scratch,
        compiler_params=PARAMS,
        name=name,
    )(*args)


def on_device(volume, measured, footprint, block_voxel, block_tile, block_rows):
    (offer,) = call(
        offer_kernel,
        "offer",
        [((SHARES, 32, BLK), BF16)],
        [HBM] * 2,
        *(pltpu.with_memory_space_constraint(x, pltpu.HBM) for x in (volume, footprint)),
        scratch=[pltpu.VMEM((32, BLK), F32), pltpu.SemaphoreType.DMA],
    )
    slab_values = lax.all_to_all(offer, "angle", 0, 0)
    (part,) = call(
        forward_kernel,
        "forward",
        [((2 * 64, BLK), F32)],
        [VMEM] * 5,
        slab_values, block_voxel, block_tile, block_rows, footprint,
    )
    part = part + lax.ppermute(part, "slab", [(i, i ^ 1) for i in range(8)])
    across, left, right = (
        lax.ppermute(part, "slab", [(i, (i + 2 * k) % 8) for i in range(8)]) for k in (2, 1, 3)
    )
    live, place, column_sums, column_codes = call(
        columns_kernel,
        "columns",
        [((NB, BLK), F32)] + [((NB, BLK), jnp.int32)] * 3,
        [VMEM] * 3,
        block_voxel, block_rows, footprint,
    )
    weighted, send_back = call(
        backward_kernel,
        "backward",
        [((64, BLK), F32), ((SHARES, 32, BLK), jnp.int16)],
        [SMEM] + [VMEM] * 11,
        block_voxel, part, across, left, right, measured, block_tile, live, place, column_sums, column_codes, footprint,
    )
    received = lax.all_to_all(send_back, "angle", 0, 0)
    return call(
        update_kernel,
        "update",
        [((32, BLK), F32), ((64, BLK), F32)],
        [VMEM] * 3,
        received, volume, weighted,
    )


def solution(mesh):
    in_specs = (
        P(("slab", "angle"), None),
        P("angle", None),
        P(("slab", "angle"), None, None),
        P(("slab", "angle")),
        P(("slab", "angle")),
        P(("slab", "angle")),
    )
    out_specs = (P(("slab", "angle"), None), P("angle", None))
    return jax.shard_map(
        on_device, mesh=mesh, in_specs=in_specs, out_specs=out_specs, check_vma=False
    )
```

time: 60.7 us -> 57 us (0.939)
  blocking collectives: 42.8 us -> 38.9 us
  waiting for transfers between devices: 5.53 us -> 4.42 us
  Pallas kernels: 6.04 us -> 7.04 us
    all_to_all x1, blocking collectives: 18.3 us -> 15.5 us  [on_device(): received = lax.all_to_all(send_back, 'angle', 0, 0)]
    all_to_all x1, blocking collectives: 24.5 us -> 23.4 us  [on_device(): slab_values = lax.all_to_all(offer, 'angle', 0, 0)]
    ppermute x3, waiting for transfers between devices: 4.29 us -> 3.17 us  [on_device(): lax.ppermute(part, 'slab', [(i, (i + 2 * k) % 8) for i in range(8)])]
    pallas_call x4 -> x5, Pallas kernels: 6.04 us -> 7.04 us  [call(): pl.pallas_call(kernel, out_shape=out, in_specs=specs, out_specs=[VMEM] *...]
  transfers between devices with their start and end apart: 4 -> 4, of which waited for: 2 -> 2; matrix products, arithmetic and copies ran while one was open for 0% -> 0% of each run, Pallas kernels for 0% -> 2%
where the time goes in v5:
time: 57 us; the launch traced here: 56.6 us
  blocking collectives  38.9 us (68%)
  Pallas kernels  7.04 us (12%)
  starting transfers between devices  5.38 us (9%)
  waiting for transfers between devices  4.42 us (8%)
  between operations  0.74 us (1%)
    all_to_all x1, blocking collectives, on_device(): slab_values = lax.all_to_all(offer, 'angle', 0, 0)  23.4 us
    all_to_all x1, blocking collectives, on_device(): received = lax.all_to_all(send_back, 'angle', 0, 0)  15.5 us
    pallas_call x5, Pallas kernels, call(): pl.pallas_call(kernel, out_shape=out, in_specs=specs, out_specs=[VMEM] *...  7.04 us
    ppermute x3, starting transfers between devices, on_device(): lax.ppermute(part, 'slab', [(i, (i + 2 * k) % 8) for i in range(8)])  5.29 us
    ppermute x3, waiting for transfers between devices, on_device(): lax.ppermute(part, 'slab', [(i, (i + 2 * k) % 8) for i in range(8)])  3.17 us
    ppermute x1, waiting for transfers between devices, on_device(): part = part + lax.ppermute(part, 'slab', [(i, i ^ 1) for i in range(8)])  1.24 us
  transfers between devices with their start and end apart: 4, of which 2 were waited for; matrix products, arithmetic and copies ran while one was open for 0% of the time, Pallas kernels for 2%

profile of v5, /device:TPU:32, one launch (start us, length us, event | category | flops | bytes accessed | tf_op | source)
XLA Modules:
  0.0 56.6 jit_solution(7198444198300702758)
XLA Ops:
  0.6 0.0 copy-start
  0.6 0.0 copy-start.3
  0.7 0.0 copy-start.4
  0.7 0.0 copy-start.5
  0.7 0.9 %offer.1 = bf16[32,32,128]{2,1,0:T(8,128)(2,1)S(1)} custom-call(f32[32,128]{1,0:T(8,128)} %volume_ref.1, bf16[192,128,128]{2,1,0:T(8,128)(2,1)} %foot_ref.5), custom_call_target="tpu_custom_call" | custom-call | tf_op jit(solution)/shard_map/offer/pallas_call | solution.py:145
  1.6 23.4 %all_to_all.10.slab_ref = bf16[32,32,128]{2,1,0:T(8,128)(2,1)S(1)} all-to-all(bf16[32,32,128]{2,1,0:T(8,128)(2,1)S(1)} %offer.1), channel_id=1, replica_groups=mesh['slab'=8,'angle'=32] {'angle'}, dimensions={0} | all-to-all | bytes 524288 | tf_op jit(solution)/shard_map/all_to_all | solution.py:165
  25.0 0.0 copy-done
  25.0 0.0 copy-done.3
  25.0 0.0 copy-done.4
  25.0 0.0 copy-done.5
  25.0 0.0 copy-start.2
  25.0 2.4 %forward.1 = f32[128,128]{1,0:T(8,128)S(1)} custom-call(bf16[32,32,128]{2,1,0:T(8,128)(2,1)S(1)} %all_to_all.10.slab_ref, s32[192]{0:T(256)S(1)} %copy-done.3, s32[192]{0:T(256)S(1)} %copy-done.5, s32[192]{0:T(256)S(1)} %copy-done.4, bf16[192,128,128]{2,1,0:T(8,128)(2,1)S(1)} %copy-done), custom_call_target="tpu_custom_call" | custom-call | tf_op jit(solution)/shard_map/forward/pallas_call | solution.py:145
  27.4 0.1 collective-permute-start
  27.5 1.2 %collective-permute-done = f32[128,128]{1,0:T(8,128)S(1)} collective-permute-done((f32[128,128]{1,0:T(8,128)S(1)}, f32[128,128]{1,0:T(8,128)S(1)}, u32[]{:S(2)}, u32[]{:S(2)}) %collective-permute-start) | collective-permute-done | bytes 65568 | tf_op jit(solution)/shard_map/ppermute | solution.py:173
  28.8 0.0 copy-start.1
  28.8 3.1 %collective-permute-start.3 = (f32[128,128]{1,0:T(8,128)S(1)}, f32[128,128]{1,0:T(8,128)S(1)}, u32[]{:S(2)}, u32[]{:S(2)}) collective-permute-start(f32[128,128]{1,0:T(8,128)S(1)} %add.3.mine_ref), channel_id=1, source_target_pairs={{0,192},{32,224},{64,0},{96,32},{128,64},{160,96},{192,128},{224,1... | collective-permute-start | bytes 196616 | tf_op jit(solution)/shard_map/ppermute | solution.py:175
  31.9 0.0 collective-permute-start.2
  31.9 2.2 %collective-permute-start.1 = (f32[128,128]{1,0:T(8,128)S(1)}, f32[128,128]{1,0:T(8,128)S(1)}, u32[]{:S(2)}, u32[]{:S(2)}) collective-permute-start(f32[128,128]{1,0:T(8,128)S(1)} %add.3.mine_ref), channel_id=1, source_target_pairs={{0,128},{32,160},{64,192},{96,224},{128,0},{160,32},{192,64},{224,... | collective-permute-start | bytes 196616 | tf_op jit(solution)/shard_map/ppermute | solution.py:175
  34.1 1.1 %columns.1 = (f32[192,128]{1,0:T(8,128)S(1)}, s32[192,128]{1,0:T(8,128)S(1)}, s32[192,128]{1,0:T(8,128)S(1)}, s32[192,128]{1,0:T(8,128)S(1)}) custom-call(s32[192]{0:T(256)S(1)} %copy-done.3, s32[192]{0:T(256)S(1)} %copy-done.4, bf16[192,128,128]{2,1,0:T(8,128)(2,1)S(1)} %copy-done), custom_call_target="tpu_custom_call" | custom-call | tf_op jit(solution)/shard_map/columns/pallas_call | solution.py:145
  35.2 0.0 collective-permute-done.3.right_ref
  35.2 3.2 %collective-permute-done.2.left_ref = f32[128,128]{1,0:T(8,128)S(1)} collective-permute-done((f32[128,128]{1,0:T(8,128)S(1)}, f32[128,128]{1,0:T(8,128)S(1)}, u32[]{:S(2)}, u32[]{:S(2)}) %collective-permute-start.2) | collective-permute-done | bytes 65568 | tf_op jit(solution)/shard_map/ppermute | solution.py:175
  38.3 0.0 collective-permute-done.1.across_ref
  38.4 0.0 copy-done.2
  38.4 1.8 %backward.1 = (f32[64,128]{1,0:T(8,128)S(1)}, s16[32,32,128]{2,1,0:T(8,128)(2,1)S(1)}) custom-call(s32[192]{0:T(256)S(1)} %copy-done.3, f32[128,128]{1,0:T(8,128)S(1)} %add.3.mine_ref, f32[128,128]{1,0:T(8,128)S(1)} %collective-permute-done.1.across_ref, f32[128,128]{1,0:T(8,128)S(1)} %collective-permute-done.2.left_ref, ...), custom_call_target="tpu_custom_call" | custom-call | tf_op jit(solution)/shard_map/backward/pallas_call | solution.py:145
  40.1 15.5 %all_to_all.11.recv_ref = s16[32,32,128]{2,1,0:T(8,128)(2,1)S(1)} all-to-all(s16[32,32,128]{2,1,0:T(8,128)(2,1)S(1)} %get-tuple-element.12), channel_id=1, replica_groups=mesh['slab'=8,'angle'=32] {'angle'}, dimensions={0} | all-to-all | bytes 524288 | tf_op jit(solution)/shard_map/all_to_all | solution.py:191
  55.6 0.0 copy-done.1
  55.7 0.9 %update.1 = (f32[32,128]{1,0:T(8,128)}, f32[64,128]{1,0:T(8,128)}) custom-call(s16[32,32,128]{2,1,0:T(8,128)(2,1)S(1)} %all_to_all.11.recv_ref, f32[32,128]{1,0:T(8,128)S(1)} %copy-done.1, f32[64,128]{1,0:T(8,128)S(1)} %get-tuple-element.13.weighted_ref), custom_call_target="tpu_custom_call" | custom-call | tf_op jit(solution)/shard_map/update/pallas_call | solution.py:145
  (1 shorter events, 0.0 us)
Async XLA Ops:
  0.6 24.4 %copy-start = (bf16[192,128,128]{2,1,0:T(8,128)(2,1)S(1)}, bf16[192,128,128]{2,1,0:T(8,128)(2,1)}, u32[]{:S(2)}) copy-start(bf16[192,128,128]{2,1,0:T(8,128)(2,1)} %foot_ref.5) | copy-start | bytes 18874372
  0.6 24.4 %copy-start.3 = (s32[192]{0:T(256)S(1)}, s32[192]{0:T(256)}, u32[]{:S(2)}) copy-start(s32[192]{0:T(256)} %voxel_ref.5) | copy-start | bytes 2308
  0.7 24.3 %copy-start.4 = (s32[192]{0:T(256)S(1)}, s32[192]{0:T(256)}, u32[]{:S(2)}) copy-start(s32[192]{0:T(256)} %rows_ref.3) | copy-start | bytes 2308
  0.7 24.3 %copy-start.5 = (s32[192]{0:T(256)S(1)}, s32[192]{0:T(256)}, u32[]{:S(2)}) copy-start(s32[192]{0:T(256)} %tile_ref.3) | copy-start | bytes 2308
  25.0 13.3 %copy-start.2 = (f32[64,128]{1,0:T(8,128)S(1)}, f32[64,128]{1,0:T(8,128)}, u32[]{:S(2)}) copy-start(f32[64,128]{1,0:T(8,128)} %measured_ref.1) | copy-start | bytes 98308
  27.4 1.3 %collective-permute-start = (f32[128,128]{1,0:T(8,128)S(1)}, f32[128,128]{1,0:T(8,128)S(1)}, u32[]{:S(2)}, u32[]{:S(2)}) collective-permute-start(f32[128,128]{1,0:T(8,128)S(1)} %forward.1), channel_id=1, source_target_pairs={{0,32},{32,0},{64,96},{96,64},{128,160},{160,128},{192,224},{224,1... | collective-permute-start | bytes 196616 | tf_op jit(solution)/shard_map/ppermute | solution.py:173
  28.8 26.9 %copy-start.1 = (f32[32,128]{1,0:T(8,128)S(1)}, f32[32,128]{1,0:T(8,128)}, u32[]{:S(2)}) copy-start(f32[32,128]{1,0:T(8,128)} %volume_ref.1) | copy-start | bytes 49156
  28.8 6.4 %collective-permute-start.3 = (f32[128,128]{1,0:T(8,128)S(1)}, f32[128,128]{1,0:T(8,128)S(1)}, u32[]{:S(2)}, u32[]{:S(2)}) collective-permute-start(f32[128,128]{1,0:T(8,128)S(1)} %add.3.mine_ref), channel_id=1, source_target_pairs={{0,192},{32,224},{64,0},{96,32},{128,64},{160,96},{192,128},{224,1... | collective-permute-start | bytes 196616 | tf_op jit(solution)/shard_map/ppermute | solution.py:175
  31.9 6.5 %collective-permute-start.2 = (f32[128,128]{1,0:T(8,128)S(1)}, f32[128,128]{1,0:T(8,128)S(1)}, u32[]{:S(2)}, u32[]{:S(2)}) collective-permute-start(f32[128,128]{1,0:T(8,128)S(1)} %add.3.mine_ref), channel_id=1, source_target_pairs={{0,64},{32,96},{64,128},{96,160},{128,192},{160,224},{192,0},{224,... | collective-permute-start | bytes 196616 | tf_op jit(solution)/shard_map/ppermute | solution.py:175
  31.9 6.5 %collective-permute-start.1 = (f32[128,128]{1,0:T(8,128)S(1)}, f32[128,128]{1,0:T(8,128)S(1)}, u32[]{:S(2)}, u32[]{:S(2)}) collective-permute-start(f32[128,128]{1,0:T(8,128)S(1)} %add.3.mine_ref), channel_id=1, source_target_pairs={{0,128},{32,160},{64,192},{96,224},{128,0},{160,32},{192,64},{224,... | collective-permute-start | bytes 196616 | tf_op jit(solution)/shard_map/ppermute | solution.py:175

commit v6 on v5

--- a/solution.py
+++ b/solution.py
@@ -9,7 +9,9 @@
 NB = 192
 CAP = 12
 SHARES = 32
-SET = 64
+GROUP = 16
+TURNED = 128
+SET = NB - TURNED
 LINES = 2 * CAP
 F32 = jnp.float32
 BF16 = jnp.bfloat16
@@ -38,7 +40,7 @@
     return dot(onehot, hi, contract) + (dot(onehot, mid, contract) + dot(onehot, lo, contract))
 
 
-def per_slot(vectors, matrices, group=16):
+def per_slot(vectors, matrices, group=GROUP):
     row = iota((group, BLK), 0)
     out = []
     for g in range(0, NB, group):
@@ -52,10 +54,6 @@
     return jnp.where(iota((n, NB), 0) == ref[...].reshape(1, NB), 1.0, 0.0).astype(BF16)
 
 
-def twice(x):
-    return jnp.concatenate([x[:, g : g + SET] for g in range(0, NB, SET) for _ in range(2)], axis=1)
-
-
 def power(k):
     return lax.shift_left(jnp.ones_like(k), k).astype(F32)
 
@@ -76,21 +74,39 @@
 
 def forward_kernel(slab_ref, voxel_ref, tile_ref, rows_ref, foot_ref, part_ref):
     picked = dot(slab_ref[...].reshape(1024, BLK), hot_columns(voxel_ref, 1024), SUBLANES)
-    even = iota((1, BLK), 1) % 2 == 0
-    sums = []
-    for g in range(0, NB, SET):
-        mine = jnp.concatenate([picked[:, g : g + SET], jnp.ones((BLK, SET), F32)], axis=1)
-        cols = jnp.concatenate([jnp.where(even, mine, 0.0), jnp.where(even, 0.0, mine)], axis=0).astype(BF16)
-        total = jnp.zeros((BLK, BLK), F32)
-        for q in range(SET // 2):
-            pair = jnp.concatenate([foot_ref[g + 2 * q], foot_ref[g + 2 * q + 1]], axis=1)
-            total = jnp.where(iota((1, BLK), 1) % SET // 2 == q, dot(pair, cols), total)
-        sums.append(total)
-    live = iota((BLK, 2 * NB), 0) < twice(rows_ref[...].reshape(1, NB))
-    tile = twice(tile_ref[...].reshape(1, NB))
-    wanted = tile + jnp.where(iota((1, 2 * NB), 1) % BLK < SET, 0, 64)
-    tile_hot = jnp.where(iota((BLK, 2 * NB), 0) == wanted, 1.0, 0.0).astype(BF16)
-    part_ref[...] = exact_dot(tile_hot, jnp.where(live, jnp.concatenate(sums, axis=1), 0.0), LANES)
+    rows = rows_ref[...].reshape(1, NB)
+    tile = tile_ref[...].reshape(1, NB)
+    twice = lambda x: jnp.concatenate([x[:, TURNED:]] * 2, axis=1)
+
+    lane = iota((1, BLK), 1)
+    cols = jnp.concatenate([picked[:, TURNED:], jnp.ones((BLK, SET), F32)], axis=1)
+    cols = jnp.concatenate([jnp.where(lane % 2 == n, cols, 0.0) for n in range(2)], axis=0).astype(BF16)
+    streamed = jnp.zeros((BLK, BLK), F32)
+
+    values = picked.T
+    live = jnp.where(iota((BLK, NB), 0) < rows, 1.0, 0.0).T
+    row = iota((GROUP, BLK), 0)
+    one = jnp.ones((GROUP, BLK), F32)
+    turned = []
+    steps = TURNED // GROUP
+    for g in range(steps):
+        at = slice(GROUP * g, GROUP * (g + 1))
+        weights = jnp.concatenate([foot_ref[k].T for k in range(at.start, at.stop)], axis=0)
+        for q in range(SET // 2 * g // steps, SET // 2 * (g + 1) // steps):
+            k = TURNED + 2 * q
+            pair = jnp.concatenate([foot_ref[k], foot_ref[k + 1]], axis=1)
+            streamed = jnp.where(lane % SET // 2 == q, dot(pair, cols), streamed)
+        both = jnp.concatenate([values[at], one], axis=0)
+        both_row = jnp.concatenate([row, row], axis=0)
+        diag = jnp.concatenate([jnp.where(both_row == i, both, 0.0) for i in range(GROUP)], axis=1)
+        out = dot(diag.astype(BF16), weights)
+        turned.append(jnp.concatenate([out[:GROUP] * live[at], out[GROUP:] * live[at]], axis=1))
+    tile_hot = jnp.where(iota((64, TURNED), 0) == tile[:, :TURNED], 1.0, 0.0).astype(BF16)
+    first = exact_dot(tile_hot, jnp.concatenate(turned, axis=0))
+    wanted = twice(tile) + jnp.where(lane < SET, 0, 64)
+    tile_hot = jnp.where(iota((BLK, BLK), 0) == wanted, 1.0, 0.0).astype(BF16)
+    second = exact_dot(tile_hot, jnp.where(iota((BLK, BLK), 0) < twice(rows), streamed, 0.0), LANES)
+    part_ref[...] = jnp.concatenate([first[:, :BLK], first[:, BLK:]], axis=0) + second
 
 
 def columns_kernel(voxel_ref, rows_ref, foot_ref, live_ref, place_ref, sums_ref, codes_ref):

time: 57 us -> 56.5 us (level)
  no operation moved by 1% of the time
where the time goes in v6:
time: 56.5 us; the launch traced here: 56 us
  blocking collectives  38.9 us (69%)
  Pallas kernels  6.52 us (12%)
  starting transfers between devices  5.39 us (10%)
  waiting for transfers between devices  4.42 us (8%)
  between operations  0.74 us (1%)
    all_to_all x1, blocking collectives, on_device(): slab_values = lax.all_to_all(offer, 'angle', 0, 0)  23.4 us
    all_to_all x1, blocking collectives, on_device(): received = lax.all_to_all(send_back, 'angle', 0, 0)  15.5 us
    pallas_call x5, Pallas kernels, call(): pl.pallas_call(kernel, out_shape=out, in_specs=specs, out_specs=[VMEM] *...  6.52 us
    ppermute x3, starting transfers between devices, on_device(): lax.ppermute(part, 'slab', [(i, (i + 2 * k) % 8) for i in range(8)])  5.3 us
    ppermute x3, waiting for transfers between devices, on_device(): lax.ppermute(part, 'slab', [(i, (i + 2 * k) % 8) for i in range(8)])  3.17 us
    ppermute x1, waiting for transfers between devices, on_device(): part = part + lax.ppermute(part, 'slab', [(i, i ^ 1) for i in range(8)])  1.24 us
  transfers between devices with their start and end apart: 4, of which 2 were waited for; matrix products, arithmetic and copies ran while one was open for 0% of the time, Pallas kernels for 2%

profile of v6, /device:TPU:32, one launch (start us, length us, event | category | flops | bytes accessed | tf_op | source)
XLA Modules:
  0.0 56.0 jit_solution(8257459216187327665)
XLA Ops:
  0.6 0.0 copy-start
  0.6 0.0 copy-start.3
  0.7 0.0 copy-start.4
  0.7 0.0 copy-start.5
  0.7 0.9 %offer.1 = bf16[32,32,128]{2,1,0:T(8,128)(2,1)S(1)} custom-call(f32[32,128]{1,0:T(8,128)} %volume_ref.1, bf16[192,128,128]{2,1,0:T(8,128)(2,1)} %foot_ref.5), custom_call_target="tpu_custom_call" | custom-call | tf_op jit(solution)/shard_map/offer/pallas_call | solution.py:161
  1.6 23.4 %all_to_all.10.slab_ref = bf16[32,32,128]{2,1,0:T(8,128)(2,1)S(1)} all-to-all(bf16[32,32,128]{2,1,0:T(8,128)(2,1)S(1)} %offer.1), channel_id=1, replica_groups=mesh['slab'=8,'angle'=32] {'angle'}, dimensions={0} | all-to-all | bytes 524288 | tf_op jit(solution)/shard_map/all_to_all | solution.py:181
  25.0 0.0 copy-done
  25.0 0.0 copy-done.3
  25.0 0.0 copy-done.4
  25.0 0.0 copy-done.5
  25.0 0.0 copy-start.2
  25.0 1.9 %forward.1 = f32[128,128]{1,0:T(8,128)S(1)} custom-call(bf16[32,32,128]{2,1,0:T(8,128)(2,1)S(1)} %all_to_all.10.slab_ref, s32[192]{0:T(256)S(1)} %copy-done.3, s32[192]{0:T(256)S(1)} %copy-done.5, s32[192]{0:T(256)S(1)} %copy-done.4, bf16[192,128,128]{2,1,0:T(8,128)(2,1)S(1)} %copy-done), custom_call_target="tpu_custom_call" | custom-call | tf_op jit(solution)/shard_map/forward/pallas_call | solution.py:161
  26.9 0.1 collective-permute-start
  27.0 1.2 %collective-permute-done = f32[128,128]{1,0:T(8,128)S(1)} collective-permute-done((f32[128,128]{1,0:T(8,128)S(1)}, f32[128,128]{1,0:T(8,128)S(1)}, u32[]{:S(2)}, u32[]{:S(2)}) %collective-permute-start) | collective-permute-done | bytes 65568 | tf_op jit(solution)/shard_map/ppermute | solution.py:189
  28.2 0.0 copy-start.1
  28.3 3.1 %collective-permute-start.3 = (f32[128,128]{1,0:T(8,128)S(1)}, f32[128,128]{1,0:T(8,128)S(1)}, u32[]{:S(2)}, u32[]{:S(2)}) collective-permute-start(f32[128,128]{1,0:T(8,128)S(1)} %add.3.mine_ref), channel_id=1, source_target_pairs={{0,192},{32,224},{64,0},{96,32},{128,64},{160,96},{192,128},{224,1... | collective-permute-start | bytes 196616 | tf_op jit(solution)/shard_map/ppermute | solution.py:191
  31.3 0.0 collective-permute-start.2
  31.3 2.2 %collective-permute-start.1 = (f32[128,128]{1,0:T(8,128)S(1)}, f32[128,128]{1,0:T(8,128)S(1)}, u32[]{:S(2)}, u32[]{:S(2)}) collective-permute-start(f32[128,128]{1,0:T(8,128)S(1)} %add.3.mine_ref), channel_id=1, source_target_pairs={{0,128},{32,160},{64,192},{96,224},{128,0},{160,32},{192,64},{224,... | collective-permute-start | bytes 196616 | tf_op jit(solution)/shard_map/ppermute | solution.py:191
  33.6 1.1 %columns.1 = (f32[192,128]{1,0:T(8,128)S(1)}, s32[192,128]{1,0:T(8,128)S(1)}, s32[192,128]{1,0:T(8,128)S(1)}, s32[192,128]{1,0:T(8,128)S(1)}) custom-call(s32[192]{0:T(256)S(1)} %copy-done.3, s32[192]{0:T(256)S(1)} %copy-done.4, bf16[192,128,128]{2,1,0:T(8,128)(2,1)S(1)} %copy-done), custom_call_target="tpu_custom_call" | custom-call | tf_op jit(solution)/shard_map/columns/pallas_call | solution.py:161
  34.7 0.0 collective-permute-done.3.right_ref
  34.7 3.2 %collective-permute-done.2.left_ref = f32[128,128]{1,0:T(8,128)S(1)} collective-permute-done((f32[128,128]{1,0:T(8,128)S(1)}, f32[128,128]{1,0:T(8,128)S(1)}, u32[]{:S(2)}, u32[]{:S(2)}) %collective-permute-start.2) | collective-permute-done | bytes 65568 | tf_op jit(solution)/shard_map/ppermute | solution.py:191
  37.8 0.0 collective-permute-done.1.across_ref
  37.8 0.0 copy-done.2
  37.8 1.8 %backward.1 = (f32[64,128]{1,0:T(8,128)S(1)}, s16[32,32,128]{2,1,0:T(8,128)(2,1)S(1)}) custom-call(s32[192]{0:T(256)S(1)} %copy-done.3, f32[128,128]{1,0:T(8,128)S(1)} %add.3.mine_ref, f32[128,128]{1,0:T(8,128)S(1)} %collective-permute-done.1.across_ref, f32[128,128]{1,0:T(8,128)S(1)} %collective-permute-done.2.left_ref, ...), custom_call_target="tpu_custom_call" | custom-call | tf_op jit(solution)/shard_map/backward/pallas_call | solution.py:161
  39.6 15.5 %all_to_all.11.recv_ref = s16[32,32,128]{2,1,0:T(8,128)(2,1)S(1)} all-to-all(s16[32,32,128]{2,1,0:T(8,128)(2,1)S(1)} %get-tuple-element.12), channel_id=1, replica_groups=mesh['slab'=8,'angle'=32] {'angle'}, dimensions={0} | all-to-all | bytes 524288 | tf_op jit(solution)/shard_map/all_to_all | solution.py:207
  55.1 0.0 copy-done.1
  55.1 0.9 %update.1 = (f32[32,128]{1,0:T(8,128)}, f32[64,128]{1,0:T(8,128)}) custom-call(s16[32,32,128]{2,1,0:T(8,128)(2,1)S(1)} %all_to_all.11.recv_ref, f32[32,128]{1,0:T(8,128)S(1)} %copy-done.1, f32[64,128]{1,0:T(8,128)S(1)} %get-tuple-element.13.weighted_ref), custom_call_target="tpu_custom_call" | custom-call | tf_op jit(solution)/shard_map/update/pallas_call | solution.py:161
  (1 shorter events, 0.0 us)
Async XLA Ops:
  0.6 24.4 %copy-start = (bf16[192,128,128]{2,1,0:T(8,128)(2,1)S(1)}, bf16[192,128,128]{2,1,0:T(8,128)(2,1)}, u32[]{:S(2)}) copy-start(bf16[192,128,128]{2,1,0:T(8,128)(2,1)} %foot_ref.5) | copy-start | bytes 18874372
  0.6 24.4 %copy-start.3 = (s32[192]{0:T(256)S(1)}, s32[192]{0:T(256)}, u32[]{:S(2)}) copy-start(s32[192]{0:T(256)} %voxel_ref.5) | copy-start | bytes 2308
  0.7 24.3 %copy-start.4 = (s32[192]{0:T(256)S(1)}, s32[192]{0:T(256)}, u32[]{:S(2)}) copy-start(s32[192]{0:T(256)} %rows_ref.3) | copy-start | bytes 2308
  0.7 24.3 %copy-start.5 = (s32[192]{0:T(256)S(1)}, s32[192]{0:T(256)}, u32[]{:S(2)}) copy-start(s32[192]{0:T(256)} %tile_ref.3) | copy-start | bytes 2308
  25.0 12.8 %copy-start.2 = (f32[64,128]{1,0:T(8,128)S(1)}, f32[64,128]{1,0:T(8,128)}, u32[]{:S(2)}) copy-start(f32[64,128]{1,0:T(8,128)} %measured_ref.1) | copy-start | bytes 98308
  26.9 1.3 %collective-permute-start = (f32[128,128]{1,0:T(8,128)S(1)}, f32[128,128]{1,0:T(8,128)S(1)}, u32[]{:S(2)}, u32[]{:S(2)}) collective-permute-start(f32[128,128]{1,0:T(8,128)S(1)} %forward.1), channel_id=1, source_target_pairs={{0,32},{32,0},{64,96},{96,64},{128,160},{160,128},{192,224},{224,1... | collective-permute-start | bytes 196616 | tf_op jit(solution)/shard_map/ppermute | solution.py:189
  28.2 26.9 %copy-start.1 = (f32[32,128]{1,0:T(8,128)S(1)}, f32[32,128]{1,0:T(8,128)}, u32[]{:S(2)}) copy-start(f32[32,128]{1,0:T(8,128)} %volume_ref.1) | copy-start | bytes 49156
  28.3 6.4 %collective-permute-start.3 = (f32[128,128]{1,0:T(8,128)S(1)}, f32[128,128]{1,0:T(8,128)S(1)}, u32[]{:S(2)}, u32[]{:S(2)}) collective-permute-start(f32[128,128]{1,0:T(8,128)S(1)} %add.3.mine_ref), channel_id=1, source_target_pairs={{0,192},{32,224},{64,0},{96,32},{128,64},{160,96},{192,128},{224,1... | collective-permute-start | bytes 196616 | tf_op jit(solution)/shard_map/ppermute | solution.py:191
  31.3 6.5 %collective-permute-start.2 = (f32[128,128]{1,0:T(8,128)S(1)}, f32[128,128]{1,0:T(8,128)S(1)}, u32[]{:S(2)}, u32[]{:S(2)}) collective-permute-start(f32[128,128]{1,0:T(8,128)S(1)} %add.3.mine_ref), channel_id=1, source_target_pairs={{0,64},{32,96},{64,128},{96,160},{128,192},{160,224},{192,0},{224,... | collective-permute-start | bytes 196616 | tf_op jit(solution)/shard_map/ppermute | solution.py:191
  31.3 6.5 %collective-permute-start.1 = (f32[128,128]{1,0:T(8,128)S(1)}, f32[128,128]{1,0:T(8,128)S(1)}, u32[]{:S(2)}, u32[]{:S(2)}) collective-permute-start(f32[128,128]{1,0:T(8,128)S(1)} %add.3.mine_ref), channel_id=1, source_target_pairs={{0,128},{32,160},{64,192},{96,224},{128,0},{160,32},{192,64},{224,... | collective-permute-start | bytes 196616 | tf_op jit(solution)/shard_map/ppermute | solution.py:191

commit v7 on v6

--- a/solution.py
+++ b/solution.py
@@ -16,7 +16,6 @@
 F32 = jnp.float32
 BF16 = jnp.bfloat16
 VMEM = pl.BlockSpec(memory_space=pltpu.VMEM)
-SMEM = pl.BlockSpec(memory_space=pltpu.SMEM)
 HBM = pl.BlockSpec(memory_space=pltpu.HBM)
 PARAMS = pltpu.CompilerParams(vmem_limit_bytes=40 * 1024 * 1024)
 ROWS = ((1,), (0,))
@@ -117,7 +116,9 @@
     sums_ref[...], codes_ref[...] = quantize(per_slot(live, foot_ref), place + 32)
 
 
-def backward_kernel(voxel_ref, mine_ref, across_ref, left_ref, right_ref, measured_ref, tile_ref, live_ref, place_ref, sums_ref, codes_ref, foot_ref, weighted_ref, send_ref):
+def backward_kernel(voxel_any, mine_ref, across_ref, left_ref, right_ref, measured_ref, tile_ref, live_ref, place_ref, sums_ref, codes_ref, foot_ref, weighted_ref, send_ref, voxel_ref, sem):
+    voxel_copy = pltpu.make_async_copy(voxel_any, voxel_ref, sem)
+    voxel_copy.start()
     total = (mine_ref[...] + across_ref[...]) + (left_ref[...] + right_ref[...])
     weighted = (measured_ref[...] - total[:64]) / jnp.maximum(total[64:], 1.0)
     weighted_ref[...] = weighted
@@ -129,6 +130,7 @@
     mine = iota((LINES, BLK), 1) == (first + line) & (BLK - 1)
     spot = iota((8, BLK), 0) * BLK + iota((8, BLK), 1) - first
     spot = (spot >= 0) & (spot < LINES)
+    voxel_copy.wait()
     for j in range(NB // CAP):
         at = slice(CAP * j, CAP * (j + 1))
         code = jnp.concatenate([codes[at], codes_ref[at]], axis=0)
@@ -201,8 +203,9 @@
         backward_kernel,
         "backward",
         [((64, BLK), F32), ((SHARES, 32, BLK), jnp.int16)],
-        [SMEM] + [VMEM] * 11,
+        [VMEM] * 12,
         block_voxel, part, across, left, right, measured, block_tile, live, place, column_sums, column_codes, footprint,
+        scratch=[pltpu.SMEM((NB,), jnp.int32), pltpu.SemaphoreType.DMA],
     )
     received = lax.all_to_all(send_back, "angle", 0, 0)
     return call(

time: 56.5 us -> 56.1 us (level)
  no operation moved by 1% of the time
where the time goes in v7:
time: 56.1 us; the launch traced here: 55.6 us
  blocking collectives  38.9 us (69%)
  Pallas kernels  6.04 us (11%)
  starting transfers between devices  5.39 us (10%)
  waiting for transfers between devices  4.42 us (8%)
  between operations  0.74 us (1%)
    all_to_all x1, blocking collectives, on_device(): slab_values = lax.all_to_all(offer, 'angle', 0, 0)  23.4 us
    all_to_all x1, blocking collectives, on_device(): received = lax.all_to_all(send_back, 'angle', 0, 0)  15.5 us
    pallas_call x5, Pallas kernels, call(): pl.pallas_call(kernel, out_shape=out, in_specs=specs, out_specs=[VMEM] *...  6.04 us
    ppermute x3, starting transfers between devices, on_device(): lax.ppermute(part, 'slab', [(i, (i + 2 * k) % 8) for i in range(8)])  5.3 us
    ppermute x3, waiting for transfers between devices, on_device(): lax.ppermute(part, 'slab', [(i, (i + 2 * k) % 8) for i in range(8)])  3.17 us
    ppermute x1, waiting for transfers between devices, on_device(): part = part + lax.ppermute(part, 'slab', [(i, i ^ 1) for i in range(8)])  1.24 us
  transfers between devices with their start and end apart: 4, of which 2 were waited for; matrix products, arithmetic and copies ran while one was open for 0% of the time, Pallas kernels for 2%

profile of v7, /device:TPU:32, one launch (start us, length us, event | category | flops | bytes accessed | tf_op | source)
XLA Modules:
  0.0 55.6 jit_solution(11983958912261306291)
XLA Ops:
  0.6 0.0 copy-start
  0.6 0.0 copy-start.3
  0.7 0.0 copy-start.4
  0.7 0.0 copy-start.5
  0.7 0.9 %offer.1 = bf16[32,32,128]{2,1,0:T(8,128)(2,1)S(1)} custom-call(f32[32,128]{1,0:T(8,128)} %volume_ref.1, bf16[192,128,128]{2,1,0:T(8,128)(2,1)} %foot_ref.5), custom_call_target="tpu_custom_call" | custom-call | tf_op jit(solution)/shard_map/offer/pallas_call | solution.py:163
  1.6 23.4 %all_to_all.10.slab_ref = bf16[32,32,128]{2,1,0:T(8,128)(2,1)S(1)} all-to-all(bf16[32,32,128]{2,1,0:T(8,128)(2,1)S(1)} %offer.1), channel_id=1, replica_groups=mesh['slab'=8,'angle'=32] {'angle'}, dimensions={0} | all-to-all | bytes 524288 | tf_op jit(solution)/shard_map/all_to_all | solution.py:183
  25.0 0.0 copy-done
  25.0 0.0 copy-done.3
  25.0 0.0 copy-done.4
  25.0 0.0 copy-done.5
  25.0 0.0 copy-start.2
  25.0 1.9 %forward.1 = f32[128,128]{1,0:T(8,128)S(1)} custom-call(bf16[32,32,128]{2,1,0:T(8,128)(2,1)S(1)} %all_to_all.10.slab_ref, s32[192]{0:T(256)S(1)} %copy-done.3, s32[192]{0:T(256)S(1)} %copy-done.5, s32[192]{0:T(256)S(1)} %copy-done.4, bf16[192,128,128]{2,1,0:T(8,128)(2,1)S(1)} %copy-done), custom_call_target="tpu_custom_call" | custom-call | tf_op jit(solution)/shard_map/forward/pallas_call | solution.py:163
  26.9 0.1 collective-permute-start
  27.0 1.2 %collective-permute-done = f32[128,128]{1,0:T(8,128)S(1)} collective-permute-done((f32[128,128]{1,0:T(8,128)S(1)}, f32[128,128]{1,0:T(8,128)S(1)}, u32[]{:S(2)}, u32[]{:S(2)}) %collective-permute-start) | collective-permute-done | bytes 65568 | tf_op jit(solution)/shard_map/ppermute | solution.py:191
  28.2 0.0 copy-start.1
  28.3 3.1 %collective-permute-start.3 = (f32[128,128]{1,0:T(8,128)S(1)}, f32[128,128]{1,0:T(8,128)S(1)}, u32[]{:S(2)}, u32[]{:S(2)}) collective-permute-start(f32[128,128]{1,0:T(8,128)S(1)} %add.3.mine_ref), channel_id=1, source_target_pairs={{0,192},{32,224},{64,0},{96,32},{128,64},{160,96},{192,128},{224,1... | collective-permute-start | bytes 196616 | tf_op jit(solution)/shard_map/ppermute | solution.py:193
  31.3 0.0 collective-permute-start.2
  31.3 2.2 %collective-permute-start.1 = (f32[128,128]{1,0:T(8,128)S(1)}, f32[128,128]{1,0:T(8,128)S(1)}, u32[]{:S(2)}, u32[]{:S(2)}) collective-permute-start(f32[128,128]{1,0:T(8,128)S(1)} %add.3.mine_ref), channel_id=1, source_target_pairs={{0,128},{32,160},{64,192},{96,224},{128,0},{160,32},{192,64},{224,... | collective-permute-start | bytes 196616 | tf_op jit(solution)/shard_map/ppermute | solution.py:193
  33.6 1.1 %columns.1 = (f32[192,128]{1,0:T(8,128)S(1)}, s32[192,128]{1,0:T(8,128)S(1)}, s32[192,128]{1,0:T(8,128)S(1)}, s32[192,128]{1,0:T(8,128)S(1)}) custom-call(s32[192]{0:T(256)S(1)} %copy-done.3, s32[192]{0:T(256)S(1)} %copy-done.4, bf16[192,128,128]{2,1,0:T(8,128)(2,1)S(1)} %copy-done), custom_call_target="tpu_custom_call" | custom-call | tf_op jit(solution)/shard_map/columns/pallas_call | solution.py:163
  34.7 0.0 collective-permute-done.3.right_ref
  34.7 3.2 %collective-permute-done.2.left_ref = f32[128,128]{1,0:T(8,128)S(1)} collective-permute-done((f32[128,128]{1,0:T(8,128)S(1)}, f32[128,128]{1,0:T(8,128)S(1)}, u32[]{:S(2)}, u32[]{:S(2)}) %collective-permute-start.2) | collective-permute-done | bytes 65568 | tf_op jit(solution)/shard_map/ppermute | solution.py:193
  37.8 0.0 collective-permute-done.1.across_ref
  37.8 0.0 copy-done.2
  37.8 1.3 %backward.1 = (f32[64,128]{1,0:T(8,128)S(1)}, s16[32,32,128]{2,1,0:T(8,128)(2,1)S(1)}) custom-call(s32[192]{0:T(256)S(1)} %copy-done.3, f32[128,128]{1,0:T(8,128)S(1)} %add.3.mine_ref, f32[128,128]{1,0:T(8,128)S(1)} %collective-permute-done.1.across_ref, f32[128,128]{1,0:T(8,128)S(1)} %collective-permute-done.2.left_ref, ...), custom_call_target="tpu_custom_call" | custom-call | tf_op jit(solution)/shard_map/backward/pallas_call | solution.py:163
  39.1 15.5 %all_to_all.11.recv_ref = s16[32,32,128]{2,1,0:T(8,128)(2,1)S(1)} all-to-all(s16[32,32,128]{2,1,0:T(8,128)(2,1)S(1)} %get-tuple-element.12), channel_id=1, replica_groups=mesh['slab'=8,'angle'=32] {'angle'}, dimensions={0} | all-to-all | bytes 524288 | tf_op jit(solution)/shard_map/all_to_all | solution.py:210
  54.7 0.0 copy-done.1
  54.7 0.9 %update.1 = (f32[32,128]{1,0:T(8,128)}, f32[64,128]{1,0:T(8,128)}) custom-call(s16[32,32,128]{2,1,0:T(8,128)(2,1)S(1)} %all_to_all.11.recv_ref, f32[32,128]{1,0:T(8,128)S(1)} %copy-done.1, f32[64,128]{1,0:T(8,128)S(1)} %get-tuple-element.13.weighted_ref), custom_call_target="tpu_custom_call" | custom-call | tf_op jit(solution)/shard_map/update/pallas_call | solution.py:163
  (1 shorter events, 0.0 us)
Async XLA Ops:
  0.6 24.4 %copy-start = (bf16[192,128,128]{2,1,0:T(8,128)(2,1)S(1)}, bf16[192,128,128]{2,1,0:T(8,128)(2,1)}, u32[]{:S(2)}) copy-start(bf16[192,128,128]{2,1,0:T(8,128)(2,1)} %foot_ref.5) | copy-start | bytes 18874372
  0.6 24.4 %copy-start.3 = (s32[192]{0:T(256)S(1)}, s32[192]{0:T(256)}, u32[]{:S(2)}) copy-start(s32[192]{0:T(256)} %voxel_any.1) | copy-start | bytes 2308
  0.7 24.3 %copy-start.4 = (s32[192]{0:T(256)S(1)}, s32[192]{0:T(256)}, u32[]{:S(2)}) copy-start(s32[192]{0:T(256)} %rows_ref.3) | copy-start | bytes 2308
  0.7 24.3 %copy-start.5 = (s32[192]{0:T(256)S(1)}, s32[192]{0:T(256)}, u32[]{:S(2)}) copy-start(s32[192]{0:T(256)} %tile_ref.3) | copy-start | bytes 2308
  25.0 12.8 %copy-start.2 = (f32[64,128]{1,0:T(8,128)S(1)}, f32[64,128]{1,0:T(8,128)}, u32[]{:S(2)}) copy-start(f32[64,128]{1,0:T(8,128)} %measured_ref.1) | copy-start | bytes 98308
  26.9 1.3 %collective-permute-start = (f32[128,128]{1,0:T(8,128)S(1)}, f32[128,128]{1,0:T(8,128)S(1)}, u32[]{:S(2)}, u32[]{:S(2)}) collective-permute-start(f32[128,128]{1,0:T(8,128)S(1)} %forward.1), channel_id=1, source_target_pairs={{0,32},{32,0},{64,96},{96,64},{128,160},{160,128},{192,224},{224,1... | collective-permute-start | bytes 196616 | tf_op jit(solution)/shard_map/ppermute | solution.py:191
  28.2 26.4 %copy-start.1 = (f32[32,128]{1,0:T(8,128)S(1)}, f32[32,128]{1,0:T(8,128)}, u32[]{:S(2)}) copy-start(f32[32,128]{1,0:T(8,128)} %volume_ref.1) | copy-start | bytes 49156
  28.3 6.4 %collective-permute-start.3 = (f32[128,128]{1,0:T(8,128)S(1)}, f32[128,128]{1,0:T(8,128)S(1)}, u32[]{:S(2)}, u32[]{:S(2)}) collective-permute-start(f32[128,128]{1,0:T(8,128)S(1)} %add.3.mine_ref), channel_id=1, source_target_pairs={{0,192},{32,224},{64,0},{96,32},{128,64},{160,96},{192,128},{224,1... | collective-permute-start | bytes 196616 | tf_op jit(solution)/shard_map/ppermute | solution.py:193
  31.3 6.5 %collective-permute-start.2 = (f32[128,128]{1,0:T(8,128)S(1)}, f32[128,128]{1,0:T(8,128)S(1)}, u32[]{:S(2)}, u32[]{:S(2)}) collective-permute-start(f32[128,128]{1,0:T(8,128)S(1)} %add.3.mine_ref), channel_id=1, source_target_pairs={{0,64},{32,96},{64,128},{96,160},{128,192},{160,224},{192,0},{224,... | collective-permute-start | bytes 196616 | tf_op jit(solution)/shard_map/ppermute | solution.py:193
  31.3 6.5 %collective-permute-start.1 = (f32[128,128]{1,0:T(8,128)S(1)}, f32[128,128]{1,0:T(8,128)S(1)}, u32[]{:S(2)}, u32[]{:S(2)}) collective-permute-start(f32[128,128]{1,0:T(8,128)S(1)} %add.3.mine_ref), channel_id=1, source_target_pairs={{0,128},{32,160},{64,192},{96,224},{128,0},{160,32},{192,64},{224,... | collective-permute-start | bytes 196616 | tf_op jit(solution)/shard_map/ppermute | solution.py:193

commit v8 on v7

--- a/solution.py
+++ b/solution.py
@@ -116,7 +116,7 @@
     sums_ref[...], codes_ref[...] = quantize(per_slot(live, foot_ref), place + 32)
 
 
-def backward_kernel(voxel_any, mine_ref, across_ref, left_ref, right_ref, measured_ref, tile_ref, live_ref, place_ref, sums_ref, codes_ref, foot_ref, weighted_ref, send_ref, voxel_ref, sem):
+def backward_kernel(voxel_any, mine_ref, right_ref, left_ref, across_ref, measured_ref, tile_ref, live_ref, place_ref, sums_ref, codes_ref, foot_ref, weighted_ref, send_ref, voxel_ref, sem):
     voxel_copy = pltpu.make_async_copy(voxel_any, voxel_ref, sem)
     voxel_copy.start()
     total = (mine_ref[...] + across_ref[...]) + (left_ref[...] + right_ref[...])
@@ -189,9 +189,9 @@
         slab_values, block_voxel, block_tile, block_rows, footprint,
     )
     part = part + lax.ppermute(part, "slab", [(i, i ^ 1) for i in range(8)])
-    across, left, right = (
-        lax.ppermute(part, "slab", [(i, (i + 2 * k) % 8) for i in range(8)]) for k in (2, 1, 3)
-    )
+    left = lax.ppermute(part, "slab", [(i, i ^ 2) for i in range(8)])
+    right = lax.ppermute(part, "slab", [(i, 6 - i + 2 * (i % 2)) for i in range(8)])
+    across = lax.ppermute(part, "slab", [(i, i ^ 4) for i in range(8)])
     live, place, column_sums, column_codes = call(
         columns_kernel,
         "columns",
@@ -204,7 +204,7 @@
         "backward",
         [((64, BLK), F32), ((SHARES, 32, BLK), jnp.int16)],
         [VMEM] * 12,
-        block_voxel, part, across, left, right, measured, block_tile, live, place, column_sums, column_codes, footprint,
+        block_voxel, part, right, left, across, measured, block_tile, live, place, column_sums, column_codes, footprint,
         scratch=[pltpu.SMEM((NB,), jnp.int32), pltpu.SemaphoreType.DMA],
     )
     received = lax.all_to_all(send_back, "angle", 0, 0)

time: 56.1 us -> 55.6 us (level)
  starting transfers between devices: 5.39 us -> 4.43 us
  waiting for transfers between devices: 4.42 us -> 5.23 us
    ppermute x3, starting transfers between devices: 5.3 us -> 4.34 us  [the longest x1 3.28 us: on_device(): across = lax.ppermute(part, 'slab', [(i, i ^ 4) for i in range(8)])]
    ppermute x3, waiting for transfers between devices: 3.17 us -> 3.99 us  [the longest x1 1.83 us: on_device(): lax.ppermute(part, 'slab', [(i, 6 - i + 2 * (i % 2)) for i in range(8)])]
  transfers between devices with their start and end apart: 4 -> 4, of which waited for: 2 -> 4; matrix products, arithmetic and copies ran while one was open for 0% -> 0% of each run, Pallas kernels for 2% -> 2%
where the time goes in v8:
time: 55.6 us; the launch traced here: 55.1 us
  blocking collectives  38.6 us (69%)
  Pallas kernels  6.04 us (11%)
  waiting for transfers between devices  5.23 us (9%)
  starting transfers between devices  4.43 us (8%)
  between operations  0.73 us (1%)
    all_to_all x1, blocking collectives, on_device(): slab_values = lax.all_to_all(offer, 'angle', 0, 0)  23.4 us
    all_to_all x1, blocking collectives, on_device(): received = lax.all_to_all(send_back, 'angle', 0, 0)  15.2 us
    pallas_call x5, Pallas kernels, call(): pl.pallas_call(kernel, out_shape=out, in_specs=specs, out_specs=[VMEM] *...  6.04 us
    ppermute x1, starting transfers between devices, on_device(): across = lax.ppermute(part, 'slab', [(i, i ^ 4) for i in range(8)])  3.28 us
    ppermute x1, waiting for transfers between devices, on_device(): lax.ppermute(part, 'slab', [(i, 6 - i + 2 * (i % 2)) for i in range(8)])  1.83 us
    ppermute x1, waiting for transfers between devices, on_device(): left = lax.ppermute(part, 'slab', [(i, i ^ 2) for i in range(8)])  1.75 us
    ppermute x1, waiting for transfers between devices, on_device(): part = part + lax.ppermute(part, 'slab', [(i, i ^ 1) for i in range(8)])  1.24 us
  transfers between devices with their start and end apart: 4, of which 4 were waited for; matrix products, arithmetic and copies ran while one was open for 0% of the time, Pallas kernels for 2%

profile of v8, /device:TPU:32, one launch (start us, length us, event | category | flops | bytes accessed | tf_op | source)
XLA Modules:
  0.0 55.1 jit_solution(4700209229437304859)
XLA Ops:
  0.6 0.0 copy-start
  0.6 0.0 copy-start.3
  0.7 0.0 copy-start.4
  0.7 0.0 copy-start.5
  0.7 0.9 %offer.1 = bf16[32,32,128]{2,1,0:T(8,128)(2,1)S(1)} custom-call(f32[32,128]{1,0:T(8,128)} %volume_ref.1, bf16[192,128,128]{2,1,0:T(8,128)(2,1)} %foot_ref.5), custom_call_target="tpu_custom_call" | custom-call | tf_op jit(solution)/shard_map/offer/pallas_call | solution.py:163
  1.6 23.4 %all_to_all.10.slab_ref = bf16[32,32,128]{2,1,0:T(8,128)(2,1)S(1)} all-to-all(bf16[32,32,128]{2,1,0:T(8,128)(2,1)S(1)} %offer.1), channel_id=1, replica_groups=mesh['slab'=8,'angle'=32] {'angle'}, dimensions={0} | all-to-all | bytes 524288 | tf_op jit(solution)/shard_map/all_to_all | solution.py:183
  25.0 0.0 copy-done
  25.0 0.0 copy-done.3
  25.0 0.0 copy-done.4
  25.0 0.0 copy-done.5
  25.0 0.0 copy-start.2
  25.0 1.9 %forward.1 = f32[128,128]{1,0:T(8,128)S(1)} custom-call(bf16[32,32,128]{2,1,0:T(8,128)(2,1)S(1)} %all_to_all.10.slab_ref, s32[192]{0:T(256)S(1)} %copy-done.3, s32[192]{0:T(256)S(1)} %copy-done.5, s32[192]{0:T(256)S(1)} %copy-done.4, bf16[192,128,128]{2,1,0:T(8,128)(2,1)S(1)} %copy-done), custom_call_target="tpu_custom_call" | custom-call | tf_op jit(solution)/shard_map/forward/pallas_call | solution.py:163
  26.9 0.1 collective-permute-start
  27.0 1.2 %collective-permute-done = f32[128,128]{1,0:T(8,128)S(1)} collective-permute-done((f32[128,128]{1,0:T(8,128)S(1)}, f32[128,128]{1,0:T(8,128)S(1)}, u32[]{:S(2)}, u32[]{:S(2)}) %collective-permute-start) | collective-permute-done | bytes 65568 | tf_op jit(solution)/shard_map/ppermute | solution.py:191
  28.2 0.0 copy-start.1
  28.3 3.3 %collective-permute-start.3 = (f32[128,128]{1,0:T(8,128)S(1)}, f32[128,128]{1,0:T(8,128)S(1)}, u32[]{:S(2)}, u32[]{:S(2)}) collective-permute-start(f32[128,128]{1,0:T(8,128)S(1)} %add.3.mine_ref), channel_id=1, source_target_pairs={{0,128},{32,160},{64,192},{96,224},{128,0},{160,32},{192,64},{224,... | collective-permute-start | bytes 196616 | tf_op jit(solution)/shard_map/ppermute | solution.py:194
  31.5 0.7 %collective-permute-start.2 = (f32[128,128]{1,0:T(8,128)S(1)}, f32[128,128]{1,0:T(8,128)S(1)}, u32[]{:S(2)}, u32[]{:S(2)}) collective-permute-start(f32[128,128]{1,0:T(8,128)S(1)} %add.3.mine_ref), channel_id=1, source_target_pairs={{0,64},{32,96},{64,0},{96,32},{128,192},{160,224},{192,128},{224,1... | collective-permute-start | bytes 196616 | tf_op jit(solution)/shard_map/ppermute | solution.py:192
  32.2 0.4 collective-permute-start.1
  32.6 1.1 %columns.1 = (f32[192,128]{1,0:T(8,128)S(1)}, s32[192,128]{1,0:T(8,128)S(1)}, s32[192,128]{1,0:T(8,128)S(1)}, s32[192,128]{1,0:T(8,128)S(1)}) custom-call(s32[192]{0:T(256)S(1)} %copy-done.3, s32[192]{0:T(256)S(1)} %copy-done.4, bf16[192,128,128]{2,1,0:T(8,128)(2,1)S(1)} %copy-done), custom_call_target="tpu_custom_call" | custom-call | tf_op jit(solution)/shard_map/columns/pallas_call | solution.py:163
  33.7 0.4 collective-permute-done.3.across_ref
  34.1 1.7 %collective-permute-done.2.left_ref = f32[128,128]{1,0:T(8,128)S(1)} collective-permute-done((f32[128,128]{1,0:T(8,128)S(1)}, f32[128,128]{1,0:T(8,128)S(1)}, u32[]{:S(2)}, u32[]{:S(2)}) %collective-permute-start.2) | collective-permute-done | bytes 65568 | tf_op jit(solution)/shard_map/ppermute | solution.py:192
  35.9 1.8 %collective-permute-done.1.right_ref = f32[128,128]{1,0:T(8,128)S(1)} collective-permute-done((f32[128,128]{1,0:T(8,128)S(1)}, f32[128,128]{1,0:T(8,128)S(1)}, u32[]{:S(2)}, u32[]{:S(2)}) %collective-permute-start.1) | collective-permute-done | bytes 65568 | tf_op jit(solution)/shard_map/ppermute | solution.py:193
  37.7 0.0 copy-done.2
  37.7 1.3 %backward.1 = (f32[64,128]{1,0:T(8,128)S(1)}, s16[32,32,128]{2,1,0:T(8,128)(2,1)S(1)}) custom-call(s32[192]{0:T(256)S(1)} %copy-done.3, f32[128,128]{1,0:T(8,128)S(1)} %add.3.mine_ref, f32[128,128]{1,0:T(8,128)S(1)} %collective-permute-done.1.right_ref, f32[128,128]{1,0:T(8,128)S(1)} %collective-permute-done.2.left_ref, ...), custom_call_target="tpu_custom_call" | custom-call | tf_op jit(solution)/shard_map/backward/pallas_call | solution.py:163
  39.0 15.2 %all_to_all.11.recv_ref = s16[32,32,128]{2,1,0:T(8,128)(2,1)S(1)} all-to-all(s16[32,32,128]{2,1,0:T(8,128)(2,1)S(1)} %get-tuple-element.12), channel_id=1, replica_groups=mesh['slab'=8,'angle'=32] {'angle'}, dimensions={0} | all-to-all | bytes 524288 | tf_op jit(solution)/shard_map/all_to_all | solution.py:210
  54.2 0.0 copy-done.1
  54.2 0.9 %update.1 = (f32[32,128]{1,0:T(8,128)}, f32[64,128]{1,0:T(8,128)}) custom-call(s16[32,32,128]{2,1,0:T(8,128)(2,1)S(1)} %all_to_all.11.recv_ref, f32[32,128]{1,0:T(8,128)S(1)} %copy-done.1, f32[64,128]{1,0:T(8,128)S(1)} %get-tuple-element.13.weighted_ref), custom_call_target="tpu_custom_call" | custom-call | tf_op jit(solution)/shard_map/update/pallas_call | solution.py:163
  (1 shorter events, 0.0 us)
Async XLA Ops:
  0.6 24.4 %copy-start = (bf16[192,128,128]{2,1,0:T(8,128)(2,1)S(1)}, bf16[192,128,128]{2,1,0:T(8,128)(2,1)}, u32[]{:S(2)}) copy-start(bf16[192,128,128]{2,1,0:T(8,128)(2,1)} %foot_ref.5) | copy-start | bytes 18874372
  0.6 24.4 %copy-start.3 = (s32[192]{0:T(256)S(1)}, s32[192]{0:T(256)}, u32[]{:S(2)}) copy-start(s32[192]{0:T(256)} %voxel_any.1) | copy-start | bytes 2308
  0.7 24.3 %copy-start.4 = (s32[192]{0:T(256)S(1)}, s32[192]{0:T(256)}, u32[]{:S(2)}) copy-start(s32[192]{0:T(256)} %rows_ref.3) | copy-start | bytes 2308
  0.7 24.3 %copy-start.5 = (s32[192]{0:T(256)S(1)}, s32[192]{0:T(256)}, u32[]{:S(2)}) copy-start(s32[192]{0:T(256)} %tile_ref.3) | copy-start | bytes 2308
  25.0 12.7 %copy-start.2 = (f32[64,128]{1,0:T(8,128)S(1)}, f32[64,128]{1,0:T(8,128)}, u32[]{:S(2)}) copy-start(f32[64,128]{1,0:T(8,128)} %measured_ref.1) | copy-start | bytes 98308
  26.9 1.3 %collective-permute-start = (f32[128,128]{1,0:T(8,128)S(1)}, f32[128,128]{1,0:T(8,128)S(1)}, u32[]{:S(2)}, u32[]{:S(2)}) collective-permute-start(f32[128,128]{1,0:T(8,128)S(1)} %forward.1), channel_id=1, source_target_pairs={{0,32},{32,0},{64,96},{96,64},{128,160},{160,128},{192,224},{224,1... | collective-permute-start | bytes 196616 | tf_op jit(solution)/shard_map/ppermute | solution.py:191
  28.2 26.0 %copy-start.1 = (f32[32,128]{1,0:T(8,128)S(1)}, f32[32,128]{1,0:T(8,128)}, u32[]{:S(2)}) copy-start(f32[32,128]{1,0:T(8,128)} %volume_ref.1) | copy-start | bytes 49156
  28.3 5.9 %collective-permute-start.3 = (f32[128,128]{1,0:T(8,128)S(1)}, f32[128,128]{1,0:T(8,128)S(1)}, u32[]{:S(2)}, u32[]{:S(2)}) collective-permute-start(f32[128,128]{1,0:T(8,128)S(1)} %add.3.mine_ref), channel_id=1, source_target_pairs={{0,128},{32,160},{64,192},{96,224},{128,0},{160,32},{192,64},{224,... | collective-permute-start | bytes 196616 | tf_op jit(solution)/shard_map/ppermute | solution.py:194
  31.5 4.3 %collective-permute-start.2 = (f32[128,128]{1,0:T(8,128)S(1)}, f32[128,128]{1,0:T(8,128)S(1)}, u32[]{:S(2)}, u32[]{:S(2)}) collective-permute-start(f32[128,128]{1,0:T(8,128)S(1)} %add.3.mine_ref), channel_id=1, source_target_pairs={{0,64},{32,96},{64,0},{96,32},{128,192},{160,224},{192,128},{224,1... | collective-permute-start | bytes 196616 | tf_op jit(solution)/shard_map/ppermute | solution.py:192
  32.2 5.5 %collective-permute-start.1 = (f32[128,128]{1,0:T(8,128)S(1)}, f32[128,128]{1,0:T(8,128)S(1)}, u32[]{:S(2)}, u32[]{:S(2)}) collective-permute-start(f32[128,128]{1,0:T(8,128)S(1)} %add.3.mine_ref), channel_id=1, source_target_pairs={{0,192},{32,224},{64,128},{96,160},{128,64},{160,96},{192,0},{224,... | collective-permute-start | bytes 196616 | tf_op jit(solution)/shard_map/ppermute | solution.py:193

commit v9 on v8

--- a/solution.py
+++ b/solution.py
@@ -116,7 +116,7 @@
     sums_ref[...], codes_ref[...] = quantize(per_slot(live, foot_ref), place + 32)
 
 
-def backward_kernel(voxel_any, mine_ref, right_ref, left_ref, across_ref, measured_ref, tile_ref, live_ref, place_ref, sums_ref, codes_ref, foot_ref, weighted_ref, send_ref, voxel_ref, sem):
+def backward_kernel(voxel_any, mine_ref, left_ref, right_ref, across_ref, measured_ref, tile_ref, live_ref, place_ref, sums_ref, codes_ref, foot_ref, weighted_ref, send_ref, voxel_ref, sem):
     voxel_copy = pltpu.make_async_copy(voxel_any, voxel_ref, sem)
     voxel_copy.start()
     total = (mine_ref[...] + across_ref[...]) + (left_ref[...] + right_ref[...])
@@ -141,7 +141,8 @@
 
 def update_kernel(recv_ref, volume_ref, weighted_ref, out_ref, weighted_out_ref):
     weighted_out_ref[...] = weighted_ref[...]
-    codes = jnp.sum(recv_ref[:, LINES:, :].astype(jnp.int32), axis=0)
+    received = recv_ref[...].astype(jnp.int32)
+    codes = jnp.sum(received[:, LINES:, :], axis=0)
     scale = power(lax.shift_right_logical(codes, 7)) * 2.0**-28
     place = (codes & 127) - 1
     wanted = iota((2 * 32, BLK), 0)
@@ -152,7 +153,7 @@
         ],
         axis=1,
     ).astype(BF16)
-    values = recv_ref[:, :LINES, :].astype(F32).reshape(SHARES * LINES, BLK)
+    values = received[:, :LINES, :].astype(F32).reshape(SHARES * LINES, BLK)
     high = jnp.floor(values * (1.0 / 256.0)) * 256.0
     summed = dot(hot, high.astype(BF16)) + dot(hot, (values - high).astype(BF16))
     out_ref[...] = volume_ref[...] + summed[:32] / jnp.maximum(summed[32:], 1.0)
@@ -204,7 +205,7 @@
         "backward",
         [((64, BLK), F32), ((SHARES, 32, BLK), jnp.int16)],
         [VMEM] * 12,
-        block_voxel, part, right, left, across, measured, block_tile, live, place, column_sums, column_codes, footprint,
+        block_voxel, part, left, right, across, measured, block_tile, live, place, column_sums, column_codes, footprint,
         scratch=[pltpu.SMEM((NB,), jnp.int32), pltpu.SemaphoreType.DMA],
     )
     received = lax.all_to_all(send_back, "angle", 0, 0)

time: 55.6 us -> 55.3 us (level)
  waiting for transfers between devices: 5.23 us -> 4.56 us
    ppermute x1, waiting for transfers between devices: 1.75 us -> 0.01 us  [on_device(): left = lax.ppermute(part, 'slab', [(i, i ^ 2) for i in range(8)])]
    ppermute x1, waiting for transfers between devices: 1.83 us -> 2.9 us  [on_device(): lax.ppermute(part, 'slab', [(i, 6 - i + 2 * (i % 2)) for i in range(8)])]
    ppermute x1, starting transfers between devices: 0.68 us -> 0.01 us  [on_device(): left = lax.ppermute(part, 'slab', [(i, i ^ 2) for i in range(8)])]
    ppermute x1, starting transfers between devices: 0.38 us -> 1.06 us  [on_device(): lax.ppermute(part, 'slab', [(i, 6 - i + 2 * (i % 2)) for i in range(8)])]
  transfers between devices with their start and end apart: 4 -> 4, of which waited for: 4 -> 3; matrix products, arithmetic and copies ran while one was open for 0% -> 0% of each run, Pallas kernels for 2% -> 2%
where the time goes in v9:
time: 55.3 us; the launch traced here: 54.6 us
  blocking collectives  38.8 us (70%)
  Pallas kernels  6.04 us (11%)
  waiting for transfers between devices  4.56 us (8%)
  starting transfers between devices  4.43 us (8%)
  between operations  0.73 us (1%)
    all_to_all x1, blocking collectives, on_device(): slab_values = lax.all_to_all(offer, 'angle', 0, 0)  23.4 us
    all_to_all x1, blocking collectives, on_device(): received = lax.all_to_all(send_back, 'angle', 0, 0)  15.4 us
    pallas_call x5, Pallas kernels, call(): pl.pallas_call(kernel, out_shape=out, in_specs=specs, out_specs=[VMEM] *...  6.04 us
    ppermute x1, starting transfers between devices, on_device(): across = lax.ppermute(part, 'slab', [(i, i ^ 4) for i in range(8)])  3.28 us
    ppermute x1, waiting for transfers between devices, on_device(): lax.ppermute(part, 'slab', [(i, 6 - i + 2 * (i % 2)) for i in range(8)])  2.9 us
    ppermute x1, waiting for transfers between devices, on_device(): part = part + lax.ppermute(part, 'slab', [(i, i ^ 1) for i in range(8)])  1.24 us
  transfers between devices with their start and end apart: 4, of which 3 were waited for; matrix products, arithmetic and copies ran while one was open for 0% of the time, Pallas kernels for 2%

profile of v9, /device:TPU:32, one launch (start us, length us, event | category | flops | bytes accessed | tf_op | source)
XLA Modules:
  0.0 54.6 jit_solution(8571375653053467823)
XLA Ops:
  0.6 0.0 copy-start
  0.6 0.0 copy-start.3
  0.7 0.0 copy-start.4
  0.7 0.0 copy-start.5
  0.7 0.9 %offer.1 = bf16[32,32,128]{2,1,0:T(8,128)(2,1)S(1)} custom-call(f32[32,128]{1,0:T(8,128)} %volume_ref.1, bf16[192,128,128]{2,1,0:T(8,128)(2,1)} %foot_ref.5), custom_call_target="tpu_custom_call" | custom-call | tf_op jit(solution)/shard_map/offer/pallas_call | solution.py:164
  1.6 23.4 %all_to_all.10.slab_ref = bf16[32,32,128]{2,1,0:T(8,128)(2,1)S(1)} all-to-all(bf16[32,32,128]{2,1,0:T(8,128)(2,1)S(1)} %offer.1), channel_id=1, replica_groups=mesh['slab'=8,'angle'=32] {'angle'}, dimensions={0} | all-to-all | bytes 524288 | tf_op jit(solution)/shard_map/all_to_all | solution.py:184
  25.0 0.0 copy-done
  25.0 0.0 copy-done.3
  25.0 0.0 copy-done.4
  25.0 0.0 copy-done.5
  25.0 0.0 copy-start.2
  25.0 1.9 %forward.1 = f32[128,128]{1,0:T(8,128)S(1)} custom-call(bf16[32,32,128]{2,1,0:T(8,128)(2,1)S(1)} %all_to_all.10.slab_ref, s32[192]{0:T(256)S(1)} %copy-done.3, s32[192]{0:T(256)S(1)} %copy-done.5, s32[192]{0:T(256)S(1)} %copy-done.4, bf16[192,128,128]{2,1,0:T(8,128)(2,1)S(1)} %copy-done), custom_call_target="tpu_custom_call" | custom-call | tf_op jit(solution)/shard_map/forward/pallas_call | solution.py:164
  26.9 0.1 collective-permute-start
  27.0 1.2 %collective-permute-done = f32[128,128]{1,0:T(8,128)S(1)} collective-permute-done((f32[128,128]{1,0:T(8,128)S(1)}, f32[128,128]{1,0:T(8,128)S(1)}, u32[]{:S(2)}, u32[]{:S(2)}) %collective-permute-start) | collective-permute-done | bytes 65568 | tf_op jit(solution)/shard_map/ppermute | solution.py:192
  28.2 0.0 copy-start.1
  28.3 3.3 %collective-permute-start.3 = (f32[128,128]{1,0:T(8,128)S(1)}, f32[128,128]{1,0:T(8,128)S(1)}, u32[]{:S(2)}, u32[]{:S(2)}) collective-permute-start(f32[128,128]{1,0:T(8,128)S(1)} %add.3.mine_ref), channel_id=1, source_target_pairs={{0,128},{32,160},{64,192},{96,224},{128,0},{160,32},{192,64},{224,... | collective-permute-start | bytes 196616 | tf_op jit(solution)/shard_map/ppermute | solution.py:195
  31.5 1.1 %collective-permute-start.2 = (f32[128,128]{1,0:T(8,128)S(1)}, f32[128,128]{1,0:T(8,128)S(1)}, u32[]{:S(2)}, u32[]{:S(2)}) collective-permute-start(f32[128,128]{1,0:T(8,128)S(1)} %add.3.mine_ref), channel_id=1, source_target_pairs={{0,192},{32,224},{64,128},{96,160},{128,64},{160,96},{192,0},{224,... | collective-permute-start | bytes 196616 | tf_op jit(solution)/shard_map/ppermute | solution.py:194
  32.6 0.0 collective-permute-start.1
  32.6 1.1 %columns.1 = (f32[192,128]{1,0:T(8,128)S(1)}, s32[192,128]{1,0:T(8,128)S(1)}, s32[192,128]{1,0:T(8,128)S(1)}, s32[192,128]{1,0:T(8,128)S(1)}) custom-call(s32[192]{0:T(256)S(1)} %copy-done.3, s32[192]{0:T(256)S(1)} %copy-done.4, bf16[192,128,128]{2,1,0:T(8,128)(2,1)S(1)} %copy-done), custom_call_target="tpu_custom_call" | custom-call | tf_op jit(solution)/shard_map/columns/pallas_call | solution.py:164
  33.7 0.4 collective-permute-done.3.across_ref
  34.1 2.9 %collective-permute-done.2.right_ref = f32[128,128]{1,0:T(8,128)S(1)} collective-permute-done((f32[128,128]{1,0:T(8,128)S(1)}, f32[128,128]{1,0:T(8,128)S(1)}, u32[]{:S(2)}, u32[]{:S(2)}) %collective-permute-start.2) | collective-permute-done | bytes 65568 | tf_op jit(solution)/shard_map/ppermute | solution.py:194
  37.0 0.0 collective-permute-done.1.left_ref
  37.0 0.0 copy-done.2
  37.0 1.3 %backward.1 = (f32[64,128]{1,0:T(8,128)S(1)}, s16[32,32,128]{2,1,0:T(8,128)(2,1)S(1)}) custom-call(s32[192]{0:T(256)S(1)} %copy-done.3, f32[128,128]{1,0:T(8,128)S(1)} %add.3.mine_ref, f32[128,128]{1,0:T(8,128)S(1)} %collective-permute-done.1.left_ref, f32[128,128]{1,0:T(8,128)S(1)} %collective-permute-done.2.right_ref, ...), custom_call_target="tpu_custom_call" | custom-call | tf_op jit(solution)/shard_map/backward/pallas_call | solution.py:164
  38.3 15.4 %all_to_all.11.recv_ref = s16[32,32,128]{2,1,0:T(8,128)(2,1)S(1)} all-to-all(s16[32,32,128]{2,1,0:T(8,128)(2,1)S(1)} %get-tuple-element.12), channel_id=1, replica_groups=mesh['slab'=8,'angle'=32] {'angle'}, dimensions={0} | all-to-all | bytes 524288 | tf_op jit(solution)/shard_map/all_to_all | solution.py:211
  53.7 0.0 copy-done.1
  53.7 0.9 %update.1 = (f32[32,128]{1,0:T(8,128)}, f32[64,128]{1,0:T(8,128)}) custom-call(s16[32,32,128]{2,1,0:T(8,128)(2,1)S(1)} %all_to_all.11.recv_ref, f32[32,128]{1,0:T(8,128)S(1)} %copy-done.1, f32[64,128]{1,0:T(8,128)S(1)} %get-tuple-element.13.weighted_ref), custom_call_target="tpu_custom_call" | custom-call | tf_op jit(solution)/shard_map/update/pallas_call | solution.py:164
  (1 shorter events, 0.0 us)
Async XLA Ops:
  0.6 24.4 %copy-start = (bf16[192,128,128]{2,1,0:T(8,128)(2,1)S(1)}, bf16[192,128,128]{2,1,0:T(8,128)(2,1)}, u32[]{:S(2)}) copy-start(bf16[192,128,128]{2,1,0:T(8,128)(2,1)} %foot_ref.5) | copy-start | bytes 18874372
  0.6 24.4 %copy-start.3 = (s32[192]{0:T(256)S(1)}, s32[192]{0:T(256)}, u32[]{:S(2)}) copy-start(s32[192]{0:T(256)} %voxel_any.1) | copy-start | bytes 2308
  0.7 24.3 %copy-start.4 = (s32[192]{0:T(256)S(1)}, s32[192]{0:T(256)}, u32[]{:S(2)}) copy-start(s32[192]{0:T(256)} %rows_ref.3) | copy-start | bytes 2308
  0.7 24.3 %copy-start.5 = (s32[192]{0:T(256)S(1)}, s32[192]{0:T(256)}, u32[]{:S(2)}) copy-start(s32[192]{0:T(256)} %tile_ref.3) | copy-start | bytes 2308
  25.0 12.0 %copy-start.2 = (f32[64,128]{1,0:T(8,128)S(1)}, f32[64,128]{1,0:T(8,128)}, u32[]{:S(2)}) copy-start(f32[64,128]{1,0:T(8,128)} %measured_ref.1) | copy-start | bytes 98308
  26.9 1.3 %collective-permute-start = (f32[128,128]{1,0:T(8,128)S(1)}, f32[128,128]{1,0:T(8,128)S(1)}, u32[]{:S(2)}, u32[]{:S(2)}) collective-permute-start(f32[128,128]{1,0:T(8,128)S(1)} %forward.1), channel_id=1, source_target_pairs={{0,32},{32,0},{64,96},{96,64},{128,160},{160,128},{192,224},{224,1... | collective-permute-start | bytes 196616 | tf_op jit(solution)/shard_map/ppermute | solution.py:192
  28.2 25.5 %copy-start.1 = (f32[32,128]{1,0:T(8,128)S(1)}, f32[32,128]{1,0:T(8,128)}, u32[]{:S(2)}) copy-start(f32[32,128]{1,0:T(8,128)} %volume_ref.1) | copy-start | bytes 49156
  28.3 5.9 %collective-permute-start.3 = (f32[128,128]{1,0:T(8,128)S(1)}, f32[128,128]{1,0:T(8,128)S(1)}, u32[]{:S(2)}, u32[]{:S(2)}) collective-permute-start(f32[128,128]{1,0:T(8,128)S(1)} %add.3.mine_ref), channel_id=1, source_target_pairs={{0,128},{32,160},{64,192},{96,224},{128,0},{160,32},{192,64},{224,... | collective-permute-start | bytes 196616 | tf_op jit(solution)/shard_map/ppermute | solution.py:195
  31.5 5.5 %collective-permute-start.2 = (f32[128,128]{1,0:T(8,128)S(1)}, f32[128,128]{1,0:T(8,128)S(1)}, u32[]{:S(2)}, u32[]{:S(2)}) collective-permute-start(f32[128,128]{1,0:T(8,128)S(1)} %add.3.mine_ref), channel_id=1, source_target_pairs={{0,192},{32,224},{64,128},{96,160},{128,64},{160,96},{192,0},{224,... | collective-permute-start | bytes 196616 | tf_op jit(solution)/shard_map/ppermute | solution.py:194
  32.6 4.4 %collective-permute-start.1 = (f32[128,128]{1,0:T(8,128)S(1)}, f32[128,128]{1,0:T(8,128)S(1)}, u32[]{:S(2)}, u32[]{:S(2)}) collective-permute-start(f32[128,128]{1,0:T(8,128)S(1)} %add.3.mine_ref), channel_id=1, source_target_pairs={{0,64},{32,96},{64,0},{96,32},{128,192},{160,224},{192,128},{224,1... | collective-permute-start | bytes 196616 | tf_op jit(solution)/shard_map/ppermute | solution.py:193

commit v10 on v9

--- a/solution.py
+++ b/solution.py
@@ -13,6 +13,7 @@
 TURNED = 128
 SET = NB - TURNED
 LINES = 2 * CAP
+PAD = 16
 F32 = jnp.float32
 BF16 = jnp.bfloat16
 VMEM = pl.BlockSpec(memory_space=pltpu.VMEM)
@@ -108,35 +109,67 @@
     part_ref[...] = jnp.concatenate([first[:, :BLK], first[:, BLK:]], axis=0) + second
 
 
-def columns_kernel(voxel_ref, rows_ref, foot_ref, live_ref, place_ref, sums_ref, codes_ref):
+def padded(x):
+    gap = jnp.zeros((PAD - CAP, x.shape[1]), x.dtype)
+    return jnp.concatenate([y for j in range(NB // CAP) for y in (x[CAP * j : CAP * (j + 1)], gap)], axis=0)
+
+
+def own_lanes(count, start):
+    first = LINES * lax.axis_index("angle") + start
+    line = iota((PAD, BLK), 0)
+    mine = (iota((PAD, BLK), 1) == (first + line) & (BLK - 1)) & (line < count)
+    spot = iota((8, BLK), 0) * BLK + iota((8, BLK), 1) - first
+    return mine, (spot >= 0) & (spot < count)
+
+
+def code_rows(code, mine, spot):
+    code = jnp.sum(jnp.where(mine, code, 0), axis=0, keepdims=True)
+    return jnp.where(spot, jnp.broadcast_to(code, spot.shape), 0)
+
+
+def columns_kernel(voxel_ref, tile_ref, rows_ref, foot_ref, live_ref, place_ref, hot_ref, block_ref):
     live = jnp.where(iota((BLK, NB), 0) < rows_ref[...].reshape(1, NB), 1.0, 0.0).T
-    live_ref[...] = live
-    place = (jnp.broadcast_to(voxel_ref[...].reshape(1, NB), (BLK, NB)) & 31).astype(F32).T.astype(jnp.int32)
+    live_ref[...] = padded(live)
+    turned = lambda ref: jnp.broadcast_to(ref[...].reshape(1, NB), (BLK, NB)).astype(F32).T.astype(jnp.int32)
+    place = padded(turned(voxel_ref) & 31)
     place_ref[...] = place
-    sums_ref[...], codes_ref[...] = quantize(per_slot(live, foot_ref), place + 32)
-
-
-def backward_kernel(voxel_any, mine_ref, left_ref, right_ref, across_ref, measured_ref, tile_ref, live_ref, place_ref, sums_ref, codes_ref, foot_ref, weighted_ref, send_ref, voxel_ref, sem):
+    tile = padded(turned(tile_ref) + 1) - 1
+    hot_ref[...] = jnp.where(tile[:, :64] == iota((PAD * NB // CAP, 64), 1), 1.0, 0.0).astype(BF16)
+    sums, codes = quantize(padded(per_slot(live, foot_ref)), place + 32)
+    mine, spot = own_lanes(CAP, CAP)
+    none = jnp.zeros((CAP, BLK), jnp.int32)
+    for j in range(NB // CAP):
+        at = slice(PAD * j, PAD * (j + 1))
+        code = code_rows(codes[at], mine, spot)
+        block_ref[j] = jnp.concatenate([none, sums[at][:CAP], code], axis=0)
+
+
+def backward_kernel(voxel_any, mine_ref, left_ref, right_ref, across_ref, measured_ref, live_ref, place_ref, hot_ref, block_ref, foot_ref, weighted_ref, send_ref, voxel_ref, sem):
     voxel_copy = pltpu.make_async_copy(voxel_any, voxel_ref, sem)
     voxel_copy.start()
     total = (mine_ref[...] + across_ref[...]) + (left_ref[...] + right_ref[...])
     weighted = (measured_ref[...] - total[:64]) / jnp.maximum(total[64:], 1.0)
     weighted_ref[...] = weighted
-    residual = dot(hot_columns(tile_ref, 64), weighted.astype(BF16), SUBLANES) * live_ref[...]
-    backs, codes = quantize(per_slot(residual, foot_ref), place_ref[...])
+    residual = dot(hot_ref[...], weighted.astype(BF16)) * live_ref[...]
     send_ref[...] = jnp.zeros_like(send_ref)
-    first = LINES * lax.axis_index("angle")
-    line = iota((LINES, BLK), 0)
-    mine = iota((LINES, BLK), 1) == (first + line) & (BLK - 1)
-    spot = iota((8, BLK), 0) * BLK + iota((8, BLK), 1) - first
-    spot = (spot >= 0) & (spot < LINES)
+    mine, spot = own_lanes(CAP, 0)
+    row = iota((PAD, BLK), 0)
+    none = jnp.zeros((8, BLK), jnp.int32)
+
+    def product(j):
+        vectors = residual[PAD * j : PAD * (j + 1)]
+        diag = jnp.concatenate([jnp.where(row == i, vectors, 0.0) for i in range(CAP)], axis=1).astype(BF16)
+        return dot(diag, foot_ref[CAP * j : CAP * (j + 1)].reshape(CAP * BLK, BLK))
+
+    products = [product(j) for j in range(NB // CAP)]
+    blocks = []
+    for j in range(NB // CAP):
+        back, code = quantize(products[j], place_ref[PAD * j : PAD * (j + 1)])
+        block = jnp.concatenate([back, none, code_rows(code, mine, spot)], axis=0) + block_ref[j]
+        blocks.append(block.astype(jnp.int16))
     voxel_copy.wait()
     for j in range(NB // CAP):
-        at = slice(CAP * j, CAP * (j + 1))
-        code = jnp.concatenate([codes[at], codes_ref[at]], axis=0)
-        code = jnp.sum(jnp.where(mine, code, 0), axis=0, keepdims=True)
-        code = jnp.where(spot, jnp.broadcast_to(code, (8, BLK)), 0)
-        send_ref[voxel_ref[CAP * j] >> 5] = jnp.concatenate([backs[at], sums_ref[at], code], axis=0).astype(jnp.int16)
+        send_ref[voxel_ref[CAP * j] >> 5] = blocks[j]
 
 
 def update_kernel(recv_ref, volume_ref, weighted_ref, out_ref, weighted_out_ref):
@@ -193,19 +226,19 @@
     left = lax.ppermute(part, "slab", [(i, i ^ 2) for i in range(8)])
     right = lax.ppermute(part, "slab", [(i, 6 - i + 2 * (i % 2)) for i in range(8)])
     across = lax.ppermute(part, "slab", [(i, i ^ 4) for i in range(8)])
-    live, place, column_sums, column_codes = call(
+    live, place, tile_hot, blocks = call(
         columns_kernel,
         "columns",
-        [((NB, BLK), F32)] + [((NB, BLK), jnp.int32)] * 3,
-        [VMEM] * 3,
-        block_voxel, block_rows, footprint,
+        [((256, BLK), F32), ((256, BLK), jnp.int32), ((256, 64), BF16), ((NB // CAP, 32, BLK), jnp.int32)],
+        [VMEM] * 4,
+        block_voxel, block_tile, block_rows, footprint,
     )
     weighted, send_back = call(
         backward_kernel,
         "backward",
         [((64, BLK), F32), ((SHARES, 32, BLK), jnp.int16)],
-        [VMEM] * 12,
-        block_voxel, part, left, right, across, measured, block_tile, live, place, column_sums, column_codes, footprint,
+        [VMEM] * 11,
+        block_voxel, part, left, right, across, measured, live, place, tile_hot, blocks, footprint,
         scratch=[pltpu.SMEM((NB,), jnp.int32), pltpu.SemaphoreType.DMA],
     )
     received = lax.all_to_all(send_back, "angle", 0, 0)

time: 55.3 us -> 55.3 us (level)
  no operation moved by 1% of the time
where the time goes in v10:
time: 55.3 us; the launch traced here: 54.6 us
  blocking collectives  38.8 us (70%)
  Pallas kernels  6 us (11%)
  waiting for transfers between devices  4.55 us (8%)
  starting transfers between devices  4.43 us (8%)
  between operations  0.74 us (1%)
    all_to_all x1, blocking collectives, on_device(): slab_values = lax.all_to_all(offer, 'angle', 0, 0)  23.4 us
    all_to_all x1, blocking collectives, on_device(): received = lax.all_to_all(send_back, 'angle', 0, 0)  15.4 us
    pallas_call x5, Pallas kernels, call(): pl.pallas_call(kernel, out_shape=out, in_specs=specs, out_specs=[VMEM] *...  6 us
    ppermute x1, starting transfers between devices, on_device(): across = lax.ppermute(part, 'slab', [(i, i ^ 4) for i in range(8)])  3.28 us
    ppermute x1, waiting for transfers between devices, on_device(): lax.ppermute(part, 'slab', [(i, 6 - i + 2 * (i % 2)) for i in range(8)])  2.9 us
    ppermute x1, waiting for transfers between devices, on_device(): part = part + lax.ppermute(part, 'slab', [(i, i ^ 1) for i in range(8)])  1.24 us
  transfers between devices with their start and end apart: 4, of which 3 were waited for; matrix products, arithmetic and copies ran while one was open for 0% of the time, Pallas kernels for 2%

profile of v10, /device:TPU:32, one launch (start us, length us, event | category | flops | bytes accessed | tf_op | source)
XLA Modules:
  0.0 54.6 jit_solution(15225004085058904595)
XLA Ops:
  0.6 0.0 copy-start
  0.6 0.0 copy-start.3
  0.7 0.0 copy-start.5
  0.7 0.0 copy-start.4
  0.7 0.9 %offer.1 = bf16[32,32,128]{2,1,0:T(8,128)(2,1)S(1)} custom-call(f32[32,128]{1,0:T(8,128)} %volume_ref.1, bf16[192,128,128]{2,1,0:T(8,128)(2,1)} %foot_ref.5), custom_call_target="tpu_custom_call" | custom-call | tf_op jit(solution)/shard_map/offer/pallas_call | solution.py:197
  1.6 23.4 %all_to_all.10.slab_ref = bf16[32,32,128]{2,1,0:T(8,128)(2,1)S(1)} all-to-all(bf16[32,32,128]{2,1,0:T(8,128)(2,1)S(1)} %offer.1), channel_id=1, replica_groups=mesh['slab'=8,'angle'=32] {'angle'}, dimensions={0} | all-to-all | bytes 524288 | tf_op jit(solution)/shard_map/all_to_all | solution.py:217
  25.0 0.0 copy-done
  25.0 0.0 copy-done.3
  25.0 0.0 copy-done.5
  25.0 0.0 copy-done.4
  25.0 0.0 copy-start.2
  25.0 1.9 %forward.1 = f32[128,128]{1,0:T(8,128)S(1)} custom-call(bf16[32,32,128]{2,1,0:T(8,128)(2,1)S(1)} %all_to_all.10.slab_ref, s32[192]{0:T(256)S(1)} %copy-done.3, s32[192]{0:T(256)S(1)} %copy-done.4, s32[192]{0:T(256)S(1)} %copy-done.5, bf16[192,128,128]{2,1,0:T(8,128)(2,1)S(1)} %copy-done), custom_call_target="tpu_custom_call" | custom-call | tf_op jit(solution)/shard_map/forward/pallas_call | solution.py:197
  26.9 0.1 collective-permute-start
  27.0 1.2 %collective-permute-done = f32[128,128]{1,0:T(8,128)S(1)} collective-permute-done((f32[128,128]{1,0:T(8,128)S(1)}, f32[128,128]{1,0:T(8,128)S(1)}, u32[]{:S(2)}, u32[]{:S(2)}) %collective-permute-start) | collective-permute-done | bytes 65568 | tf_op jit(solution)/shard_map/ppermute | solution.py:225
  28.2 0.0 copy-start.1
  28.3 3.3 %collective-permute-start.3 = (f32[128,128]{1,0:T(8,128)S(1)}, f32[128,128]{1,0:T(8,128)S(1)}, u32[]{:S(2)}, u32[]{:S(2)}) collective-permute-start(f32[128,128]{1,0:T(8,128)S(1)} %add.3.mine_ref), channel_id=1, source_target_pairs={{0,128},{32,160},{64,192},{96,224},{128,0},{160,32},{192,64},{224,... | collective-permute-start | bytes 196616 | tf_op jit(solution)/shard_map/ppermute | solution.py:228
  31.5 1.1 %collective-permute-start.2 = (f32[128,128]{1,0:T(8,128)S(1)}, f32[128,128]{1,0:T(8,128)S(1)}, u32[]{:S(2)}, u32[]{:S(2)}) collective-permute-start(f32[128,128]{1,0:T(8,128)S(1)} %add.3.mine_ref), channel_id=1, source_target_pairs={{0,192},{32,224},{64,128},{96,160},{128,64},{160,96},{192,0},{224,... | collective-permute-start | bytes 196616 | tf_op jit(solution)/shard_map/ppermute | solution.py:227
  32.6 0.0 collective-permute-start.1
  32.6 1.1 %columns.1 = (f32[256,128]{1,0:T(8,128)S(1)}, s32[256,128]{1,0:T(8,128)S(1)}, bf16[256,64]{1,0:T(8,128)(2,1)S(1)}, s32[16,32,128]{2,1,0:T(8,128)S(1)}) custom-call(s32[192]{0:T(256)S(1)} %copy-done.3, s32[192]{0:T(256)S(1)} %copy-done.4, s32[192]{0:T(256)S(1)} %copy-done.5, bf16[192,128,128]{2,1,0:T(8,128)(2,1)S(1)} %copy-done), custom_call_target="tpu_custom_call" | custom-call | tf_op jit(solution)/shard_map/columns/pallas_call | solution.py:197
  33.7 0.4 collective-permute-done.3.across_ref
  34.1 2.9 %collective-permute-done.2.right_ref = f32[128,128]{1,0:T(8,128)S(1)} collective-permute-done((f32[128,128]{1,0:T(8,128)S(1)}, f32[128,128]{1,0:T(8,128)S(1)}, u32[]{:S(2)}, u32[]{:S(2)}) %collective-permute-start.2) | collective-permute-done | bytes 65568 | tf_op jit(solution)/shard_map/ppermute | solution.py:227
  37.0 0.0 collective-permute-done.1.left_ref
  37.0 0.0 copy-done.2
  37.0 1.2 %backward.1 = (f32[64,128]{1,0:T(8,128)S(1)}, s16[32,32,128]{2,1,0:T(8,128)(2,1)S(1)}) custom-call(s32[192]{0:T(256)S(1)} %copy-done.3, f32[128,128]{1,0:T(8,128)S(1)} %add.3.mine_ref, f32[128,128]{1,0:T(8,128)S(1)} %collective-permute-done.1.left_ref, f32[128,128]{1,0:T(8,128)S(1)} %collective-permute-done.2.right_ref, ...), custom_call_target="tpu_custom_call" | custom-call | tf_op jit(solution)/shard_map/backward/pallas_call | solution.py:197
  38.3 15.4 %all_to_all.11.recv_ref = s16[32,32,128]{2,1,0:T(8,128)(2,1)S(1)} all-to-all(s16[32,32,128]{2,1,0:T(8,128)(2,1)S(1)} %get-tuple-element.12), channel_id=1, replica_groups=mesh['slab'=8,'angle'=32] {'angle'}, dimensions={0} | all-to-all | bytes 524288 | tf_op jit(solution)/shard_map/all_to_all | solution.py:244
  53.7 0.0 copy-done.1
  53.7 0.9 %update.1 = (f32[32,128]{1,0:T(8,128)}, f32[64,128]{1,0:T(8,128)}) custom-call(s16[32,32,128]{2,1,0:T(8,128)(2,1)S(1)} %all_to_all.11.recv_ref, f32[32,128]{1,0:T(8,128)S(1)} %copy-done.1, f32[64,128]{1,0:T(8,128)S(1)} %get-tuple-element.13.weighted_ref), custom_call_target="tpu_custom_call" | custom-call | tf_op jit(solution)/shard_map/update/pallas_call | solution.py:197
  (1 shorter events, 0.0 us)
Async XLA Ops:
  0.6 24.4 %copy-start = (bf16[192,128,128]{2,1,0:T(8,128)(2,1)S(1)}, bf16[192,128,128]{2,1,0:T(8,128)(2,1)}, u32[]{:S(2)}) copy-start(bf16[192,128,128]{2,1,0:T(8,128)(2,1)} %foot_ref.5) | copy-start | bytes 18874372
  0.6 24.4 %copy-start.3 = (s32[192]{0:T(256)S(1)}, s32[192]{0:T(256)}, u32[]{:S(2)}) copy-start(s32[192]{0:T(256)} %voxel_any.1) | copy-start | bytes 2308
  0.7 24.3 %copy-start.5 = (s32[192]{0:T(256)S(1)}, s32[192]{0:T(256)}, u32[]{:S(2)}) copy-start(s32[192]{0:T(256)} %rows_ref.3) | copy-start | bytes 2308
  0.7 24.3 %copy-start.4 = (s32[192]{0:T(256)S(1)}, s32[192]{0:T(256)}, u32[]{:S(2)}) copy-start(s32[192]{0:T(256)} %tile_ref.3) | copy-start | bytes 2308
  25.0 12.0 %copy-start.2 = (f32[64,128]{1,0:T(8,128)S(1)}, f32[64,128]{1,0:T(8,128)}, u32[]{:S(2)}) copy-start(f32[64,128]{1,0:T(8,128)} %measured_ref.1) | copy-start | bytes 98308
  26.9 1.3 %collective-permute-start = (f32[128,128]{1,0:T(8,128)S(1)}, f32[128,128]{1,0:T(8,128)S(1)}, u32[]{:S(2)}, u32[]{:S(2)}) collective-permute-start(f32[128,128]{1,0:T(8,128)S(1)} %forward.1), channel_id=1, source_target_pairs={{0,32},{32,0},{64,96},{96,64},{128,160},{160,128},{192,224},{224,1... | collective-permute-start | bytes 196616 | tf_op jit(solution)/shard_map/ppermute | solution.py:225
  28.2 25.4 %copy-start.1 = (f32[32,128]{1,0:T(8,128)S(1)}, f32[32,128]{1,0:T(8,128)}, u32[]{:S(2)}) copy-start(f32[32,128]{1,0:T(8,128)} %volume_ref.1) | copy-start | bytes 49156
  28.3 5.9 %collective-permute-start.3 = (f32[128,128]{1,0:T(8,128)S(1)}, f32[128,128]{1,0:T(8,128)S(1)}, u32[]{:S(2)}, u32[]{:S(2)}) collective-permute-start(f32[128,128]{1,0:T(8,128)S(1)} %add.3.mine_ref), channel_id=1, source_target_pairs={{0,128},{32,160},{64,192},{96,224},{128,0},{160,32},{192,64},{224,... | collective-permute-start | bytes 196616 | tf_op jit(solution)/shard_map/ppermute | solution.py:228
  31.5 5.5 %collective-permute-start.2 = (f32[128,128]{1,0:T(8,128)S(1)}, f32[128,128]{1,0:T(8,128)S(1)}, u32[]{:S(2)}, u32[]{:S(2)}) collective-permute-start(f32[128,128]{1,0:T(8,128)S(1)} %add.3.mine_ref), channel_id=1, source_target_pairs={{0,192},{32,224},{64,128},{96,160},{128,64},{160,96},{192,0},{224,... | collective-permute-start | bytes 196616 | tf_op jit(solution)/shard_map/ppermute | solution.py:227
  32.6 4.4 %collective-permute-start.1 = (f32[128,128]{1,0:T(8,128)S(1)}, f32[128,128]{1,0:T(8,128)S(1)}, u32[]{:S(2)}, u32[]{:S(2)}) collective-permute-start(f32[128,128]{1,0:T(8,128)S(1)} %add.3.mine_ref), channel_id=1, source_target_pairs={{0,64},{32,96},{64,0},{96,32},{128,192},{160,224},{192,128},{224,1... | collective-permute-start | bytes 196616 | tf_op jit(solution)/shard_map/ppermute | solution.py:226

commit v11 on v10

--- a/solution.py
+++ b/solution.py
@@ -144,7 +144,7 @@
         block_ref[j] = jnp.concatenate([none, sums[at][:CAP], code], axis=0)
 
 
-def backward_kernel(voxel_any, mine_ref, left_ref, right_ref, across_ref, measured_ref, live_ref, place_ref, hot_ref, block_ref, foot_ref, weighted_ref, send_ref, voxel_ref, sem):
+def backward_kernel(voxel_any, mine_ref, left_ref, across_ref, right_ref, measured_ref, live_ref, place_ref, hot_ref, block_ref, foot_ref, weighted_ref, send_ref, voxel_ref, sem):
     voxel_copy = pltpu.make_async_copy(voxel_any, voxel_ref, sem)
     voxel_copy.start()
     total = (mine_ref[...] + across_ref[...]) + (left_ref[...] + right_ref[...])
@@ -238,7 +238,7 @@
         "backward",
         [((64, BLK), F32), ((SHARES, 32, BLK), jnp.int16)],
         [VMEM] * 11,
-        block_voxel, part, left, right, across, measured, live, place, tile_hot, blocks, footprint,
+        block_voxel, part, left, across, right, measured, live, place, tile_hot, blocks, footprint,
         scratch=[pltpu.SMEM((NB,), jnp.int32), pltpu.SemaphoreType.DMA],
     )
     received = lax.all_to_all(send_back, "angle", 0, 0)

time: 55.3 us -> 55.3 us (level)
  waiting for transfers between devices: 4.55 us -> 5.13 us
    ppermute x1, starting transfers between devices: 3.28 us -> 0.63 us  [on_device(): across = lax.ppermute(part, 'slab', [(i, i ^ 4) for i in range(8)])]
    ppermute x1, waiting for transfers between devices: 0.4 us -> 2.97 us  [on_device(): across = lax.ppermute(part, 'slab', [(i, i ^ 4) for i in range(8)])]
    ppermute x1, starting transfers between devices: 1.06 us -> 3.1 us  [on_device(): lax.ppermute(part, 'slab', [(i, 6 - i + 2 * (i % 2)) for i in range(8)])]
    ppermute x1, waiting for transfers between devices: 2.9 us -> 0.92 us  [on_device(): lax.ppermute(part, 'slab', [(i, 6 - i + 2 * (i % 2)) for i in range(8)])]
where the time goes in v11:
time: 55.3 us; the launch traced here: 54.8 us
  blocking collectives  38.6 us (70%)
  Pallas kernels  6 us (11%)
  waiting for transfers between devices  5.13 us (9%)
  starting transfers between devices  4.27 us (8%)
  between operations  0.74 us (1%)
    all_to_all x1, blocking collectives, on_device(): slab_values = lax.all_to_all(offer, 'angle', 0, 0)  23.4 us
    all_to_all x1, blocking collectives, on_device(): received = lax.all_to_all(send_back, 'angle', 0, 0)  15.2 us
    pallas_call x5, Pallas kernels, call(): pl.pallas_call(kernel, out_shape=out, in_specs=specs, out_specs=[VMEM] *...  6 us
    ppermute x1, starting transfers between devices, on_device(): lax.ppermute(part, 'slab', [(i, 6 - i + 2 * (i % 2)) for i in range(8)])  3.1 us
    ppermute x1, waiting for transfers between devices, on_device(): across = lax.ppermute(part, 'slab', [(i, i ^ 4) for i in range(8)])  2.97 us
    ppermute x1, waiting for transfers between devices, on_device(): part = part + lax.ppermute(part, 'slab', [(i, i ^ 1) for i in range(8)])  1.24 us
  transfers between devices with their start and end apart: 4, of which 3 were waited for; matrix products, arithmetic and copies ran while one was open for 0% of the time, Pallas kernels for 2%

profile of v11, /device:TPU:32, one launch (start us, length us, event | category | flops | bytes accessed | tf_op | source)
XLA Modules:
  0.0 54.8 jit_solution(11932092129194241511)
XLA Ops:
  0.6 0.0 copy-start
  0.6 0.0 copy-start.3
  0.7 0.0 copy-start.5
  0.7 0.0 copy-start.4
  0.7 0.9 %offer.1 = bf16[32,32,128]{2,1,0:T(8,128)(2,1)S(1)} custom-call(f32[32,128]{1,0:T(8,128)} %volume_ref.1, bf16[192,128,128]{2,1,0:T(8,128)(2,1)} %foot_ref.5), custom_call_target="tpu_custom_call" | custom-call | tf_op jit(solution)/shard_map/offer/pallas_call | solution.py:197
  1.6 23.4 %all_to_all.10.slab_ref = bf16[32,32,128]{2,1,0:T(8,128)(2,1)S(1)} all-to-all(bf16[32,32,128]{2,1,0:T(8,128)(2,1)S(1)} %offer.1), channel_id=1, replica_groups=mesh['slab'=8,'angle'=32] {'angle'}, dimensions={0} | all-to-all | bytes 524288 | tf_op jit(solution)/shard_map/all_to_all | solution.py:217
  25.0 0.0 copy-done
  25.0 0.0 copy-done.3
  25.0 0.0 copy-done.5
  25.0 0.0 copy-done.4
  25.0 0.0 copy-start.2
  25.0 1.9 %forward.1 = f32[128,128]{1,0:T(8,128)S(1)} custom-call(bf16[32,32,128]{2,1,0:T(8,128)(2,1)S(1)} %all_to_all.10.slab_ref, s32[192]{0:T(256)S(1)} %copy-done.3, s32[192]{0:T(256)S(1)} %copy-done.4, s32[192]{0:T(256)S(1)} %copy-done.5, bf16[192,128,128]{2,1,0:T(8,128)(2,1)S(1)} %copy-done), custom_call_target="tpu_custom_call" | custom-call | tf_op jit(solution)/shard_map/forward/pallas_call | solution.py:197
  26.9 0.1 collective-permute-start
  27.0 1.2 %collective-permute-done = f32[128,128]{1,0:T(8,128)S(1)} collective-permute-done((f32[128,128]{1,0:T(8,128)S(1)}, f32[128,128]{1,0:T(8,128)S(1)}, u32[]{:S(2)}, u32[]{:S(2)}) %collective-permute-start) | collective-permute-done | bytes 65568 | tf_op jit(solution)/shard_map/ppermute | solution.py:225
  28.2 0.0 copy-start.1
  28.3 3.1 %collective-permute-start.3 = (f32[128,128]{1,0:T(8,128)S(1)}, f32[128,128]{1,0:T(8,128)S(1)}, u32[]{:S(2)}, u32[]{:S(2)}) collective-permute-start(f32[128,128]{1,0:T(8,128)S(1)} %add.3.mine_ref), channel_id=1, source_target_pairs={{0,192},{32,224},{64,128},{96,160},{128,64},{160,96},{192,0},{224,... | collective-permute-start | bytes 196616 | tf_op jit(solution)/shard_map/ppermute | solution.py:227
  31.4 0.6 %collective-permute-start.2 = (f32[128,128]{1,0:T(8,128)S(1)}, f32[128,128]{1,0:T(8,128)S(1)}, u32[]{:S(2)}, u32[]{:S(2)}) collective-permute-start(f32[128,128]{1,0:T(8,128)S(1)} %add.3.mine_ref), channel_id=1, source_target_pairs={{0,128},{32,160},{64,192},{96,224},{128,0},{160,32},{192,64},{224,... | collective-permute-start | bytes 196616 | tf_op jit(solution)/shard_map/ppermute | solution.py:228
  32.0 0.5 collective-permute-start.1
  32.4 1.1 %columns.1 = (f32[256,128]{1,0:T(8,128)S(1)}, s32[256,128]{1,0:T(8,128)S(1)}, bf16[256,64]{1,0:T(8,128)(2,1)S(1)}, s32[16,32,128]{2,1,0:T(8,128)S(1)}) custom-call(s32[192]{0:T(256)S(1)} %copy-done.3, s32[192]{0:T(256)S(1)} %copy-done.4, s32[192]{0:T(256)S(1)} %copy-done.5, bf16[192,128,128]{2,1,0:T(8,128)(2,1)S(1)} %copy-done), custom_call_target="tpu_custom_call" | custom-call | tf_op jit(solution)/shard_map/columns/pallas_call | solution.py:197
  33.5 0.9 %collective-permute-done.3.right_ref = f32[128,128]{1,0:T(8,128)S(1)} collective-permute-done((f32[128,128]{1,0:T(8,128)S(1)}, f32[128,128]{1,0:T(8,128)S(1)}, u32[]{:S(2)}, u32[]{:S(2)}) %collective-permute-start.3) | collective-permute-done | bytes 65568 | tf_op jit(solution)/shard_map/ppermute | solution.py:227
  34.5 3.0 %collective-permute-done.2.across_ref = f32[128,128]{1,0:T(8,128)S(1)} collective-permute-done((f32[128,128]{1,0:T(8,128)S(1)}, f32[128,128]{1,0:T(8,128)S(1)}, u32[]{:S(2)}, u32[]{:S(2)}) %collective-permute-start.2) | collective-permute-done | bytes 65568 | tf_op jit(solution)/shard_map/ppermute | solution.py:228
  37.4 0.0 collective-permute-done.1.left_ref
  37.4 0.0 copy-done.2
  37.4 1.2 %backward.1 = (f32[64,128]{1,0:T(8,128)S(1)}, s16[32,32,128]{2,1,0:T(8,128)(2,1)S(1)}) custom-call(s32[192]{0:T(256)S(1)} %copy-done.3, f32[128,128]{1,0:T(8,128)S(1)} %add.3.mine_ref, f32[128,128]{1,0:T(8,128)S(1)} %collective-permute-done.1.left_ref, f32[128,128]{1,0:T(8,128)S(1)} %collective-permute-done.2.across_ref, ...), custom_call_target="tpu_custom_call" | custom-call | tf_op jit(solution)/shard_map/backward/pallas_call | solution.py:197
  38.7 15.2 %all_to_all.11.recv_ref = s16[32,32,128]{2,1,0:T(8,128)(2,1)S(1)} all-to-all(s16[32,32,128]{2,1,0:T(8,128)(2,1)S(1)} %get-tuple-element.12), channel_id=1, replica_groups=mesh['slab'=8,'angle'=32] {'angle'}, dimensions={0} | all-to-all | bytes 524288 | tf_op jit(solution)/shard_map/all_to_all | solution.py:244
  53.8 0.0 copy-done.1
  53.9 0.9 %update.1 = (f32[32,128]{1,0:T(8,128)}, f32[64,128]{1,0:T(8,128)}) custom-call(s16[32,32,128]{2,1,0:T(8,128)(2,1)S(1)} %all_to_all.11.recv_ref, f32[32,128]{1,0:T(8,128)S(1)} %copy-done.1, f32[64,128]{1,0:T(8,128)S(1)} %get-tuple-element.13.weighted_ref), custom_call_target="tpu_custom_call" | custom-call | tf_op jit(solution)/shard_map/update/pallas_call | solution.py:197
  (1 shorter events, 0.0 us)
Async XLA Ops:
  0.6 24.4 %copy-start = (bf16[192,128,128]{2,1,0:T(8,128)(2,1)S(1)}, bf16[192,128,128]{2,1,0:T(8,128)(2,1)}, u32[]{:S(2)}) copy-start(bf16[192,128,128]{2,1,0:T(8,128)(2,1)} %foot_ref.5) | copy-start | bytes 18874372
  0.6 24.4 %copy-start.3 = (s32[192]{0:T(256)S(1)}, s32[192]{0:T(256)}, u32[]{:S(2)}) copy-start(s32[192]{0:T(256)} %voxel_any.1) | copy-start | bytes 2308
  0.7 24.3 %copy-start.5 = (s32[192]{0:T(256)S(1)}, s32[192]{0:T(256)}, u32[]{:S(2)}) copy-start(s32[192]{0:T(256)} %rows_ref.3) | copy-start | bytes 2308
  0.7 24.3 %copy-start.4 = (s32[192]{0:T(256)S(1)}, s32[192]{0:T(256)}, u32[]{:S(2)}) copy-start(s32[192]{0:T(256)} %tile_ref.3) | copy-start | bytes 2308
  25.0 12.4 %copy-start.2 = (f32[64,128]{1,0:T(8,128)S(1)}, f32[64,128]{1,0:T(8,128)}, u32[]{:S(2)}) copy-start(f32[64,128]{1,0:T(8,128)} %measured_ref.1) | copy-start | bytes 98308
  26.9 1.3 %collective-permute-start = (f32[128,128]{1,0:T(8,128)S(1)}, f32[128,128]{1,0:T(8,128)S(1)}, u32[]{:S(2)}, u32[]{:S(2)}) collective-permute-start(f32[128,128]{1,0:T(8,128)S(1)} %forward.1), channel_id=1, source_target_pairs={{0,32},{32,0},{64,96},{96,64},{128,160},{160,128},{192,224},{224,1... | collective-permute-start | bytes 196616 | tf_op jit(solution)/shard_map/ppermute | solution.py:225
  28.2 25.6 %copy-start.1 = (f32[32,128]{1,0:T(8,128)S(1)}, f32[32,128]{1,0:T(8,128)}, u32[]{:S(2)}) copy-start(f32[32,128]{1,0:T(8,128)} %volume_ref.1) | copy-start | bytes 49156
  28.3 6.2 %collective-permute-start.3 = (f32[128,128]{1,0:T(8,128)S(1)}, f32[128,128]{1,0:T(8,128)S(1)}, u32[]{:S(2)}, u32[]{:S(2)}) collective-permute-start(f32[128,128]{1,0:T(8,128)S(1)} %add.3.mine_ref), channel_id=1, source_target_pairs={{0,192},{32,224},{64,128},{96,160},{128,64},{160,96},{192,0},{224,... | collective-permute-start | bytes 196616 | tf_op jit(solution)/shard_map/ppermute | solution.py:227
  31.4 6.1 %collective-permute-start.2 = (f32[128,128]{1,0:T(8,128)S(1)}, f32[128,128]{1,0:T(8,128)S(1)}, u32[]{:S(2)}, u32[]{:S(2)}) collective-permute-start(f32[128,128]{1,0:T(8,128)S(1)} %add.3.mine_ref), channel_id=1, source_target_pairs={{0,128},{32,160},{64,192},{96,224},{128,0},{160,32},{192,64},{224,... | collective-permute-start | bytes 196616 | tf_op jit(solution)/shard_map/ppermute | solution.py:228
  32.0 5.5 %collective-permute-start.1 = (f32[128,128]{1,0:T(8,128)S(1)}, f32[128,128]{1,0:T(8,128)S(1)}, u32[]{:S(2)}, u32[]{:S(2)}) collective-permute-start(f32[128,128]{1,0:T(8,128)S(1)} %add.3.mine_ref), channel_id=1, source_target_pairs={{0,64},{32,96},{64,0},{96,32},{128,192},{160,224},{192,128},{224,1... | collective-permute-start | bytes 196616 | tf_op jit(solution)/shard_map/ppermute | solution.py:226
